TPU v7x, 32 devices: a whole 2x2x4 slice. The times are simulated.
32 devices in a mesh: rows: 8 (over z, x), tp: 4 (over y, core).
Axes of the slice: x: 2, y: 2, z: 4, core: 2. Of those that a mesh axis runs over, the one named last changes fastest.
Arguments:
- node_feats: bfloat16 [2048, 512], P('rows'), may hold values from -6 to 6
- edge_feats: bfloat16 [16384, 512], P('rows'), may hold values from -6 to 6
- edge_receiver: int32 [16384], P('rows'), may hold values from 0 to 255
- edge_slot: int32 [16384], P('rows'), may hold values from 0 to 255
- edge_mask: int32 [16384], P('rows'), may hold values 0 or 1
- serve_rows: int32 [64, 32], P('rows'), may hold values from 0 to 255
- node_cot: bfloat16 [2048, 512], P('rows')
- edge_cot: bfloat16 [16384, 512], P('rows')
- edge_in_weight: float32 [1536, 512], P(None, 'tp'), may hold values from -0.15625 to 0.15625
- edge_out_weight: float32 [512, 512], P('tp'), may hold values from -0.25 to 0.25
- node_in_weight: float32 [1024, 512], P(None, 'tp'), may hold values from -0.1875 to 0.1875
- node_out_weight: float32 [512, 512], P('tp'), may hold values from -0.25 to 0.25
- hidden_bias: float32 [2, 512], P(None, 'tp'), may hold values from -3 to 3
- feature_vectors: float32 [6, 512], replicated
- edge_in_first: float32 [1536, 512], P(None, 'tp')
- edge_out_first: float32 [512, 512], P('tp')
- node_in_first: float32 [1024, 512], P(None, 'tp')
- node_out_first: float32 [512, 512], P('tp')
- hidden_bias_first: float32 [2, 512], P(None, 'tp')
- feature_vectors_first: float32 [6, 512], replicated
- edge_in_second: float32 [1536, 512], P(None, 'tp')
- edge_out_second: float32 [512, 512], P('tp')
- node_in_second: float32 [1024, 512], P(None, 'tp')
- node_out_second: float32 [512, 512], P('tp')
- hidden_bias_second: float32 [2, 512], P(None, 'tp')
- feature_vectors_second: float32 [6, 512], replicated
Outputs:
- new_nodes: bfloat16 [2048, 512], P('rows')
- new_edges: bfloat16 [16384, 512], P('rows')
- node_gradient: bfloat16 [2048, 512], P('rows')
- edge_gradient: bfloat16 [16384, 512], P('rows')
- gradient_norm: float32 [1], replicated
- new_edge_in: float32 [1536, 512], P(None, 'tp')
- new_edge_out: float32 [512, 512], P('tp')
- new_node_in: float32 [1024, 512], P(None, 'tp')
- new_node_out: float32 [512, 512], P('tp')
- new_hidden_bias: float32 [2, 512], P(None, 'tp')
- new_feature_vectors: float32 [6, 512], replicated
- new_edge_in_first: float32 [1536, 512], P(None, 'tp')
- new_edge_out_first: float32 [512, 512], P('tp')
- new_node_in_first: float32 [1024, 512], P(None, 'tp')
- new_node_out_first: float32 [512, 512], P('tp')
- new_hidden_bias_first: float32 [2, 512], P(None, 'tp')
- new_feature_vectors_first: float32 [6, 512], replicated
- new_edge_in_second: float32 [1536, 512], P(None, 'tp')
- new_edge_out_second: float32 [512, 512], P('tp')
- new_node_in_second: float32 [1024, 512], P(None, 'tp')
- new_node_out_second: float32 [512, 512], P('tp')
- new_hidden_bias_second: float32 [2, 512], P(None, 'tp')
- new_feature_vectors_second: float32 [6, 512], replicated
Inputs may be any that keep to these rules, and one draw needn't show every extreme that they name: `serve_rows`: row p * 8 + d holds the local indices of the 32 nodes of device p whose latents device d receives. `edge_slot`: an edge of device d with slot s has as sender the node named in entry s % 32 of row (s // 32) * 8 + d of serve_rows. `edge_receiver`: index of the receiver among the 256 nodes of the edge's own device.
All inputs are finite; a program needn't handle non-finite values. No bound on the sum of `edge_mask` on one device may be relied on, other than what follows from the above.
Results may differ from a plain program's by a relative error of at most 0.0081.
Values may be sent and summed in bfloat16 or wider, within the bound.
A program may use at most 128 MiB of HBM per device.

v0:
```python
import jax
import jax.numpy as jnp
from jax import lax
from jax.sharding import PartitionSpec as P

beta_one = 0.9
beta_two = 0.999
adam_step = 7.0
adam_eps = 1e-08
learn_rate = 0.05
vector_rate = 0.3
decay_rate = 0.1
clip_level = 1.0


def matmul(left, right):
    return jnp.dot(left, right, preferred_element_type=jnp.float32)


def exact_mul(left, right):
    return jnp.dot(left, right, precision=lax.Precision.HIGHEST, preferred_element_type=jnp.float32)


def dot_rows(left, right):
    return lax.dot_general(
        left, right, (((0,), (0,)), ((), ())), preferred_element_type=jnp.float32
    )


def exact_rows(left, right):
    return lax.dot_general(
        left,
        right,
        (((0,), (0,)), ((), ())),
        precision=lax.Precision.HIGHEST,
        preferred_element_type=jnp.float32,
    )


def dot_cols(left, right):
    return lax.dot_general(
        left, right, (((1,), (1,)), ((), ())), preferred_element_type=jnp.float32
    )


def one_hot_table(index, count, dtype):
    return (index[:, None] == jnp.arange(count, dtype=jnp.int32)[None, :]).astype(dtype)


def normalize(values):
    center = values - jnp.mean(values, axis=1, keepdims=True)
    inverse = lax.rsqrt(jnp.mean(center * center, axis=1, keepdims=True) + 1e-05)
    return (center * inverse, inverse)


def norm_back(upstream, normed, inverse, gain):
    scaled = upstream * gain
    centered = scaled - jnp.mean(scaled, axis=1, keepdims=True)
    return inverse * (centered - normed * jnp.mean(scaled * normed, axis=1, keepdims=True))


def silu_slope(values):
    logistic = jax.nn.sigmoid(values)
    return logistic * (1.0 + values * (1.0 - logistic))


def adam_update(weight, first, second, gradient, factor, rate):
    clipped = gradient * factor
    first_new = beta_one * first + (1.0 - beta_one) * clipped
    second_new = beta_two * second + (1.0 - beta_two) * clipped * clipped
    bias_one = 1.0 - beta_one**adam_step
    bias_two = 1.0 - beta_two**adam_step
    moved = (
        first_new / bias_one / (jnp.sqrt(second_new / bias_two) + adam_eps) + decay_rate * weight
    )
    return (weight - rate * moved, first_new, second_new)


def local(
    node_feats,
    edge_feats,
    edge_receiver,
    edge_slot,
    edge_mask,
    serve_rows,
    node_cot,
    edge_cot,
    edge_in_weight,
    edge_out_weight,
    node_in_weight,
    node_out_weight,
    hidden_bias,
    feature_vectors,
    edge_in_first,
    edge_out_first,
    node_in_first,
    node_out_first,
    hidden_bias_first,
    feature_vectors_first,
    edge_in_second,
    edge_out_second,
    node_in_second,
    node_out_second,
    hidden_bias_second,
    feature_vectors_second,
):
    owners = lax.axis_size("rows")
    latent = node_feats.shape[1]
    nodes_here = node_feats.shape[0]
    slot_count = owners * serve_rows.shape[1]
    serve_flat = serve_rows.reshape(-1)
    edge_first = edge_in_weight.astype(jnp.bfloat16)
    edge_second = edge_out_weight.astype(jnp.bfloat16)
    node_first = node_in_weight.astype(jnp.bfloat16)
    node_second = node_out_weight.astype(jnp.bfloat16)
    edge_first_full, node_first_full = (
        lax.all_gather(edge_first, "tp", axis=1, tiled=True),
        lax.all_gather(node_first, "tp", axis=1, tiled=True),
    )
    edge_second_full, node_second_full = (
        lax.all_gather(edge_second, "tp", axis=0, tiled=True),
        lax.all_gather(node_second, "tp", axis=0, tiled=True),
    )
    mask_col = edge_mask.astype(jnp.float32)[:, None]
    receiver_hot = one_hot_table(edge_receiver, nodes_here, jnp.bfloat16)
    slot_hot = one_hot_table(edge_slot, slot_count, jnp.bfloat16)
    serve_hot = one_hot_table(serve_flat, nodes_here, jnp.float32)
    receiver_feats = node_feats[edge_receiver]
    own_part = matmul(edge_feats, edge_first[:latent]) + matmul(
        receiver_feats, edge_first[2 * latent :]
    )
    served = lax.all_to_all(node_feats[serve_rows], "rows", split_axis=0, concat_axis=0, tiled=True)
    sent_feats = served.reshape(slot_count, latent)[edge_slot]
    sender_term = matmul(sent_feats, edge_first[latent : 2 * latent])
    edge_pre = own_part + sender_term + hidden_bias[0]
    edge_hidden = jax.nn.silu(edge_pre).astype(jnp.bfloat16)
    edge_wide = lax.all_gather(edge_hidden, "tp", axis=1, tiled=True)
    edge_outer = matmul(edge_wide, edge_second_full) + feature_vectors[0]
    edge_normed, edge_inverse = normalize(edge_outer)
    update = edge_normed * feature_vectors[1] + feature_vectors[2]
    masked = mask_col * update
    new_edges = (edge_feats.astype(jnp.float32) + masked).astype(jnp.bfloat16)
    aggregate = exact_rows(receiver_hot.astype(jnp.float32), masked).astype(jnp.bfloat16)
    node_pre = (
        matmul(node_feats, node_first[:latent])
        + matmul(aggregate, node_first[latent:])
        + hidden_bias[1]
    )
    node_hidden = jax.nn.silu(node_pre).astype(jnp.bfloat16)
    node_wide = lax.all_gather(node_hidden, "tp", axis=1, tiled=True)
    node_outer = matmul(node_wide, node_second_full) + feature_vectors[3]
    node_normed, node_inverse = normalize(node_outer)
    new_nodes = (
        node_feats.astype(jnp.float32) + (node_normed * feature_vectors[4] + feature_vectors[5])
    ).astype(jnp.bfloat16)
    node_up = node_cot.astype(jnp.float32)
    node_outer_grad = norm_back(node_up, node_normed, node_inverse, feature_vectors[4]).astype(
        jnp.bfloat16
    )
    node_slope = (dot_cols(node_outer_grad, node_second) * silu_slope(node_pre)).astype(
        jnp.bfloat16
    )
    node_slope_wide = lax.all_gather(node_slope, "tp", axis=1, tiled=True)
    node_input_grad = dot_cols(node_slope_wide, node_first_full)
    edge_cot_float = edge_cot.astype(jnp.float32)
    edge_up = mask_col * (edge_cot_float + node_input_grad[:, latent:][edge_receiver])
    edge_outer_grad = norm_back(edge_up, edge_normed, edge_inverse, feature_vectors[1]).astype(
        jnp.bfloat16
    )
    edge_slope = (dot_cols(edge_outer_grad, edge_second) * silu_slope(edge_pre)).astype(
        jnp.bfloat16
    )
    edge_slope_wide = lax.all_gather(edge_slope, "tp", axis=1, tiled=True)
    edge_gradient = (edge_cot_float + dot_cols(edge_slope_wide, edge_first_full[:latent])).astype(
        jnp.bfloat16
    )
    receiver_slope = dot_rows(receiver_hot, edge_slope_wide)
    receiver_weight = edge_first_full[2 * latent :].astype(jnp.float32)
    node_total = node_up + node_input_grad[:, :latent]
    node_total = node_total + exact_mul(receiver_slope, receiver_weight.T)
    slot_slope_wide = dot_rows(slot_hot, edge_slope_wide)
    sender_weight_full = edge_first_full[latent : 2 * latent].astype(jnp.float32)
    slot_grad = exact_mul(slot_slope_wide, sender_weight_full.T)
    returned = lax.all_to_all(
        slot_grad.reshape(owners, -1, latent), "rows", split_axis=0, concat_axis=0, tiled=True
    )
    node_total = node_total + exact_rows(serve_hot, returned.reshape(slot_count, latent))
    sender_weight_grad = dot_rows(sent_feats, edge_slope)
    node_gradient = node_total.astype(jnp.bfloat16)
    edge_in_grad = jnp.concatenate(
        [
            dot_rows(edge_feats, edge_slope),
            sender_weight_grad,
            dot_rows(receiver_feats, edge_slope),
        ],
        axis=0,
    )
    edge_out_grad = dot_rows(edge_hidden, edge_outer_grad)
    node_in_grad = jnp.concatenate(
        [dot_rows(node_feats, node_slope), dot_rows(aggregate, node_slope)], axis=0
    )
    node_out_grad = dot_rows(node_hidden, node_outer_grad)
    bias_grad = jnp.stack(
        [
            jnp.sum(edge_slope.astype(jnp.float32), axis=0),
            jnp.sum(node_slope.astype(jnp.float32), axis=0),
        ]
    )
    vector_grad = jnp.stack(
        [
            jnp.sum(edge_outer_grad.astype(jnp.float32), axis=0),
            jnp.sum(edge_up * edge_normed, axis=0),
            jnp.sum(edge_up, axis=0),
            jnp.sum(node_outer_grad.astype(jnp.float32), axis=0),
            jnp.sum(node_up * node_normed, axis=0),
            jnp.sum(node_up, axis=0),
        ]
    )
    summed_grads = lax.psum(
        (edge_in_grad, edge_out_grad, node_in_grad, node_out_grad, bias_grad, vector_grad), "rows"
    )
    split_square = jnp.sum(summed_grads[0] * summed_grads[0]) + jnp.sum(
        summed_grads[1] * summed_grads[1]
    )
    split_square = (
        split_square
        + jnp.sum(summed_grads[2] * summed_grads[2])
        + jnp.sum(summed_grads[3] * summed_grads[3])
    )
    split_square = split_square + jnp.sum(summed_grads[4] * summed_grads[4])
    square_sum = lax.psum(split_square, "tp") + jnp.sum(summed_grads[5] * summed_grads[5])
    gradient_norm = jnp.sqrt(square_sum)
    factor = clip_level / jnp.maximum(gradient_norm, clip_level)
    edge_in_new = adam_update(
        edge_in_weight, edge_in_first, edge_in_second, summed_grads[0], factor, learn_rate
    )
    edge_out_new = adam_update(
        edge_out_weight, edge_out_first, edge_out_second, summed_grads[1], factor, learn_rate
    )
    node_in_new = adam_update(
        node_in_weight, node_in_first, node_in_second, summed_grads[2], factor, learn_rate
    )
    node_out_new = adam_update(
        node_out_weight, node_out_first, node_out_second, summed_grads[3], factor, learn_rate
    )
    bias_new = adam_update(
        hidden_bias, hidden_bias_first, hidden_bias_second, summed_grads[4], factor, vector_rate
    )
    vector_new = adam_update(
        feature_vectors,
        feature_vectors_first,
        feature_vectors_second,
        summed_grads[5],
        factor,
        vector_rate,
    )
    return (
        new_nodes,
        new_edges,
        node_gradient,
        edge_gradient,
        gradient_norm.reshape(1),
        edge_in_new[0],
        edge_out_new[0],
        node_in_new[0],
        node_out_new[0],
        bias_new[0],
        vector_new[0],
        edge_in_new[1],
        edge_out_new[1],
        node_in_new[1],
        node_out_new[1],
        bias_new[1],
        vector_new[1],
        edge_in_new[2],
        edge_out_new[2],
        node_in_new[2],
        node_out_new[2],
        bias_new[2],
        vector_new[2],
    )


def solution(mesh):
    return jax.shard_map(
        local,
        mesh=mesh,
        in_specs=(
            P("rows", None),
            P("rows", None),
            P("rows"),
            P("rows"),
            P("rows"),
            P("rows", None),
            P("rows", None),
            P("rows", None),
            P(None, "tp"),
            P("tp", None),
            P(None, "tp"),
            P("tp", None),
            P(None, "tp"),
            P(),
            P(None, "tp"),
            P("tp", None),
            P(None, "tp"),
            P("tp", None),
            P(None, "tp"),
            P(),
            P(None, "tp"),
            P("tp", None),
            P(None, "tp"),
            P("tp", None),
            P(None, "tp"),
            P(),
        ),
        out_specs=(
            P("rows", None),
            P("rows", None),
            P("rows", None),
            P("rows", None),
            P(),
            P(None, "tp"),
            P("tp", None),
            P(None, "tp"),
            P("tp", None),
            P(None, "tp"),
            P(),
            P(None, "tp"),
            P("tp", None),
            P(None, "tp"),
            P("tp", None),
            P(None, "tp"),
            P(),
            P(None, "tp"),
            P("tp", None),
            P(None, "tp"),
            P("tp", None),
            P(None, "tp"),
            P(),
        ),
        check_vma=False,
    )
```

profile of v0, /device:TPU:0, one launch (start us, length us, event | category | flops | bytes accessed | tf_op | source)
XLA Modules:
  0.0 314.9 jit_solution(6605639263682125148)
XLA Ops:
  7.2 0.8 compare_select_fusion.2
  8.1 2.9 gather_fusion.1
  11.0 7.3 %all-to-all-start = ((bf16[8,32,512]{2,1,0:T(8,128)(2,1)}), bf16[8,32,512]{2,1,0:T(8,128)(2,1)S(1)}, u32[]{:S(2)}, u32[]{:S(2)}) async-start(bf16[8,32,512]{2,1,0:T(8,128)(2,1)} %bitcast), calls=%async_computation | async-start | bytes 524288 | tf_op jit(solution)/shard_map/all_to_all | solution.py:132
  18.4 9.2 %gather_fusion = bf16[2048,512]{1,0:T(8,128)(2,1)} fusion(bf16[256,512]{1,0:T(8,128)(2,1)S(1)} %copy-done, s32[2048]{0:T(1024)S(1)} %fusion.46), kind=kCustom, calls=%fused_computation | custom fusion | bytes 4202496 | tf_op jit(solution)/shard_map/gather | solution.py:128
  29.2 1.7 convolution_add_fusion.1
  30.9 9.2 %gather_fusion.2 = bf16[2048,512]{1,0:T(8,128)(2,1)} fusion(bf16[256,512]{1,0:T(8,128)(2,1)S(1)} %bitcast.62, s32[2048]{0:T(1024)S(1)} %fusion.47), kind=kCustom, calls=%fused_computation.2 | custom fusion | bytes 4202496 | tf_op jit(solution)/shard_map/gather | solution.py:133
  40.1 3.8 %multiply_convert_fusion.1 = (bf16[2048,128]{1,0:T(8,128)(2,1)}, f32[2048,128]{1,0:T(8,128)}) fusion(f32[128]{0:T(128)S(1)} %get-tuple-element.92, f32[2048,128]{1,0:T(8,128)} %convolution_add_fusion.1, bf16[2048,512]{1,0:T(8,128)(2,1)} %gather_fusion.2, bf16[1536,128]{1,0:T(8,128)(2,1)S(1)} %convert_element_type.81), kind=kOutput, calls=%fused_computation.46 | convolution fusion | flops 270270464 | bytes 4850176 | tf_op jit(solution)/shard_map/dot_general | solution.py:17
  44.8 1.8 fusion.42
  46.6 2.5 copy.49
  49.2 7.6 %all_gather.25 = bf16[512,512]{1,0:T(8,128)(2,1)S(1)} all-gather(bf16[128,512]{1,0:T(8,128)(2,1)S(1)} %convert_element_type.83), channel_id=1, replica_groups=mesh['rows'=8,'tp'=4] {'tp'}, dimensions={0}, use_global_device_ids=true | all-gather | bytes 655360 | tf_op jit(solution)/shard_map/all_gather | solution.py:121
  57.6 10.9 %all_gather.27 = bf16[512,512]{1,0:T(8,128)(2,1)S(1)} all-gather(bf16[128,512]{1,0:T(8,128)(2,1)S(1)} %convert_element_type.86), channel_id=1, replica_groups=mesh['rows'=8,'tp'=4] {'tp'}, dimensions={0}, use_global_device_ids=true | all-gather | bytes 655360 | tf_op jit(solution)/shard_map/all_gather | solution.py:122
  68.5 4.0 %copy.50 = bf16[2048,512]{0,1:T(8,128)(2,1)} copy(bf16[2048,512]{1,0:T(8,128)(2,1)} %param.33) | data formatting | bytes 4194304 | tf_op args[7]
  72.4 3.0 add_reduce_fusion
  76.1 1.2 copy-done.1
  77.4 3.7 %fusion.13 = bf16[256,512]{1,0:T(8,128)(2,1)S(1)} fusion(f32[512]{0:T(512)S(1)} %bitcast.79, f32[512]{0:T(512)S(1)} %bitcast.71, f32[2048]{0:T(1024)S(1)} %convert_element_type.80, s32[2048]{0:T(1024)S(1)} %copy-done.63, f32[2048,512]{0,1:T(8,128)S(1)} %get-tuple-element.96, f32[2048]{0:T(1024)S(1)} %add_rsqrt_fusion, ...), kind=kOutput, calls=%fused_computation.36 | convolution fusion | flops 3228696576 | bytes 4495360 | tf_op jit(solution)/shard_map/dot_general | solution.py:31
  81.4 7.7 %all_gather.26 = bf16[256,512]{1,0:T(8,128)(2,1)S(1)} all-gather(bf16[256,128]{1,0:T(8,128)(2,1)S(1)} %get-tuple-element.97), channel_id=1, replica_groups=mesh['rows'=8,'tp'=4] {'tp'}, dimensions={1}, use_global_device_ids=true | all-gather | bytes 327680 | tf_op jit(solution)/shard_map/all_gather | solution.py:150
  89.7 0.8 fusion.29
  90.5 1.6 convert_reduce_fusion.3
  92.8 6.1 %all_gather.28 = bf16[256,512]{1,0:T(8,128)(2,1)S(1)} all-gather(bf16[256,128]{1,0:T(8,128)(2,1)S(1)} %get-tuple-element.102), channel_id=1, replica_groups=mesh['rows'=8,'tp'=4] {'tp'}, dimensions={1}, use_global_device_ids=true | all-gather | bytes 327680 | tf_op jit(solution)/shard_map/all_gather | solution.py:163
  98.9 1.7 fusion.59
  100.6 1.0 copy-done.9
  101.6 8.9 %gather_fusion.3 = f32[2048,512]{1,0:T(8,128)} fusion(f32[256,512]{1,0:T(8,128)S(1)} %slice.88, s32[2048]{0:T(1024)S(1)} %fusion.46), kind=kCustom, calls=%fused_computation.3 | custom fusion | bytes 8396800 | tf_op jit(solution)/shard_map/gather | solution.py:166
  110.5 5.5 %copy.51 = f32[2048,512]{0,1:T(8,128)} copy(f32[2048,512]{1,0:T(8,128)} %gather_fusion.3) | data formatting | bytes 8388608 | tf_op jit(solution)/shard_map/gather | solution.py:166
  116.1 7.4 %multiply_reduce_fusion = (f32[512]{0:T(512)S(1)}, f32[2048]{0:T(1024)S(1)}, f32[2048]{0:T(1024)S(1)}, f32[512]{0:T(512)S(1)}, f32[2048,512]{0,1:T(8,128)S(1)}, /*index=5*/bf16[2048,512]{0,1:T(8,128)(2,1)}) fusion(f32[2048]{0:T(1024)S(1)} %copy-done.42, f32[2048]{0:T(1024)S(1)} %broadcast_multiply_fusion.2, f32[2048,512]{0,1:T(8,128)} %copy-done.1, ...), kind=kLoop, calls=%fused_computation.8 | loop fusion | flops 19917824 | bytes 18925568 | tf_op jit(solution)/shard_map/reduce_sum | solution.py:212
  123.6 2.6 convert_reduce_fusion
  126.2 0.8 convert_reduce_fusion.1
  127.5 2.3 fusion.61
  130.9 1.1 copy-done.6
  132.1 1.5 fusion.62
  134.1 0.9 fusion.64
  135.0 0.8 pad_maximum_fusion.1
  135.8 0.9 pad_maximum_fusion
  138.4 1.0 copy.63
  139.4 1.1 copy.56
  140.5 1.1 copy.57
  141.7 2.2 copy.60
  143.9 2.2 copy.61
  146.1 39.1 %all-reduce = (f32[2,128]{1,0:T(2,128)S(1)}, f32[6,512]{1,0:T(8,128)S(1)}) all-reduce(f32[2,128]{1,0:T(2,128)S(1)} %pad_maximum_fusion.2, f32[6,512]{1,0:T(8,128)S(1)} %stack.39), channel_id=1, replica_groups=mesh['rows'=8,'tp'=4] {'rows'}, use_global_device_ids=true, to_apply=%region_18.19 | all-reduce | flops 3328 | bytes 26624 | tf_op jit(solution)/shard_map/psum | solution.py:219
  186.4 49.7 %all-reduce.4.cloned.1.call-done = (f32[1536,128]{0,1:T(8,128)}, f32[128,512]{1,0:T(8,128)}, f32[1024,128]{0,1:T(8,128)}, f32[128,512]{1,0:T(8,128)}) async-done(((f32[1536,128]{0,1:T(8,128)}, f32[128,512]{1,0:T(8,128)}, f32[1024,128]{0,1:T(8,128)}, f32[128,512]{1,0:T(8,128)}), (f32[1536,128]{0,1:T(8,128)}, f32[128,512]{1,0:T(8,128)}, f32[1024,128]{0,1:T(8,128)}, ...) | async-done | bytes 1835024 | tf_op jit(solution)/shard_map/psum | solution.py:219
  236.2 1.9 multiply_reduce_fusion.4
  238.1 1.6 multiply_reduce_fusion.8
  241.1 1.8 multiply_reduce_fusion.5
  243.5 1.6 multiply_reduce_fusion.7
  246.4 2.5 copy.64
  249.0 8.4 %psum.54 = f32[]{:T(128)} all-reduce(f32[]{:T(128)S(6)} %add.297), channel_id=1, replica_groups=mesh['rows'=8,'tp'=4] {'tp'}, use_global_device_ids=true, to_apply=%region_20.21 | all-reduce | flops 1 | bytes 8 | tf_op jit(solution)/shard_map/psum | solution.py:231
  258.8 3.3 %multiply_subtract_fusion = (f32[1536,128]{0,1:T(8,128)}, f32[1536,128]{0,1:T(8,128)S(1)}, f32[1536,128]{0,1:T(8,128)S(1)}) fusion(f32[1536,128]{0,1:T(8,128)S(1)} %copy.59, f32[1536,128]{0,1:T(8,128)} %get-tuple-element.56, f32[]{:T(128)S(6)} %div.125, f32[1536,128]{0,1:T(8,128)} %copy.56, f32[1536,128]{0,1:T(8,128)} %copy.57), kind=kLoop, calls=%fused_computation.57 | loop fusion | flops 3145728 | bytes 5505028 | tf_op jit(solution)/shard_map/sub | solution.py:76
  262.1 2.3 copy.66
  264.3 2.7 multiply_subtract_fusion.1
  267.1 2.1 copy.67
  269.2 1.1 copy.68
  270.4 1.0 copy.69
  271.4 1.1 copy.70
  272.5 1.0 copy.71
  274.2 2.0 multiply_subtract_fusion.3
  276.2 1.0 multiply_subtract_fusion.2
  277.2 2.7 fusion.10
  279.9 1.6 all-gather.11.cloned.1.call-done
  281.5 2.5 fusion.31
  284.0 5.5 %all-to-all-start.1 = ((f32[8,32,512]{2,1,0:T(8,128)}), f32[8,32,512]{2,1,0:T(8,128)S(1)}, u32[]{:S(2)}, u32[]{:S(2)}) async-start(f32[8,32,512]{2,1,0:T(8,128)} %bitcast.10), calls=%async_computation.1 | async-start | bytes 1048576 | tf_op jit(solution)/shard_map/all_to_all | solution.py:184
  290.1 4.3 %fusion.1 = bf16[2048,512]{0,1:T(8,128)(2,1)} fusion(bf16[2048,512]{0,1:T(8,128)(2,1)S(1)} %copy-done.7, bf16[2048,512]{1,0:T(8,128)(2,1)} %all-gather.9.cloned.1.call-done, bf16[1536,512]{1,0:T(8,128)(2,1)} %all-gather.11.cloned.1.call-done), kind=kOutput, calls=%fused_computation.7 | convolution fusion | flops 1076887552 | bytes 6815744 | tf_op jit(solution)/shard_map/dot_general | solution.py:41
  294.4 3.9 %copy.65 = bf16[2048,512]{1,0:T(8,128)(2,1)} copy(bf16[2048,512]{0,1:T(8,128)(2,1)} %fusion.1) | data formatting | bytes 4194304
  298.3 2.8 fusion.8
  301.1 3.3 %all-to-all-done.1 = f32[8,32,512]{2,1,0:T(8,128)S(1)} async-done(((f32[8,32,512]{2,1,0:T(8,128)}), f32[8,32,512]{2,1,0:T(8,128)S(1)}, u32[]{:S(2)}, u32[]{:S(2)}) %all-to-all-start.1) | async-done | bytes 524320 | tf_op jit(solution)/shard_map/all_to_all | solution.py:184
  304.9 2.4 fusion.12
  (195 shorter events, 12.5 us)
Async XLA Ops:
  7.2 11.2 %copy-start = (bf16[256,512]{1,0:T(8,128)(2,1)S(1)}, bf16[256,512]{1,0:T(8,128)(2,1)}, u32[]{:S(2)}) copy-start(bf16[256,512]{1,0:T(8,128)(2,1)} %param.26) | copy-start | bytes 786436
  7.2 11.1 %copy-start.11 = (f32[1536,128]{1,0:T(8,128)S(1)}, f32[1536,128]{1,0:T(8,128)}, u32[]{:S(2)}) copy-start(f32[1536,128]{1,0:T(8,128)} %param.34) | copy-start | bytes 2359300
  7.2 11.1 %copy-start.62 = (s32[2048]{0:T(1024)S(1)}, s32[2048]{0:T(1024)}, u32[]{:S(2)}) copy-start(s32[2048]{0:T(1024)} %param.28) | copy-start | bytes 24580
  11.0 19.9 %all-to-all-start = ((bf16[8,32,512]{2,1,0:T(8,128)(2,1)}), bf16[8,32,512]{2,1,0:T(8,128)(2,1)S(1)}, u32[]{:S(2)}, u32[]{:S(2)}) async-start(bf16[8,32,512]{2,1,0:T(8,128)(2,1)} %bitcast), calls=%async_computation | async-start | bytes 524288 | tf_op jit(solution)/shard_map/all_to_all | solution.py:132
  18.2 54.2 %all-gather.5.cloned.1.call-start = ((), (), s32[]{:S(2)}) async-start(), calls=%async_computation.2 | async-start | bytes 2621440 | tf_op jit(solution)/shard_map/all_gather | solution.py:137
  18.3 21.8 %copy-start.13 = (bf16[1536,128]{1,0:T(8,128)(2,1)}, bf16[1536,128]{1,0:T(8,128)(2,1)S(1)}, u32[]{:S(2)}) copy-start(bf16[1536,128]{1,0:T(8,128)(2,1)S(1)} %convert_element_type.81) | copy-start | bytes 1179652
  18.4 9.2 %copy-start.60 = (s32[2048]{0:T(1024)S(1)}, s32[2048]{0:T(1024)}, u32[]{:S(2)}) copy-start(s32[2048]{0:T(1024)} %param.29) | copy-start | bytes 24580
  18.4 9.2 %copy-start.3 = (bf16[2048,512]{1,0:T(8,128)(2,1)S(1)}, bf16[2048,512]{1,0:T(8,128)(2,1)}, u32[]{:S(2)}) copy-start(bf16[2048,512]{1,0:T(8,128)(2,1)} %param.27) | copy-start | bytes 6291460
  40.1 3.8 %copy-start.16 = (f32[1024,128]{1,0:T(8,128)S(1)}, f32[1024,128]{1,0:T(8,128)}, u32[]{:S(2)}) copy-start(f32[1024,128]{1,0:T(8,128)} %param.36) | copy-start | bytes 1572868
  43.9 55.0 %all-gather.7.cloned.1.call-start = ((), (), s32[]{:S(2)}) async-start(), calls=%async_computation.3 | async-start | bytes 1310720 | tf_op jit(solution)/shard_map/all_gather | solution.py:118
  44.7 191.5 %all-reduce.4.cloned.1.call-start = ((), (), s32[]{:S(2)}) async-start(), calls=%async_computation.6 | async-start | bytes 3670016 | tf_op jit(solution)/shard_map/psum | solution.py:219
  46.6 2.5 copy-start.43
  46.6 2.6 copy-start.59
  46.6 2.6 copy-start.23
  46.6 10.3 %copy-start.25 = (f32[128,512]{1,0:T(8,128)S(1)}, f32[128,512]{1,0:T(8,128)}, u32[]{:S(2)}) copy-start(f32[128,512]{1,0:T(8,128)} %param.37) | copy-start | bytes 786436
  49.1 27.0 %copy-start.47 = (f32[1,512]{1,0:T(1,128)}, f32[1,512]{1,0:T(1,128)S(1)}, u32[]{:S(2)}) copy-start(f32[1,512]{1,0:T(1,128)S(1)} %get-tuple-element.89) | copy-start | bytes 6148
  49.1 27.0 %copy-start.49 = (f32[1,512]{1,0:T(1,128)}, f32[1,512]{1,0:T(1,128)S(1)}, u32[]{:S(2)}) copy-start(f32[1,512]{1,0:T(1,128)S(1)} %get-tuple-element.88) | copy-start | bytes 6148
  49.1 27.0 %copy-start.57 = (f32[1,512]{1,0:T(1,128)}, f32[1,512]{1,0:T(1,128)S(1)}, u32[]{:S(2)}) copy-start(f32[1,512]{1,0:T(1,128)S(1)} %get-tuple-element.87) | copy-start | bytes 6148
  49.2 26.9 %copy-start.45 = (f32[2048]{0:T(1024)}, f32[2048]{0:T(1024)S(1)}, u32[]{:S(2)}) copy-start(f32[2048]{0:T(1024)S(1)} %convert_element_type.80) | copy-start | bytes 24580
  49.2 7.7 %copy-start.31 = (bf16[128,512]{1,0:T(8,128)(2,1)}, bf16[128,512]{1,0:T(8,128)(2,1)S(1)}, u32[]{:S(2)}) copy-start(bf16[128,512]{1,0:T(8,128)(2,1)S(1)} %convert_element_type.83) | copy-start | bytes 393220
  77.4 3.7 %copy-start.22 = (bf16[1024,128]{1,0:T(8,128)(2,1)S(1)}, bf16[1024,128]{1,0:T(8,128)(2,1)}, u32[]{:S(2)}) copy-start(bf16[1024,128]{1,0:T(8,128)(2,1)} %convert_element_type.79) | copy-start | bytes 786436
  77.4 3.7 %copy-start.40 = (f32[256,128]{1,0:T(8,128)S(1)}, f32[256,128]{1,0:T(8,128)}, u32[]{:S(2)}) copy-start(f32[256,128]{1,0:T(8,128)} %fusion.42) | copy-start | bytes 393220
  77.4 3.7 %copy-start.71 = (f32[128]{0:T(128)S(1)}, f32[128]{0:T(128)}, u32[]{:S(2)}) copy-start(f32[128]{0:T(128)} %get-tuple-element.91) | copy-start | bytes 1540
  81.1 11.0 %copy-start.35 = (bf16[256,512]{1,0:T(8,128)(2,1)}, bf16[256,512]{1,0:T(8,128)(2,1)S(1)}, u32[]{:S(2)}) copy-start(bf16[256,512]{1,0:T(8,128)(2,1)S(1)} %fusion.13) | copy-start | bytes 786436
  81.1 8.6 %copy-start.14 = (bf16[256,512]{1,0:T(8,128)(2,1)S(1)}, bf16[256,512]{1,0:T(8,128)(2,1)}, u32[]{:S(2)}) copy-start(bf16[256,512]{1,0:T(8,128)(2,1)} %param.32) | copy-start | bytes 786436
  89.0 3.0 copy-start.34
  110.5 5.6 %copy-start.42 = (f32[2048]{0:T(1024)S(1)}, f32[2048]{0:T(1024)}, u32[]{:S(2)}) copy-start(f32[2048]{0:T(1024)} %copy-done.41) | copy-start | bytes 24580
  110.5 5.6 %copy-start.46 = (f32[2048]{0:T(1024)S(1)}, f32[2048]{0:T(1024)}, u32[]{:S(2)}) copy-start(f32[2048]{0:T(1024)} %copy-done.45) | copy-start | bytes 24580
  110.5 5.6 %copy-start.48 = (f32[1,512]{1,0:T(1,128)S(1)}, f32[1,512]{1,0:T(1,128)}, u32[]{:S(2)}) copy-start(f32[1,512]{1,0:T(1,128)} %copy-done.47) | copy-start | bytes 6148
  110.5 5.6 %copy-start.50 = (f32[1,512]{1,0:T(1,128)S(1)}, f32[1,512]{1,0:T(1,128)}, u32[]{:S(2)}) copy-start(f32[1,512]{1,0:T(1,128)} %copy-done.49) | copy-start | bytes 6148
  110.5 5.6 %copy-start.58 = (f32[1,512]{1,0:T(1,128)S(1)}, f32[1,512]{1,0:T(1,128)}, u32[]{:S(2)}) copy-start(f32[1,512]{1,0:T(1,128)} %copy-done.57) | copy-start | bytes 6148
  116.1 7.4 %copy-start.2 = (f32[2048,512]{0,1:T(8,128)S(1)}, f32[2048,512]{0,1:T(8,128)}, u32[]{:S(2)}) copy-start(f32[2048,512]{0,1:T(8,128)} %copy-done.1) | copy-start | bytes 12582916
  123.5 2.6 copy-start.32
  123.6 2.6 copy-start.72
  127.5 2.9 copy-start.18
  136.8 2.6 copy-start.29
  136.8 140.4 %all-gather.9.cloned.1.call-start = ((), (), s32[]{:S(2)}) async-start(), calls=%async_computation.4 | async-start | bytes 2621440 | tf_op jit(solution)/shard_map/all_gather | solution.py:173
  137.4 144.1 %all-gather.11.cloned.1.call-start = ((), (), s32[]{:S(2)}) async-start(), calls=%async_computation.5 | async-start | bytes 1966080 | tf_op jit(solution)/shard_map/all_gather | solution.py:117
  140.5 5.5 %copy-start.70 = (f32[128]{0:T(128)S(1)}, f32[128]{0:T(128)}, u32[]{:S(2)}) copy-start(f32[128]{0:T(128)} %get-tuple-element.101) | copy-start | bytes 1540
  140.5 5.6 %copy-start.54 = (f32[512]{0:T(512)S(1)}, f32[512]{0:T(512)}, u32[]{:S(2)}) copy-start(f32[512]{0:T(512)} %get-tuple-element.50) | copy-start | bytes 6148
  140.5 5.6 %copy-start.55 = (f32[512]{0:T(512)S(1)}, f32[512]{0:T(512)}, u32[]{:S(2)}) copy-start(f32[512]{0:T(512)} %get-tuple-element.53) | copy-start | bytes 6148
  140.5 5.6 %copy-start.56 = (f32[512]{0:T(512)S(1)}, f32[512]{0:T(512)}, u32[]{:S(2)}) copy-start(f32[512]{0:T(512)} %get-tuple-element.78) | copy-start | bytes 6148
  140.5 5.6 %copy-start.65 = (f32[512]{0:T(512)S(1)}, f32[512]{0:T(512)}, u32[]{:S(2)}) copy-start(f32[512]{0:T(512)} %get-tuple-element.80) | copy-start | bytes 6148
  141.7 104.7 %copy-start.8 = (bf16[2048,512]{0,1:T(8,128)(2,1)S(1)}, bf16[2048,512]{0,1:T(8,128)(2,1)}, u32[]{:S(2)}) copy-start(bf16[2048,512]{0,1:T(8,128)(2,1)} %get-tuple-element.83) | copy-start | bytes 6291460
  258.8 5.6 %copy-start.20 = (f32[1024,128]{0,1:T(8,128)S(1)}, f32[1024,128]{0,1:T(8,128)}, u32[]{:S(2)}) copy-start(f32[1024,128]{0,1:T(8,128)} %get-tuple-element.58) | copy-start | bytes 1572868
  267.1 3.3 %copy-start.21 = (f32[1024,128]{0,1:T(8,128)S(1)}, f32[1024,128]{0,1:T(8,128)}, u32[]{:S(2)}) copy-start(f32[1024,128]{0,1:T(8,128)} %get-tuple-element.70) | copy-start | bytes 1572868
  270.3 3.2 %copy-start.44 = (f32[6,512]{1,0:T(8,128)S(1)}, f32[6,512]{1,0:T(8,128)}, u32[]{:S(2)}) copy-start(f32[6,512]{1,0:T(8,128)} %param.39) | copy-start | bytes 36868
  270.3 3.2 %copy-start.51 = (f32[6,512]{1,0:T(8,128)S(1)}, f32[6,512]{1,0:T(8,128)}, u32[]{:S(2)}) copy-start(f32[6,512]{1,0:T(8,128)} %param.45) | copy-start | bytes 36868
  270.3 3.2 %copy-start.52 = (f32[6,512]{1,0:T(8,128)S(1)}, f32[6,512]{1,0:T(8,128)}, u32[]{:S(2)}) copy-start(f32[6,512]{1,0:T(8,128)} %param.51) | copy-start | bytes 36868
  270.3 3.8 %copy-start.24 = (f32[128,512]{1,0:T(8,128)S(1)}, f32[128,512]{1,0:T(8,128)}, u32[]{:S(2)}) copy-start(f32[128,512]{1,0:T(8,128)} %param.35) | copy-start | bytes 786436
  270.3 3.8 %copy-start.28 = (f32[128,512]{1,0:T(8,128)S(1)}, f32[128,512]{1,0:T(8,128)}, u32[]{:S(2)}) copy-start(f32[128,512]{1,0:T(8,128)} %get-tuple-element.57) | copy-start | bytes 786436
  270.3 3.8 %copy-start.37 = (f32[128,512]{1,0:T(8,128)S(1)}, f32[128,512]{1,0:T(8,128)}, u32[]{:S(2)}) copy-start(f32[128,512]{1,0:T(8,128)} %param.41) | copy-start | bytes 786436
  271.4 4.8 %copy-start.26 = (f32[128,512]{1,0:T(8,128)S(1)}, f32[128,512]{1,0:T(8,128)}, u32[]{:S(2)}) copy-start(f32[128,512]{1,0:T(8,128)} %param.37) | copy-start | bytes 786436
  271.4 4.8 %copy-start.27 = (f32[128,512]{1,0:T(8,128)S(1)}, f32[128,512]{1,0:T(8,128)}, u32[]{:S(2)}) copy-start(f32[128,512]{1,0:T(8,128)} %get-tuple-element.59) | copy-start | bytes 786436
  271.4 4.8 %copy-start.38 = (f32[128,512]{1,0:T(8,128)S(1)}, f32[128,512]{1,0:T(8,128)}, u32[]{:S(2)}) copy-start(f32[128,512]{1,0:T(8,128)} %param.43) | copy-start | bytes 786436
  271.4 4.8 %copy-start.39 = (f32[128,512]{1,0:T(8,128)S(1)}, f32[128,512]{1,0:T(8,128)}, u32[]{:S(2)}) copy-start(f32[128,512]{1,0:T(8,128)} %param.49) | copy-start | bytes 786436
  273.5 3.7 %copy-start.61 = (s32[2048]{0:T(1024)S(1)}, s32[2048]{0:T(1024)}, u32[]{:S(2)}) copy-start(s32[2048]{0:T(1024)} %param.29) | copy-start | bytes 24580
  279.9 9.6 %copy-start.67 = (f32[2,128]{1,0:T(2,128)S(1)}, f32[2,128]{1,0:T(2,128)}, u32[]{:S(2)}) copy-start(f32[2,128]{1,0:T(2,128)} %param.38) | copy-start | bytes 3076
  279.9 9.6 %copy-start.68 = (f32[2,128]{1,0:T(2,128)S(1)}, f32[2,128]{1,0:T(2,128)}, u32[]{:S(2)}) copy-start(f32[2,128]{1,0:T(2,128)} %param.44) | copy-start | bytes 3076
  279.9 9.6 %copy-start.69 = (f32[2,128]{1,0:T(2,128)S(1)}, f32[2,128]{1,0:T(2,128)}, u32[]{:S(2)}) copy-start(f32[2,128]{1,0:T(2,128)} %param.50) | copy-start | bytes 3076
  279.9 10.2 %copy-start.7 = (bf16[2048,512]{0,1:T(8,128)(2,1)S(1)}, bf16[2048,512]{0,1:T(8,128)(2,1)}, u32[]{:S(2)}) copy-start(bf16[2048,512]{0,1:T(8,128)(2,1)} %copy.50) | copy-start | bytes 6291460
  284.0 20.4 %all-to-all-start.1 = ((f32[8,32,512]{2,1,0:T(8,128)}), f32[8,32,512]{2,1,0:T(8,128)S(1)}, u32[]{:S(2)}, u32[]{:S(2)}) async-start(f32[8,32,512]{2,1,0:T(8,128)} %bitcast.10), calls=%async_computation.1 | async-start | bytes 1048576 | tf_op jit(solution)/shard_map/all_to_all | solution.py:184
  294.4 3.9 %copy-start.64 = (s32[2048]{0:T(1024)S(1)}, s32[2048]{0:T(1024)}, u32[]{:S(2)}) copy-start(s32[2048]{0:T(1024)} %param.28) | copy-start | bytes 24580
  298.3 6.6 %copy-start.10 = (f32[256,1024]{1,0:T(8,128)S(1)}, f32[256,1024]{1,0:T(8,128)}, u32[]{:S(2)}) copy-start(f32[256,1024]{1,0:T(8,128)} %copy-done.9) | copy-start | bytes 3145732
  (16 other events, 25.9 us)
Sparse Core Ops, SparseCore 0:
  44.0 27.3 all-gather.4
  73.5 18.9 all-gather.6
  136.9 99.2 all-reduce.3
  237.6 22.5 all-gather.8
  261.6 19.8 all-gather.10
where the time goes:
time: 316 us; the launch traced here: 315 us
  blocking collectives  79.8 us (25%)
  local copies, waits for them, and re-layouts  71.4 us (23%)
  waiting for transfers between devices  55.7 us (18%)
  matrix products  39.6 us (13%)
  other arithmetic  35 us (11%)
  between operations  20.4 us (6%)
  starting transfers between devices  13 us (4%)
    psum x1, waiting for transfers between devices, local(): lax.psum((edge_in_grad, edge_out_grad, node_in_grad, node_out_grad, bias_...  49.7 us
    psum x1, blocking collectives, local(): lax.psum((edge_in_grad, edge_out_grad, node_in_grad, node_out_grad, bias_...  39.1 us
    unnamed x162, local copies, waits for them, and re-layouts  34.9 us
    gather x2, local copies, waits for them, and re-layouts, local(): node_input_grad[:, latent:][edge_receiver]  14.4 us
    dot_general x9, matrix products, dot_rows(): lax.dot_general(left, right, (((0,), (0,)), ((), ())), preferred_element_...  11.6 us
    dot_general x7, matrix products, matmul(): return jnp.dot(left, right, preferred_element_type=jnp.float32)  11.5 us
    all_gather x1, blocking collectives, local(): lax.all_gather(node_second, 'tp', axis=0, tiled=True)  10.9 us
    sub x6, other arithmetic, adam_update(): return (weight - rate * moved, first_new, second_new)  10.2 us
  transfers between devices with their start and end apart: 7, of which 3 were waited for; matrix products, arithmetic and copies ran while one was open for 27% of the time, Pallas kernels for 0%

commit v1 on v0

v1 whole, which is shorter than its diff:
```python
import functools
import types

import jax
import jax.numpy as jnp
from jax import lax
from jax.experimental import pallas as pl
from jax.experimental.pallas import tpu as pltpu
from jax.sharding import PartitionSpec as P

BF = jnp.bfloat16
F32 = jnp.float32
MESH = pl.DeviceIdType.MESH
LANES = 128
TILE = 256

beta_one = 0.9
beta_two = 0.999
adam_step = 7.0
adam_eps = 1e-08
learn_rate = 0.05
vector_rate = 0.3
decay_rate = 0.1
clip_level = 1.0


def mm(left, right):
    return jnp.dot(left, right, preferred_element_type=F32)


def nt(left, right):
    return lax.dot_general(left, right, (((1,), (1,)), ((), ())), preferred_element_type=F32)


def tn(left, right):
    return lax.dot_general(left, right, (((0,), (0,)), ((), ())), preferred_element_type=F32)


def two(values):
    high = values.astype(BF)
    return high, (values - high.astype(F32)).astype(BF)


def aligned(start, step):
    return start if isinstance(start, int) else pl.multiple_of(start, step)


def rows_of(start, size, step=16):
    return pl.ds(aligned(start, step), size)


def hot(cond):
    return jnp.where(cond, 1.0, 0.0).astype(BF)


def normalize(values):
    center = values - jnp.mean(values, axis=1, keepdims=True)
    inverse = lax.rsqrt(jnp.mean(center * center, axis=1, keepdims=True) + 1e-05)
    return center * inverse, inverse


def norm_back(scaled, normed, inverse):
    first = jnp.mean(scaled, axis=1, keepdims=True)
    second = jnp.mean(scaled * normed, axis=1, keepdims=True)
    return inverse * (scaled - first - normed * second)


def row_sum(values):
    return jnp.sum(values, axis=0, keepdims=True)


def layer(names, d, *refs):
    s = types.SimpleNamespace(**dict(zip(names, refs, strict=True)))
    R, N, E, L, H, Q, CAP = d.R, d.N, d.E, d.L, d.H, d.Q, d.CAP
    EH, S = E // 2, R * CAP
    tiles = EH // TILE
    r = lax.axis_index("rows")
    t = lax.axis_index("tp")
    h, c = t // 2, lax.rem(t, 2)
    oh, oc = 1 - h, 1 - c
    pair = t + 1 - 2 * c
    far = t + 2 - 4 * h
    diag = pair + 2 - 4 * h
    edge0 = c * EH

    def local(src, dst, sem):
        return pltpu.make_async_copy(src, dst, sem)

    def remote(src, dst, send, recv, device):
        return pltpu.make_async_remote_copy(
            src_ref=src, dst_ref=dst, send_sem=send, recv_sem=recv, device_id=device, device_id_type=MESH
        )

    loads = [
        local(s.wei_h, s.wei32, s.lsem.at[0]),
        local(s.nf_h, s.nf, s.lsem.at[1]),
        local(s.ef_h.at[rows_of(edge0, EH)], s.ef, s.lsem.at[2]),
        local(s.weo_h, s.weo32, s.lsem.at[3]),
        local(s.wni_h, s.wni32, s.lsem.at[4]),
        local(s.wno_h, s.wno32, s.lsem.at[5]),
        local(s.ncot_h, s.ncot, s.lsem.at[6]),
        local(s.ecot_h.at[rows_of(edge0, EH)], s.ecot, s.lsem.at[7]),
    ]
    for load in loads:
        load.start()

    barrier = pltpu.get_barrier_semaphore()
    for peer in (pair, far, diag):
        pl.semaphore_signal(barrier, inc=1, device_id=(r, peer), device_id_type=MESH)

    def greet(k, carry):
        pl.semaphore_signal(barrier, inc=1, device_id=(lax.rem(r + k, R), t), device_id_type=MESH)
        return carry

    lax.fori_loop(1, R, greet, 0)
    pl.semaphore_wait(barrier, R + 2)

    def block(i, tt):
        lane = pl.ds(pl.multiple_of(tt * Q, Q), Q)
        if i < 3:
            half_lane = pl.ds(pl.multiple_of(lax.rem(tt, 2) * Q, Q), Q)
            return s.wei.at[tt // 2, pl.ds((0, 2 * L, L)[i], L), half_lane]
        if i == 3:
            return s.weo.at[lane, :]
        if i < 6:
            return s.wni.at[pl.ds((L, 0)[i - 4], L), lane]
        if i == 6:
            return s.wno.at[lane, :]
        return s.bias.at[:, lane]

    def weight_copy(i, way):
        who = (t, t, far)[way]
        ref = block(i, who)
        return remote(ref, ref, s.wsend.at[i, way], s.wrecv.at[i, way], (r, (pair, far, pair)[way]))

    def weight_wait(i, way):
        ref = block(i, (pair, far, diag)[way])
        remote(ref, ref, s.wsend.at[i, way], s.wrecv.at[i, way], (r, (pair, far, pair)[way])).wait_recv()

    def weight_send(i):
        for way in (1, 0):
            weight_copy(i, way).start()

    def weight_forward(i):
        weight_wait(i, 1)
        weight_copy(i, 2).start()

    def weight_done(i):
        for way in (0, 1, 2):
            weight_copy(i, way).wait_send()

    own_lane = pl.ds(pl.multiple_of(t * Q, Q), Q)
    own_half_lane = pl.ds(pl.multiple_of(c * Q, Q), Q)
    loads[0].wait()
    for i in range(3):
        at = pl.ds((0, 2 * L, L)[i], L)
        s.wei[h, at, own_half_lane] = s.wei32[at, :].astype(BF)
        weight_send(i)
    s.bias[:, own_lane] = s.hb[...]
    weight_send(7)
    loads[1].wait()

    def serve(k, carry):
        at = rows_of(k * TILE, TILE)
        table = hot(s.serve_col[at, :] == lax.broadcasted_iota(jnp.int32, (TILE, N), 1))
        s.served[at, :] = mm(table, s.nf[...]).astype(BF)
        return carry

    lax.fori_loop(0, S // TILE, serve, 0)
    mine = rows_of(r * CAP, CAP)

    def served_copy(k):
        to = lax.rem(r + k, R)
        return remote(
            s.served.at[rows_of(to * CAP, CAP)], s.slots.at[mine], s.ssend.at[k], s.srecv.at[k], (to, t)
        )

    def served_start(k, carry):
        served_copy(k).start()
        return carry

    lax.fori_loop(1, R, served_start, 0)
    s.slots[mine, :] = s.served[mine, :]

    loads[3].wait()
    s.weo[own_lane, :] = s.weo32[...].astype(BF)
    weight_send(3)
    loads[4].wait()
    for i in (4, 5):
        at = pl.ds((L, 0)[i - 4], L)
        s.wni[at, own_lane] = s.wni32[at, :].astype(BF)
        weight_send(i)
    loads[5].wait()
    s.wno[own_lane, :] = s.wno32[...].astype(BF)
    weight_send(6)

    per = EH // LANES
    at = rows_of(c * per, per, 8)
    for source, target in ((s.rec2, s.rcol), (s.slot2, s.scol), (s.mask2, s.mcol)):
        turned = jnp.transpose(source[at, :].astype(F32))
        for k in range(per):
            target[k * LANES : (k + 1) * LANES, :] = turned[:, k : k + 1]
    lanes_here = pl.ds(pl.multiple_of(edge0, EH), EH)
    s.rhot_t[...] = hot(s.rec1[:, lanes_here] == lax.broadcasted_iota(jnp.int32, (N, EH), 0))

    def slot_table(k, carry):
        rows = rows_of(k * TILE, TILE)
        s.shot_t[rows, :] = hot(
            s.slot1[:, lanes_here] == lax.broadcasted_iota(jnp.int32, (TILE, EH), 0) + k * TILE
        )
        return carry

    lax.fori_loop(0, S // TILE, slot_table, 0)

    def receivers(k, carry):
        rows = rows_of(k * TILE, TILE)
        index = s.rcol[rows, :].astype(jnp.int32)
        table = hot(index == lax.broadcasted_iota(jnp.int32, (TILE, N), 1))
        s.rhot[rows, :] = table
        s.xr[rows, :] = mm(table, s.nf[...]).astype(BF)
        return carry

    lax.fori_loop(0, tiles, receivers, 0)

    def served_wait(k, carry):
        source = lax.rem(r + R - k, R)
        ref = s.slots.at[rows_of(source * CAP, CAP)]
        remote(ref, ref, s.ssend.at[k], s.srecv.at[k], (source, t)).wait_recv()
        served_copy(k).wait_send()
        return carry

    lax.fori_loop(1, R, served_wait, 0)

    def senders(k, carry):
        rows = rows_of(k * TILE, TILE)
        index = s.scol[rows, :].astype(jnp.int32)
        table = hot(index == lax.broadcasted_iota(jnp.int32, (TILE, S), 1))
        s.xs[rows, :] = mm(table, s.slots[...]).astype(BF)
        return carry

    lax.fori_loop(0, tiles, senders, 0)
    loads[2].wait()

    def first_layer(which):
        def body(k, carry):
            rows = rows_of(k * TILE, TILE)
            value = mm(s.ef[rows, :], s.wei[which, 0:L, :])
            value = value + mm(s.xr[rows, :], s.wei[which, 2 * L : 3 * L, :])
            s.pre[which, rows, :] = value + mm(s.xs[rows, :], s.wei[which, L : 2 * L, :])
            return carry

        lax.fori_loop(0, tiles, body, 0)

    for i in range(3):
        weight_wait(i, 0)
    first_layer(h)
    for i in range(4):
        weight_forward(i)
    for i in range(3):
        weight_wait(i, 2)
    first_layer(oh)
    weight_wait(7, 0)
    weight_forward(7)
    weight_wait(7, 2)
    weight_wait(3, 0)
    weight_wait(3, 2)

    half = H // 2
    s.aggp[...] = jnp.zeros_like(s.aggp)

    def out_copies(k, source, target, which):
        here = s.__dict__[source].at[rows_of(k * TILE, TILE)]
        there = s.__dict__[target].at[rows_of(edge0 + k * TILE, TILE)]
        other = s.__dict__[target].at[rows_of(oc * EH + k * TILE, TILE)]
        keep = local(here, there, s.osem.at[which, k])
        send = remote(here, there, s.osend.at[which, k], s.orecv.at[which, k], (r, pair))
        take = remote(here, other, s.osend.at[which, k], s.orecv.at[which, k], (r, pair))
        return keep, send, take

    def forward(k, carry):
        rows = rows_of(k * TILE, TILE)
        hidden = []
        for p in (0, 1):
            pre = s.pre[p, rows, :] + s.bias[0:1, p * half : (p + 1) * half]
            sig = 1.0 / (1.0 + jnp.exp(-pre))
            value = (pre * sig).astype(BF)
            s.hid[p, rows, :] = value
            s.pre[p, rows, :] = sig * (1.0 + pre * (1.0 - sig))
            hidden.append(value)
        outer = mm(hidden[0], s.weo[0:half, :]) + mm(hidden[1], s.weo[half:H, :]) + s.fv[0:1, :]
        normed, inverse = normalize(outer)
        s.normed[rows, :] = normed
        s.inv[rows, :] = inverse
        masked = s.mcol[rows, :] * (normed * s.fv[1:2, :] + s.fv[2:3, :])
        s.ne[rows, :] = (s.ef[rows, :].astype(F32) + masked).astype(BF)
        keep, send, _ = out_copies(k, "ne", "ne_h", 0)
        keep.start()
        send.start()
        high, low = two(masked)
        table = s.rhot_t[:, pl.ds(pl.multiple_of(k * TILE, TILE), TILE)]
        s.aggp[...] += mm(table, high) + mm(table, low)
        return carry

    lax.fori_loop(0, tiles, forward, 0)
    swap = remote(s.aggp, s.aggr, s.xsend.at[0], s.xrecv.at[0], (r, pair))
    swap.start()
    for i in (4, 5, 6):
        weight_wait(i, 0)
        weight_forward(i)
    for i in (4, 5, 6):
        weight_wait(i, 2)
    own_term = mm(s.nf[...], s.wni[0:L, :])
    swap.wait()

    agg = (s.aggp[...] + s.aggr[...]).astype(BF)
    pre = own_term + mm(agg, s.wni[L : 2 * L, :]) + s.bias[1:2, :]
    sig = 1.0 / (1.0 + jnp.exp(-pre))
    node_hidden = (pre * sig).astype(BF)
    slope_of = sig * (1.0 + pre * (1.0 - sig))
    outer = mm(node_hidden, s.wno[...]) + s.fv[3:4, :]
    normed, inverse = normalize(outer)
    s.nn[...] = (s.nf[...].astype(F32) + (normed * s.fv[4:5, :] + s.fv[5:6, :])).astype(BF)
    nn_copy = local(s.nn, s.nn_h, s.nsem.at[0])
    nn_copy.start()
    loads[6].wait()
    up = s.ncot[...].astype(F32)
    node_outer_grad = norm_back(up * s.fv[4:5, :], normed, inverse).astype(BF)
    node_slope = (nt(node_outer_grad, s.wno[...]) * slope_of).astype(BF)
    agg_high, agg_low = two(nt(node_slope, s.wni[L : 2 * L, :]))
    s.agh[...] = agg_high
    s.agl[...] = agg_low
    s.ntp[...] = 0.5 * (up + nt(node_slope, s.wni[0:L, :]))
    s.vsum[0:3, :] = jnp.zeros((3, L), F32)
    s.vsum[3:4, :] = 0.5 * row_sum(node_outer_grad.astype(F32))
    s.vsum[4:5, :] = 0.5 * row_sum(up * normed)
    s.vsum[5:6, :] = 0.5 * row_sum(up)
    s.vsum[6:7, :] = jnp.zeros((1, H), F32)
    s.vsum[7:8, :] = 0.5 * row_sum(node_slope.astype(F32))
    for q in range(H // Q):
        s.nsl[q] = node_slope[:, q * Q : (q + 1) * Q]
        s.nhid[q] = node_hidden[:, q * Q : (q + 1) * Q]
    s.g[c, 0:L, :] = tn(s.nf[...], s.nsl[t])
    s.g[c, L : 2 * L, :] = tn(agg, s.nsl[t])
    node_out_grad = tn(s.nhid[t], node_outer_grad)
    for q in range(L // LANES):
        s.g[c, 2 * L + q * Q : 2 * L + (q + 1) * Q, :] = node_out_grad[:, q * LANES : (q + 1) * LANES]

    loads[7].wait()
    s.rs[...] = jnp.zeros_like(s.rs)
    s.ss[...] = jnp.zeros_like(s.ss)

    def backward(k, carry):
        rows = rows_of(k * TILE, TILE)
        cot = s.ecot[rows, :].astype(F32)
        table = s.rhot[rows, :]
        up = s.mcol[rows, :] * (cot + (mm(table, s.agh[...]) + mm(table, s.agl[...])))
        normed = s.normed[rows, :]
        grad = norm_back(up * s.fv[1:2, :], normed, s.inv[rows, :]).astype(BF)
        s.og[rows, :] = grad
        s.vsum[0:1, :] += row_sum(grad.astype(F32))
        s.vsum[1:2, :] += row_sum(up * normed)
        s.vsum[2:3, :] += row_sum(up)
        wide = []
        for p in (0, 1):
            value = nt(grad, s.weo[p * half : (p + 1) * half, :]) * s.pre[p, rows, :]
            value = value.astype(BF)
            s.sl[p, rows, :] = value
            s.vsum[6:7, p * half : (p + 1) * half] += row_sum(value.astype(F32))
            wide.append(value)
        s.eg[rows, :] = (cot + (nt(wide[0], s.wei[0, 0:L, :]) + nt(wide[1], s.wei[1, 0:L, :]))).astype(BF)
        keep, send, _ = out_copies(k, "eg", "eg_h", 1)
        keep.start()
        send.start()
        lanes = pl.ds(pl.multiple_of(k * TILE, TILE), TILE)
        table = s.rhot_t[:, lanes]
        for p in (0, 1):
            s.rs[p] += mm(table, wide[p])

        def slots(j, carry):
            at = rows_of(j * TILE, TILE)
            for p in (0, 1):
                s.ss[p, at, :] += mm(s.shot_t[at, lanes], wide[p])
            return carry

        lax.fori_loop(0, S // TILE, slots, 0)
        return carry

    lax.fori_loop(0, tiles, backward, 0)

    def slot_grad(k, carry):
        at = rows_of(k * TILE, TILE)
        value = nt(s.ss[0, at, :].astype(BF), s.wei[0, L : 2 * L, :])
        s.served[at, :] = (value + nt(s.ss[1, at, :].astype(BF), s.wei[1, L : 2 * L, :])).astype(BF)
        return carry

    lax.fori_loop(0, S // TILE, slot_grad, 0)

    def back_copy(k):
        to = lax.rem(r + k, R)
        return remote(
            s.served.at[rows_of(to * CAP, CAP)], s.ret.at[mine], s.bsend.at[k], s.brecv.at[k], (to, t)
        )

    def back_start(k, carry):
        back_copy(k).start()
        return carry

    lax.fori_loop(1, R, back_start, 0)
    s.ret[mine, :] = s.served[mine, :]

    node_rows, edge_out_rows, edge_in_rows = 0, 3 * L, 4 * L
    edge_part = tn(s.ef[...], s.sl[h])
    recv_part = tn(s.nf[...], s.rs[h].astype(BF))
    out_part = tn(s.hid[h], s.og[...])
    for p in (0, 1):
        cols = slice(p * Q, (p + 1) * Q)
        s.g[p, edge_in_rows : edge_in_rows + L, :] = edge_part[:, cols]
        s.g[p, edge_in_rows + 2 * L : edge_in_rows + 3 * L, :] = recv_part[:, cols]
        for q in range(L // LANES):
            at = edge_out_rows + q * Q
            s.g[p, at : at + Q, :] = out_part[cols, q * LANES : (q + 1) * LANES]
        s.g[p, edge_in_rows + L : edge_in_rows + 2 * L, :] = jnp.zeros((L, Q), F32)

    def sender_part(k, carry):
        at = rows_of(k * TILE, TILE)
        value = tn(s.slots[at, :], s.ss[h, at, :].astype(BF))
        for p in (0, 1):
            s.g[p, edge_in_rows + L : edge_in_rows + 2 * L, :] += value[:, p * Q : (p + 1) * Q]
        return carry

    lax.fori_loop(0, S // TILE, sender_part, 0)

    def partner(bit):
        value = lax.rem(r // bit, 2)
        return value, (r + bit - 2 * bit * value, t)

    def plan(base, size, paired):
        steps = []
        low, count = base, size
        if paired:
            steps.append(("pair", (r, pair), base, base, size))
        bit = 1
        while bit < R:
            value, device = partner(bit)
            if (count // 2) % 16 == 0:
                count = count // 2
                keep, send = low + value * count, low + (1 - value) * count
                steps.append(("halve", device, send, keep, count))
                low = keep
            else:
                steps.append(("whole", device, low, low, count))
            bit *= 2
        return steps

    def reduce_copy(n, k, step):
        kind, device, send, keep, count = step
        return remote(
            s.sb.at[rows_of(send, count)],
            s.rb.at[k, rows_of(send, count)],
            s.gsend.at[n, k],
            s.grecv.at[n, k],
            device,
        )

    def reduce_start(n, k, step):
        kind, device, send, keep, count = step
        at = rows_of(send, count)
        s.sb[at, :] = s.g[oc if kind == "pair" else c, at, :].astype(BF)
        reduce_copy(n, k, step).start()

    def reduce_finish(n, k, step):
        kind, device, send, keep, count = step
        reduce_copy(n, k, step).wait_send()
        at = rows_of(keep, count)
        ref = s.rb.at[k, at]
        remote(ref, ref, s.gsend.at[n, k], s.grecv.at[n, k], device).wait_recv()
        own = s.sb[at, :].astype(F32) if kind == "whole" else s.g[c, at, :]
        s.g[c, at, :] = own + s.rb[k, at, :].astype(F32)

    def spread_copy(n, k, step, start):
        kind, device, send, keep, count = step
        at = rows_of(start, count)
        return remote(s.fin.at[at], s.fin.at[at], s.fsend.at[n, k], s.frecv.at[n, k], device)

    def chunk_sum(n, steps):
        for k, step in enumerate(steps):
            reduce_start(n, k, step)
            reduce_finish(n, k, step)
        kind, device, send, keep, count = steps[-1]
        at = rows_of(keep, count)
        s.fin[at, :] = s.g[c, at, :].astype(BF)
        for k, step in reversed(list(enumerate(steps))):
            if step[0] == "halve":
                spread_copy(n, k, step, step[3]).start()
                spread_copy(n, k, step, step[3]).wait_send()
                spread_copy(n, k, step, step[2]).wait_recv()

    peers = [(r, pair)]
    bit = 1
    while bit < R:
        peers.append(partner(bit)[1])
        bit *= 2
    for k, device in enumerate(peers):
        copy = remote(s.vsum, s.vrecv.at[k], s.vsem.at[0, k], s.vsem.at[1, k], device)
        copy.start()
        copy.wait()
        s.vsum[...] += s.vrecv[k]

    chunk_sum(0, plan(node_rows, 3 * L, False))
    chunk_sum(1, plan(edge_out_rows, 4 * L, True))

    def back_wait(k, carry):
        source = lax.rem(r + R - k, R)
        ref = s.ret.at[rows_of(source * CAP, CAP)]
        remote(ref, ref, s.bsend.at[k], s.brecv.at[k], (source, t)).wait_recv()
        back_copy(k).wait_send()
        return carry

    lax.fori_loop(1, R, back_wait, 0)
    for p in (0, 1):
        s.ntp[...] += nt(s.rs[p].astype(BF), s.wei[p, 2 * L : 3 * L, :])

    def gathered(k, carry):
        lanes = pl.ds(pl.multiple_of(k * TILE, TILE), TILE)
        table = hot(s.serve_row[:, lanes] == lax.broadcasted_iota(jnp.int32, (N, TILE), 0))
        s.ntp[...] += mm(table, s.ret[rows_of(k * TILE, TILE), :])
        return carry

    lax.fori_loop(0, S // TILE, gathered, 0)
    swap = remote(s.ntp, s.ntr, s.xsend.at[1], s.xrecv.at[1], (r, pair))
    swap.start()
    swap.wait()
    s.ng[...] = (s.ntp[...] + s.ntr[...]).astype(BF)
    ng_copy = local(s.ng, s.ng_h, s.nsem.at[1])
    ng_copy.start()

    total = jnp.zeros((8, LANES), F32)
    squares = s.fin[...].astype(F32)
    squares = squares * squares
    total = jnp.sum(squares.reshape(-1, 8, LANES), axis=0)
    own_bias = s.vsum[:, own_lane]
    row = lax.broadcasted_iota(jnp.int32, (8, LANES), 0)
    total = total + jnp.where(row >= 6, own_bias * own_bias, 0.0)
    own_rows = rows_of(t * 8, 8, 8)
    s.nsq[own_rows, :] = total
    for k, peer in enumerate((pair, far, diag)):
        ref = s.nsq.at[own_rows]
        remote(ref, ref, s.qsem.at[0, k], s.qsem.at[1, k], (r, peer)).start()
    for k, peer in enumerate((pair, far, diag)):
        ref = s.nsq.at[rows_of(peer * 8, 8, 8)]
        remote(ref, ref, s.qsem.at[0, k], s.qsem.at[1, k], (r, peer)).wait()
    total = s.nsq[0:8, :] + s.nsq[8:16, :] + s.nsq[16:24, :] + s.nsq[24:32, :]
    vectors = s.vsum[0:6, :]
    square = jnp.sum(total) + jnp.sum(vectors * vectors)
    s.norm_o[...] = jnp.sqrt(jnp.full((8, LANES), square, F32))
    s.fin_o[...] = s.fin[...]
    s.vec_o[...] = s.vsum[...]

    for i in range(8):
        weight_done(i)

    def finish(k, carry):
        for source, target, which in (("ne", "ne_h", 0), ("eg", "eg_h", 1)):
            keep, send, take = out_copies(k, source, target, which)
            keep.wait()
            send.wait_send()
            take.wait_recv()
        return carry

    lax.fori_loop(0, tiles, finish, 0)
    nn_copy.wait()
    ng_copy.wait()


def adam(weight, first, second, gradient, factor, rate):
    clipped = gradient * factor
    first_new = beta_one * first + (1.0 - beta_one) * clipped
    second_new = beta_two * second + (1.0 - beta_two) * clipped * clipped
    bias_one = 1.0 - beta_one**adam_step
    bias_two = 1.0 - beta_two**adam_step
    moved = first_new / bias_one / (jnp.sqrt(second_new / bias_two) + adam_eps) + decay_rate * weight
    return weight - rate * moved, first_new, second_new


def update(L, fin, vec, bias_grad, norm, *refs):
    ins, outs = refs[:18], refs[18:]
    factor = clip_level / jnp.maximum(norm[0:1, 0:1], clip_level)

    def one(k, grad, at, rate):
        values = adam(ins[k][at], ins[6 + k][at], ins[12 + k][at], grad, factor, rate)
        for n, value in enumerate(values):
            outs[6 * n + k][at] = value

    one(2, fin[0 : 2 * L, :].astype(F32), (slice(None), slice(None)), learn_rate)
    one(0, fin[4 * L : 7 * L, :].astype(F32), (slice(None), slice(None)), learn_rate)
    for q in range(L // LANES):
        at = (slice(None), slice(q * LANES, (q + 1) * LANES))
        one(3, fin[2 * L + q * LANES : 2 * L + (q + 1) * LANES, :].astype(F32), at, learn_rate)
        one(1, fin[3 * L + q * LANES : 3 * L + (q + 1) * LANES, :].astype(F32), at, learn_rate)
    one(4, bias_grad[...], (slice(None), slice(None)), vector_rate)
    one(5, vec[0:6, :], (slice(None), slice(None)), vector_rate)


def device_step(
    node_feats,
    edge_feats,
    edge_receiver,
    edge_slot,
    edge_mask,
    serve_rows,
    node_cot,
    edge_cot,
    *rest,
):
    weights = rest[:6]
    d = types.SimpleNamespace()
    d.R = lax.axis_size("rows")
    d.N, d.L = node_feats.shape
    d.E = edge_feats.shape[0]
    d.Q = weights[0].shape[1]
    d.H = d.Q * lax.axis_size("tp")
    d.CAP = serve_rows.shape[1]
    R, N, E, L, H, Q = d.R, d.N, d.E, d.L, d.H, d.Q
    EH, S = E // 2, R * d.CAP
    steps = 1
    while 2 ** (steps - 1) < R:
        steps += 1
    tiles = EH // TILE
    G = 7 * L
    any_spec = pl.BlockSpec(memory_space=pl.ANY)
    vmem_spec = pl.BlockSpec(memory_space=pltpu.VMEM)
    inputs = dict(
        nf_h=(node_feats, any_spec),
        ef_h=(edge_feats, any_spec),
        ncot_h=(node_cot, any_spec),
        ecot_h=(edge_cot, any_spec),
        wei_h=(weights[0], any_spec),
        weo_h=(weights[1], any_spec),
        wni_h=(weights[2], any_spec),
        wno_h=(weights[3], any_spec),
        hb=(jnp.pad(weights[4], ((0, 6), (0, 0))), vmem_spec),
        fv=(jnp.pad(weights[5], ((0, 2), (0, 0))), vmem_spec),
        rec2=(edge_receiver.reshape(-1, LANES), vmem_spec),
        slot2=(edge_slot.reshape(-1, LANES), vmem_spec),
        mask2=(edge_mask.reshape(-1, LANES), vmem_spec),
        rec1=(edge_receiver.reshape(1, -1), vmem_spec),
        slot1=(edge_slot.reshape(1, -1), vmem_spec),
        serve_col=(serve_rows.reshape(-1, 1), vmem_spec),
        serve_row=(serve_rows.reshape(1, -1), vmem_spec),
    )
    outputs = dict(
        nn_h=(jax.ShapeDtypeStruct((N, L), BF), any_spec),
        ne_h=(jax.ShapeDtypeStruct((E, L), BF), any_spec),
        ng_h=(jax.ShapeDtypeStruct((N, L), BF), any_spec),
        eg_h=(jax.ShapeDtypeStruct((E, L), BF), any_spec),
        fin_o=(jax.ShapeDtypeStruct((G, Q), BF), vmem_spec),
        vec_o=(jax.ShapeDtypeStruct((8, L), F32), vmem_spec),
        norm_o=(jax.ShapeDtypeStruct((8, LANES), F32), vmem_spec),
    )
    dma = pltpu.SemaphoreType.DMA
    scratch = dict(
        wei32=pltpu.VMEM((3 * L, Q), F32),
        weo32=pltpu.VMEM((Q, L), F32),
        wni32=pltpu.VMEM((2 * L, Q), F32),
        wno32=pltpu.VMEM((Q, L), F32),
        nf=pltpu.VMEM((N, L), BF),
        ef=pltpu.VMEM((EH, L), BF),
        ncot=pltpu.VMEM((N, L), BF),
        ecot=pltpu.VMEM((EH, L), BF),
        wei=pltpu.VMEM((2, 3 * L, H // 2), BF),
        weo=pltpu.VMEM((H, L), BF),
        wni=pltpu.VMEM((2 * L, H), BF),
        wno=pltpu.VMEM((H, L), BF),
        bias=pltpu.VMEM((8, H), F32),
        served=pltpu.VMEM((S, L), BF),
        slots=pltpu.VMEM((S, L), BF),
        ret=pltpu.VMEM((S, L), BF),
        rcol=pltpu.VMEM((EH, 1), F32),
        scol=pltpu.VMEM((EH, 1), F32),
        mcol=pltpu.VMEM((EH, 1), F32),
        rhot=pltpu.VMEM((EH, N), BF),
        rhot_t=pltpu.VMEM((N, EH), BF),
        shot_t=pltpu.VMEM((S, EH), BF),
        xr=pltpu.VMEM((EH, L), BF),
        xs=pltpu.VMEM((EH, L), BF),
        pre=pltpu.VMEM((2, EH, H // 2), F32),
        hid=pltpu.VMEM((2, EH, H // 2), BF),
        normed=pltpu.VMEM((EH, L), F32),
        inv=pltpu.VMEM((EH, 1), F32),
        ne=pltpu.VMEM((EH, L), BF),
        eg=pltpu.VMEM((EH, L), BF),
        aggp=pltpu.VMEM((N, L), F32),
        aggr=pltpu.VMEM((N, L), F32),
        nn=pltpu.VMEM((N, L), BF),
        ng=pltpu.VMEM((N, L), BF),
        agh=pltpu.VMEM((N, L), BF),
        agl=pltpu.VMEM((N, L), BF),
        ntp=pltpu.VMEM((N, L), F32),
        ntr=pltpu.VMEM((N, L), F32),
        nsl=pltpu.VMEM((H // Q, N, Q), BF),
        nhid=pltpu.VMEM((H // Q, N, Q), BF),
        og=pltpu.VMEM((EH, L), BF),
        sl=pltpu.VMEM((2, EH, H // 2), BF),
        rs=pltpu.VMEM((2, N, H // 2), F32),
        ss=pltpu.VMEM((2, S, H // 2), F32),
        g=pltpu.VMEM((2, G, Q), F32),
        sb=pltpu.VMEM((G, Q), BF),
        rb=pltpu.VMEM((steps, G, Q), BF),
        fin=pltpu.VMEM((G, Q), BF),
        vsum=pltpu.VMEM((8, L), F32),
        vrecv=pltpu.VMEM((steps, 8, L), F32),
        nsq=pltpu.VMEM((32, LANES), F32),
        lsem=dma((8,)),
        wsend=dma((8, 3)),
        wrecv=dma((8, 3)),
        ssend=dma((R,)),
        srecv=dma((R,)),
        bsend=dma((R,)),
        brecv=dma((R,)),
        osem=dma((2, tiles)),
        osend=dma((2, tiles)),
        orecv=dma((2, tiles)),
        xsend=dma((2,)),
        xrecv=dma((2,)),
        nsem=dma((2,)),
        gsend=dma((2, steps)),
        grecv=dma((2, steps)),
        fsend=dma((2, steps)),
        frecv=dma((2, steps)),
        vsem=dma((2, steps)),
        qsem=dma((2, 3)),
    )
    names = (*inputs, *outputs, *scratch)
    new_nodes, new_edges, node_gradient, edge_gradient, fin, vec, norm = pl.pallas_call(
        functools.partial(layer, names, d),
        out_shape=[shape for shape, _ in outputs.values()],
        in_specs=[spec for _, spec in inputs.values()],
        out_specs=[spec for _, spec in outputs.values()],
        scratch_shapes=list(scratch.values()),
        compiler_params=pltpu.CompilerParams(
            collective_id=0, has_side_effects=True, vmem_limit_bytes=60 * 1024 * 1024
        ),
    )(*[value for value, _ in inputs.values()])

    bias_grad = lax.dynamic_slice(vec, (6, lax.axis_index("tp") * Q), (2, Q))
    states = rest
    new_states = pl.pallas_call(
        functools.partial(update, L),
        out_shape=[jax.ShapeDtypeStruct(x.shape, F32) for x in states],
        in_specs=[vmem_spec] * (4 + len(states)),
        out_specs=[vmem_spec] * len(states),
        compiler_params=pltpu.CompilerParams(vmem_limit_bytes=48 * 1024 * 1024),
    )(fin, vec, bias_grad, norm, *states)
    return (new_nodes, new_edges, node_gradient, edge_gradient, norm[0, 0:1], *new_states)


def solution(mesh):
    split = [P(None, "tp"), P("tp", None), P(None, "tp"), P("tp", None), P(None, "tp"), P()]
    row = P("rows", None)
    return jax.shard_map(
        device_step,
        mesh=mesh,
        in_specs=(row, row, P("rows"), P("rows"), P("rows"), row, row, row, *split, *split, *split),
        out_specs=(row, row, row, row, P(), *split, *split, *split),
        check_vma=False,
    )
```

time: 316 us -> 136 us (0.43)
  Pallas kernels: 0 us -> 117 us
  blocking collectives: 79.8 us -> 0 us
  waiting for transfers between devices: 55.7 us -> 0 us
  local copies, waits for them, and re-layouts: 71.4 us -> 18.2 us
  matrix products: 39.6 us -> 0 us
  other arithmetic: 35 us -> 0 us
  between operations: 20.4 us -> 0.86 us
  starting transfers between devices: 13 us -> 0 us
    pallas_call x0 -> x2, Pallas kernels: none -> 117 us  [the longest x1 111 us: device_step(): pl.pallas_call(functools.partial(layer, names, d), out_shape=[shape for s...]
    psum x1 -> x0, waiting for transfers between devices: 49.7 us -> none  [local(): lax.psum((edge_in_grad, edge_out_grad, node_in_grad, node_out_grad, bias_...]
    psum x2 -> x0, blocking collectives: 47.5 us -> none  [the longest x1 39.1 us: local(): lax.psum((edge_in_grad, edge_out_grad, node_in_grad, node_out_grad, bias_...]
    dot_general x24 -> x0, matrix products: 39.6 us -> none  [the longest x9 11.6 us: dot_rows(): lax.dot_general(left, right, (((0,), (0,)), ((), ())), preferred_element_...]
    gather x5 -> x0, local copies, waits for them, and re-layouts: 35.7 us -> none  [the longest x2 14.4 us: local(): node_input_grad[:, latent:][edge_receiver]]
    all_gather x4 -> x0, blocking collectives: 32.3 us -> none  [the longest x1 10.9 us: local(): lax.all_gather(node_second, 'tp', axis=0, tiled=True)]
    unnamed x162 -> x52, local copies, waits for them, and re-layouts: 34.9 us -> 10.9 us
    reduce_sum x12 -> x0, other arithmetic: 21.4 us -> none  [the longest x1 7.43 us: local(): jnp.sum(edge_up * edge_normed, axis=0)]
  transfers between devices with their start and end apart: 7 -> 0, of which waited for: 3 -> 0; matrix products, arithmetic and copies ran while one was open for 27% -> 0% of each run, Pallas kernels for 0% -> 0%
where the time goes in v1:
time: 136 us
  Pallas kernels  117 us (86%)
  local copies, waits for them, and re-layouts  18.2 us (13%)
    pallas_call x1, Pallas kernels, device_step(): pl.pallas_call(functools.partial(layer, names, d), out_shape=[shape for s...  111 us
    unnamed x52, local copies, waits for them, and re-layouts  10.9 us
    pallas_call x1, Pallas kernels, device_step(): pl.pallas_call(functools.partial(update, L), out_shape=[jax.ShapeDtypeStr...  5.08 us

profile of v1, /device:TPU:0, one launch (start us, length us, event | category | flops | bytes accessed | tf_op | source)
XLA Modules:
  0.0 135.6 jit_solution(5203291980825323327)
XLA Ops:
  0.7 1.3 reshape.73.refs_16_
  2.0 1.3 pad.8.refs_8_
  3.3 1.3 pad.9.refs_9_
  4.6 1.5 %reshape.74.refs_15_ = s32[256,1]{1,0:T(8,128)} reshape(s32[8,32]{1,0:T(8,128)} %param.31) | data formatting | bytes 2048 | tf_op jit(solution)/shard_map/reshape | solution.py:648
  6.1 0.0 copy-start
  6.1 0.0 copy-start.1
  6.1 0.0 copy-start.2
  6.1 0.0 copy-start.3
  6.1 0.0 copy-start.4
  6.1 0.0 copy-start.5
  6.1 0.0 copy-start.6
  6.1 0.0 copy-start.12
  6.1 0.0 copy-start.14
  6.1 0.0 copy-start.15
  6.1 0.0 copy-start.17
  6.2 0.0 copy-start.18
  6.2 0.0 copy-start.19
  6.2 111.4 %shard_map.425 = (bf16[256,512]{1,0:T(8,128)(2,1)}, bf16[2048,512]{1,0:T(8,128)(2,1)}, bf16[256,512]{1,0:T(8,128)(2,1)}, bf16[2048,512]{1,0:T(8,128)(2,1)}, bf16...) custom-call(bf16[256,512]{1,0:T(8,128)(2,1)} %refs_0_.2, bf16[2048,512]{1,0:T(8,128)(2,1)} %refs_1_.2, ...), custom_call_target="tpu_custom_call" | custom-call | tf_op jit(solution)/shard_map/pallas_call | solution.py:734
  117.6 1.2 slice.3
  118.8 0.7 constant_dynamic-slice_fusion.bias_grad
  119.6 0.0 copy-done
  119.6 0.0 copy-done.1
  119.6 0.0 copy-done.2
  119.6 0.0 copy-done.3
  119.6 0.0 copy-done.4
  119.6 0.0 copy-done.5
  119.6 0.0 copy-done.6
  119.6 0.0 copy-done.12
  119.6 0.0 copy-done.14
  119.6 0.0 copy-done.15
  119.6 0.0 copy-done.17
  119.7 0.0 copy-done.18
  119.7 0.0 copy-done.19
  119.7 0.0 copy-start.7
  119.7 1.0 copy-done.7
  120.7 0.0 copy-start.8
  120.7 0.9 copy-done.8
  121.7 0.0 copy-start.9
  121.7 0.9 copy-done.9
  122.6 0.0 copy-start.10
  122.6 0.9 copy-done.10
  123.6 0.0 copy-start.11
  123.6 0.9 copy-done.11
  124.5 0.0 copy-start.13
  124.5 0.7 copy-done.13
  125.2 0.0 copy-start.16
  125.2 0.7 copy-done.16
  125.9 0.0 copy-start.23
  125.9 0.0 copy-start.21
  125.9 5.1 %shard_map.426 = (f32[1536,128]{1,0:T(8,128)}, f32[128,512]{1,0:T(8,128)}, f32[1024,128]{1,0:T(8,128)}, f32[128,512]{1,0:T(8,128)}, f32[2,128]{1,0:T(2,128)}, /*...) custom-call(bf16[3584,128]{1,0:T(8,128)(2,1)} %get-tuple-element.53., ...), custom_call_target="tpu_custom_call" | custom-call | tf_op jit(solution)/shard_map/pallas_call | solution.py:747
  131.0 0.0 copy-done.23
  131.0 0.7 copy.54
  131.7 0.0 copy-done.21
  131.7 0.0 copy-start.22
  131.7 0.0 copy-start.20
  131.7 1.3 copy.55
  133.1 0.0 copy-done.22
  133.1 0.7 copy.56
  133.8 0.5 copy-done.20
  134.3 1.3 copy.57
Async XLA Ops:
  6.1 113.5 %copy-start = (f32[1536,128]{1,0:T(8,128)S(1)}, f32[1536,128]{1,0:T(8,128)}, u32[]{:S(2)}) copy-start(f32[1536,128]{1,0:T(8,128)} %refs_0_.3) | copy-start | bytes 2359300
  6.1 113.5 %copy-start.1 = (f32[1024,128]{1,0:T(8,128)S(1)}, f32[1024,128]{1,0:T(8,128)}, u32[]{:S(2)}) copy-start(f32[1024,128]{1,0:T(8,128)} %refs_2_.3) | copy-start | bytes 1572868
  6.1 113.5 %copy-start.2 = (f32[128,512]{1,0:T(8,128)S(1)}, f32[128,512]{1,0:T(8,128)}, u32[]{:S(2)}) copy-start(f32[128,512]{1,0:T(8,128)} %refs_1_.3) | copy-start | bytes 786436
  6.1 113.5 %copy-start.3 = (f32[128,512]{1,0:T(8,128)S(1)}, f32[128,512]{1,0:T(8,128)}, u32[]{:S(2)}) copy-start(f32[128,512]{1,0:T(8,128)} %refs_3_.3) | copy-start | bytes 786436
  6.1 113.5 %copy-start.4 = (f32[1536,128]{1,0:T(8,128)S(1)}, f32[1536,128]{1,0:T(8,128)}, u32[]{:S(2)}) copy-start(f32[1536,128]{1,0:T(8,128)} %refs_6_.3) | copy-start | bytes 2359300
  6.1 113.5 %copy-start.5 = (f32[1536,128]{1,0:T(8,128)S(1)}, f32[1536,128]{1,0:T(8,128)}, u32[]{:S(2)}) copy-start(f32[1536,128]{1,0:T(8,128)} %refs_12_.1) | copy-start | bytes 2359300
  6.1 113.5 %copy-start.6 = (f32[1024,128]{1,0:T(8,128)S(1)}, f32[1024,128]{1,0:T(8,128)}, u32[]{:S(2)}) copy-start(f32[1024,128]{1,0:T(8,128)} %refs_8_.1) | copy-start | bytes 1572868
  6.1 113.5 %copy-start.12 = (f32[6,512]{1,0:T(8,128)S(1)}, f32[6,512]{1,0:T(8,128)}, u32[]{:S(2)}) copy-start(f32[6,512]{1,0:T(8,128)} %refs_5_.3) | copy-start | bytes 36868
  6.1 113.5 %copy-start.14 = (f32[6,512]{1,0:T(8,128)S(1)}, f32[6,512]{1,0:T(8,128)}, u32[]{:S(2)}) copy-start(f32[6,512]{1,0:T(8,128)} %refs_11_.1) | copy-start | bytes 36868
  6.1 113.5 %copy-start.15 = (f32[6,512]{1,0:T(8,128)S(1)}, f32[6,512]{1,0:T(8,128)}, u32[]{:S(2)}) copy-start(f32[6,512]{1,0:T(8,128)} %refs_17_.1) | copy-start | bytes 36868
  6.1 113.5 %copy-start.17 = (f32[2,128]{1,0:T(2,128)S(1)}, f32[2,128]{1,0:T(2,128)}, u32[]{:S(2)}) copy-start(f32[2,128]{1,0:T(2,128)} %refs_4_.3) | copy-start | bytes 3076
  6.2 113.5 %copy-start.18 = (f32[2,128]{1,0:T(2,128)S(1)}, f32[2,128]{1,0:T(2,128)}, u32[]{:S(2)}) copy-start(f32[2,128]{1,0:T(2,128)} %refs_10_.1) | copy-start | bytes 3076
  6.2 113.5 %copy-start.19 = (f32[2,128]{1,0:T(2,128)S(1)}, f32[2,128]{1,0:T(2,128)}, u32[]{:S(2)}) copy-start(f32[2,128]{1,0:T(2,128)} %refs_16_.1) | copy-start | bytes 3076
  119.7 1.0 copy-start.7
  120.7 0.9 copy-start.8
  121.7 0.9 copy-start.9
  122.6 0.9 copy-start.10
  123.6 0.9 copy-start.11
  124.5 0.7 copy-start.13
  125.2 0.7 copy-start.16
  125.9 5.1 %copy-start.23 = (bf16[256,512]{1,0:T(8,128)(2,1)S(1)}, bf16[256,512]{1,0:T(8,128)(2,1)}, u32[]{:S(2)}) copy-start(bf16[256,512]{1,0:T(8,128)(2,1)} %get-tuple-element.96) | copy-start | bytes 786436
  125.9 5.8 %copy-start.21 = (bf16[2048,512]{1,0:T(8,128)(2,1)S(1)}, bf16[2048,512]{1,0:T(8,128)(2,1)}, u32[]{:S(2)}) copy-start(bf16[2048,512]{1,0:T(8,128)(2,1)} %get-tuple-element.97) | copy-start | bytes 6291460
  131.7 1.3 copy-start.22
  131.7 2.5 %copy-start.20 = (bf16[2048,512]{1,0:T(8,128)(2,1)S(1)}, bf16[2048,512]{1,0:T(8,128)(2,1)}, u32[]{:S(2)}) copy-start(bf16[2048,512]{1,0:T(8,128)(2,1)} %get-tuple-element.99) | copy-start | bytes 6291460

commit v2 on v1

v2 whole, which is shorter than its diff:
```python
import functools
import math
import types

import jax
import jax.numpy as jnp
from jax import lax
from jax.experimental import pallas as pl
from jax.experimental.pallas import tpu as pltpu
from jax.sharding import PartitionSpec as P

BF = jnp.bfloat16
F32 = jnp.float32
MESH = pl.DeviceIdType.MESH
LANES = 128
TILE = 256

beta_one = 0.9
beta_two = 0.999
adam_step = 7.0
adam_eps = 1e-08
learn_rate = 0.05
vector_rate = 0.3
decay_rate = 0.1
clip_level = 1.0


def mm(left, right):
    return jnp.dot(left, right, preferred_element_type=F32)


def nt(left, right):
    return lax.dot_general(left, right, (((1,), (1,)), ((), ())), preferred_element_type=F32)


def tn(left, right):
    return lax.dot_general(left, right, (((0,), (0,)), ((), ())), preferred_element_type=F32)


def two(values):
    high = values.astype(BF)
    return high, (values - high.astype(F32)).astype(BF)


def aligned(start, step):
    return start if isinstance(start, int) else pl.multiple_of(start, step)


def rows_of(start, size, step=16):
    return pl.ds(aligned(start, step), size)


def hot(cond):
    return jnp.where(cond, 1.0, 0.0).astype(BF)


def normalize(values):
    center = values - jnp.mean(values, axis=1, keepdims=True)
    inverse = lax.rsqrt(jnp.mean(center * center, axis=1, keepdims=True) + 1e-05)
    return center * inverse, inverse


def norm_back(scaled, normed, inverse):
    first = jnp.mean(scaled, axis=1, keepdims=True)
    second = jnp.mean(scaled * normed, axis=1, keepdims=True)
    return inverse * (scaled - first - normed * second)


def row_sum(values):
    return jnp.sum(values, axis=0, keepdims=True)


def layer(names, d, *refs):
    s = types.SimpleNamespace(**dict(zip(names, refs, strict=True)))
    R, N, E, L, H, Q, CAP = d.R, d.N, d.E, d.L, d.H, d.Q, d.CAP
    EH, S, half, LH = E // 2, R * CAP, H // 2, L // 2
    tiles, slot_tiles, nb = EH // TILE, S // TILE, R // 4
    r = lax.axis_index("rows")
    t = lax.axis_index("tp")
    h, c = t // 2, lax.rem(t, 2)
    oh, oc = 1 - h, 1 - c
    pair = t + 1 - 2 * c
    far = t + 2 - 4 * h
    diag = pair + 2 - 4 * h
    a, b = lax.rem(r, 4), r // 4
    edge0 = c * EH
    own_lane = pl.ds(pl.multiple_of(t * Q, Q), Q)
    core_lane = pl.ds(pl.multiple_of(c * Q, Q), Q)
    col_lane = pl.ds(pl.multiple_of(c * LH, LH), LH)

    def local(src, dst, sem):
        return pltpu.make_async_copy(src, dst, sem)

    def remote(src, dst, send, recv, device):
        return pltpu.make_async_remote_copy(
            src_ref=src, dst_ref=dst, send_sem=send, recv_sem=recv, device_id=device, device_id_type=MESH
        )

    def loop(low, high, body):
        def step(k, carry):
            body(k)
            return carry

        lax.fori_loop(low, high, step, 0)

    loads = [
        local(s.wei_h, s.wei32, s.lsem.at[0]),
        local(s.nf_h, s.nf, s.lsem.at[1]),
        local(s.ef_h.at[rows_of(edge0, EH)], s.ef, s.lsem.at[2]),
        local(s.weo_h, s.weo32, s.lsem.at[3]),
        local(s.wni_h, s.wni32, s.lsem.at[4]),
        local(s.wno_h, s.wno32, s.lsem.at[5]),
        local(s.ncot_h, s.ncot, s.lsem.at[6]),
        local(s.ecot_h.at[rows_of(edge0, EH)], s.ecot, s.lsem.at[7]),
    ]
    for load in loads:
        load.start()

    barrier = pltpu.get_barrier_semaphore()
    for peer in (pair, far, diag):
        pl.semaphore_signal(barrier, inc=1, device_id=(r, peer), device_id_type=MESH)

    def greet(k):
        pl.semaphore_signal(barrier, inc=1, device_id=(lax.rem(r + k, R), t), device_id_type=MESH)

    loop(1, R, greet)

    def block(i, tt):
        lane = pl.ds(pl.multiple_of(tt * Q, Q), Q)
        if i < 3:
            half_lane = pl.ds(pl.multiple_of(lax.rem(tt, 2) * Q, Q), Q)
            return s.wei.at[tt // 2, pl.ds((0, 2 * L, L)[i], L), half_lane]
        if i == 3:
            return s.weo.at[lane, :]
        if i < 6:
            return s.wni.at[pl.ds((L, 0)[i - 4], L), lane]
        if i == 6:
            return s.wno.at[lane, :]
        return s.bias.at[:, lane]

    def weight_copy(i, way, who):
        ref = block(i, who)
        return remote(ref, ref, s.wsend.at[i, way], s.wrecv.at[i, way], (r, (pair, far, pair)[way]))

    def weight_send(i):
        weight_copy(i, 1, t).start()
        weight_copy(i, 0, t).start()

    def weight_wait(i, way):
        weight_copy(i, way, (pair, far, diag)[way]).wait_recv()

    def weight_forward(i):
        weight_wait(i, 1)
        weight_copy(i, 2, far).start()

    loads[0].wait()
    for i in range(3):
        at = pl.ds((0, 2 * L, L)[i], L)
        s.wei[h, at, core_lane] = s.wei32[at, :].astype(BF)
    s.bias[0:2, own_lane] = s.hb[...]
    s.bias[2:8, own_lane] = jnp.zeros((6, Q), F32)
    loads[1].wait()

    turned = jnp.transpose(s.serve[...].astype(F32))
    for k in range(R):
        s.serve_col[k * CAP : (k + 1) * CAP, :] = turned[:, k : k + 1]

    def serve(k):
        at = rows_of(k * TILE, TILE)
        table = s.serve_col[at, :].astype(jnp.int32) == lax.broadcasted_iota(jnp.int32, (TILE, N), 1)
        table = jnp.where(table, 1.0, 0.0)
        s.serve_t[:, pl.ds(pl.multiple_of(k * TILE, TILE), TILE)] = jnp.transpose(table).astype(BF)
        s.served[at, :] = mm(table.astype(BF), s.nf[:, col_lane]).astype(BF)

    loop(0, slot_tiles, serve)
    pl.semaphore_wait(barrier, R + 2)

    for i in range(3):
        weight_send(i)
    weight_send(7)
    mine = rows_of(r * CAP, CAP)

    def served_copy(k):
        to = lax.rem(r + k, R)
        return remote(
            s.served.at[rows_of(to * CAP, CAP)],
            s.slots.at[mine, col_lane],
            s.ssend.at[k],
            s.srecv.at[k],
            (to, t),
        )

    loop(1, R, lambda k: served_copy(k).start())
    s.slots[mine, col_lane] = s.served[mine, :]
    loads[3].wait()
    s.weo[own_lane, :] = s.weo32[...].astype(BF)
    weight_send(3)
    loads[4].wait()
    for i in (4, 5):
        at = pl.ds((L, 0)[i - 4], L)
        s.wni[at, own_lane] = s.wni32[at, :].astype(BF)
        weight_send(i)
    loads[5].wait()
    s.wno[own_lane, :] = s.wno32[...].astype(BF)
    weight_send(6)

    per = EH // LANES
    at = rows_of(c * per, per, 8)
    for source, target in ((s.rec2, s.rcol), (s.slot2, s.scol), (s.mask2, s.mcol)):
        turned = jnp.transpose(source[at, :].astype(F32))
        for k in range(per):
            target[k * LANES : (k + 1) * LANES, :] = turned[:, k : k + 1]
    lanes_here = pl.ds(pl.multiple_of(edge0, EH), EH)
    s.rhot_t[...] = hot(s.rec1[:, lanes_here] == lax.broadcasted_iota(jnp.int32, (N, EH), 0))

    def slot_table(k):
        rows = rows_of(k * TILE, TILE)
        s.shot_t[rows, :] = hot(
            s.slot1[:, lanes_here] == lax.broadcasted_iota(jnp.int32, (TILE, EH), 0) + k * TILE
        )

    loop(0, slot_tiles, slot_table)

    def receivers(k):
        rows = rows_of(k * TILE, TILE)
        index = s.rcol[rows, :].astype(jnp.int32)
        table = hot(index == lax.broadcasted_iota(jnp.int32, (TILE, N), 1))
        s.rhot[rows, :] = table
        s.xr[rows, :] = mm(table, s.nf[...]).astype(BF)

    loop(0, tiles, receivers)
    s.g[...] = jnp.zeros_like(s.g)
    loads[2].wait()

    def first_edges(which):
        def body(k):
            rows = rows_of(k * TILE, TILE)
            s.pre[which, rows, :] = mm(s.ef[rows, :], s.wei[which, 0:L, :])

        loop(0, tiles, body)

    def first_more(which, source, low):
        def body(k):
            rows = rows_of(k * TILE, TILE)
            s.pre[which, rows, :] += mm(source[rows, :], s.wei[which, low : low + L, :])

        loop(0, tiles, body)

    weight_wait(0, 0)
    first_edges(h)
    weight_wait(1, 0)
    first_more(h, s.xr, 2 * L)
    weight_forward(0)

    def served_wait(k):
        source = lax.rem(r + R - k, R)
        ref = s.slots.at[rows_of(source * CAP, CAP), col_lane]
        remote(ref, ref, s.ssend.at[k], s.srecv.at[k], (source, t)).wait_recv()

    loop(1, R, served_wait)
    slot_swap = remote(s.slots.at[:, col_lane], s.slots.at[:, col_lane], s.xsend.at[2], s.xrecv.at[2], (r, pair))
    slot_swap.start()
    weight_wait(0, 2)
    first_edges(oh)
    weight_forward(1)
    other_lane = pl.ds(pl.multiple_of(oc * LH, LH), LH)
    ref = s.slots.at[:, other_lane]
    remote(ref, ref, s.xsend.at[2], s.xrecv.at[2], (r, pair)).wait_recv()

    def senders(k):
        rows = rows_of(k * TILE, TILE)
        index = s.scol[rows, :].astype(jnp.int32)
        table = hot(index == lax.broadcasted_iota(jnp.int32, (TILE, S), 1))
        s.xs[rows, :] = mm(table, s.slots[...]).astype(BF)

    loop(0, tiles, senders)
    weight_wait(2, 0)
    first_more(h, s.xs, L)
    weight_wait(1, 2)
    first_more(oh, s.xr, 2 * L)
    weight_forward(2)
    weight_forward(7)
    weight_forward(3)
    weight_wait(2, 2)
    first_more(oh, s.xs, L)
    weight_wait(7, 0)
    weight_wait(7, 2)
    weight_wait(3, 0)
    weight_wait(3, 2)

    s.aggp[...] = jnp.zeros_like(s.aggp)

    def out_copies(k, source, target, which):
        here = source.at[rows_of(k * TILE, TILE)]
        there = target.at[rows_of(edge0 + k * TILE, TILE)]
        keep = local(here, there, s.osem.at[which, k])
        send = remote(here, there, s.osend.at[which, k], s.orecv.at[which, k], (r, pair))
        return keep, send

    def out_start(k, source, target, which):
        keep, send = out_copies(k, source, target, which)
        keep.start()
        send.start()

    def out_wait(k, source, target, which):
        keep, send = out_copies(k, source, target, which)
        keep.wait()
        send.wait_send()
        ref = target.at[rows_of(oc * EH + k * TILE, TILE)]
        remote(ref, ref, s.osend.at[which, k], s.orecv.at[which, k], (r, pair)).wait_recv()

    def forward(k):
        rows = rows_of(k * TILE, TILE)
        hidden = []
        for p in (0, 1):
            pre = s.pre[p, rows, :] + s.bias[0:1, p * half : (p + 1) * half]
            sig = 1.0 / (1.0 + jnp.exp(-pre))
            value = (pre * sig).astype(BF)
            s.hid[p, rows, :] = value
            s.pre[p, rows, :] = sig * (1.0 + pre * (1.0 - sig))
            hidden.append(value)
        outer = mm(hidden[0], s.weo[0:half, :]) + mm(hidden[1], s.weo[half:H, :]) + s.fv[0:1, :]
        normed, inverse = normalize(outer)
        s.normed[rows, :] = normed
        s.inv[rows, :] = inverse
        masked = s.mcol[rows, :] * (normed * s.fv[1:2, :] + s.fv[2:3, :])
        s.ne[rows, :] = (s.ef[rows, :].astype(F32) + masked).astype(BF)
        out_start(k, s.ne, s.ne_h, 0)
        high, low = two(masked)
        table = s.rhot_t[:, pl.ds(pl.multiple_of(k * TILE, TILE), TILE)]
        s.aggp[...] += mm(table, high) + mm(table, low)

    loop(0, tiles, forward)
    swap = remote(s.aggp, s.aggr, s.xsend.at[0], s.xrecv.at[0], (r, pair))
    swap.start()
    weight_wait(5, 0)
    weight_forward(4)
    weight_forward(5)
    weight_wait(5, 2)
    own_term = mm(s.nf[...], s.wni[0:L, :])
    weight_wait(4, 0)
    weight_wait(4, 2)
    swap.wait()

    agg = (s.aggp[...] + s.aggr[...]).astype(BF)
    pre = own_term + mm(agg, s.wni[L : 2 * L, :]) + s.bias[1:2, :]
    sig = 1.0 / (1.0 + jnp.exp(-pre))
    node_hidden = (pre * sig).astype(BF)
    slope_of = sig * (1.0 + pre * (1.0 - sig))
    weight_forward(6)
    weight_wait(6, 0)
    weight_wait(6, 2)
    outer = mm(node_hidden, s.wno[...]) + s.fv[3:4, :]
    normed, inverse = normalize(outer)
    s.nn[...] = (s.nf[...].astype(F32) + (normed * s.fv[4:5, :] + s.fv[5:6, :])).astype(BF)
    nn_copy = local(s.nn, s.nn_h, s.nsem.at[0])
    nn_copy.start()
    loads[6].wait()
    up = s.ncot[...].astype(F32)
    node_outer_grad = norm_back(up * s.fv[4:5, :], normed, inverse).astype(BF)
    node_slope = (nt(node_outer_grad, s.wno[...]) * slope_of).astype(BF)
    agg_high, agg_low = two(nt(node_slope, s.wni[L : 2 * L, :]))
    s.agh[...] = agg_high
    s.agl[...] = agg_low

    for q in range(H // Q):
        s.nsl[q] = node_slope[:, q * Q : (q + 1) * Q]
        s.nhid[q] = node_hidden[:, q * Q : (q + 1) * Q]
    s.vsum[...] = jnp.zeros_like(s.vsum)
    s.vsum[3:4, :] = 0.5 * row_sum(node_outer_grad.astype(F32))
    s.vsum[4:5, :] = 0.5 * row_sum(up * normed)
    s.vsum[5:6, :] = 0.5 * row_sum(up)
    base_node, base_out, base_in, base_vec = d.base_node, d.base_out, d.base_in, d.base_in + 3 * L
    s.g[c, 0:L, :] = tn(s.nf[...], s.nsl[t])
    s.g[c, L : 2 * L, :] = tn(agg, s.nsl[t])
    node_out_grad = tn(s.nhid[t], node_outer_grad)
    for q in range(L // LANES):
        s.g[c, 2 * L + q * Q : 2 * L + (q + 1) * Q, :] = node_out_grad[:, q * LANES : (q + 1) * LANES]

    chunks = ((base_node, d.size_node), (base_out, d.size_out), (base_in, d.size_in))

    def piece(n, q, bb):
        base, size = chunks[n]
        count = size // R
        return rows_of(base + (q * nb + bb) * count, count)

    def pair_copy(n):
        at = pl.ds(*chunks[n])
        return remote(s.sb.at[at], s.rbp.at[at], s.psend.at[n], s.precv.at[n], (r, pair))

    def pair_start(n):
        at = pl.ds(*chunks[n])
        s.sb[at, :] = s.g[oc, at, :].astype(BF)
        pair_copy(n).start()

    def pair_finish(n):
        pair_copy(n).wait()
        at = pl.ds(*chunks[n])
        if n == 2:
            vec = pl.ds(base_vec, 32)
            s.g[c, vec, :] = s.g[c, vec, :].astype(BF).astype(F32)
        s.g[c, at, :] += s.rbp[at, :].astype(F32)

    def a_row(j):
        return b * 4 + lax.rem(a + j, 4)

    def b_row(j):
        return lax.rem(b + j, nb) * 4 + a

    def a_copy(n, jj, j, q):
        at = piece(n, q, lax.rem(b + jj, nb))
        return remote(s.sb.at[at], s.rba.at[j - 1, at], s.asend.at[n, jj, j], s.arecv.at[n, jj, j], (a_row(j), t))

    def b_slot(n):
        base, size = chunks[n]
        return pl.ds(base // R, size // R)

    def b_copy(n, jj, bb):
        return remote(
            s.sb.at[piece(n, a, bb)],
            s.rbb.at[jj - 1, b_slot(n)],
            s.bsend.at[n, jj],
            s.brecv.at[n, jj],
            (b_row(jj), t),
        )

    order = (*range(1, nb), 0)

    def a_send(n):
        at = pl.ds(*chunks[n])
        s.sb[at, :] = s.g[c, at, :].astype(BF)
        for jj in order:
            for j in (1, 2, 3):
                a_copy(n, jj, j, lax.rem(a + j, 4)).start()

    def a_sum(n, jj):
        at = piece(n, a, lax.rem(b + jj, nb))
        for j in (1, 2, 3):
            a_copy(n, jj, j, a).wait_recv()
        return s.g[c, at, :] + (
            s.rba[0, at, :].astype(F32) + s.rba[1, at, :].astype(F32) + s.rba[2, at, :].astype(F32)
        )

    def b_send(n):
        for jj in range(1, nb):
            at = piece(n, a, lax.rem(b + jj, nb))
            s.sb[at, :] = a_sum(n, jj).astype(BF)
            b_copy(n, jj, lax.rem(b + jj, nb)).start()

    def to_b(n, jj):
        ref = s.fin.at[piece(n, a, b)]
        return remote(ref, ref, s.fbsend.at[n, jj], s.fbrecv.at[n, jj], (b_row(jj), t))

    def to_a(n, jj, j):
        ref = s.fin.at[piece(n, a, lax.rem(b + nb - jj, nb))]
        return remote(ref, ref, s.fasend.at[n, jj, j], s.farecv.at[n, jj, j], (a_row(j), t))

    def b_finish(n):
        total = a_sum(n, 0)
        at = piece(n, a, b)
        for jj in range(1, nb):
            b_copy(n, jj, b).wait_recv()
            total = total + s.rbb[jj - 1, b_slot(n), :].astype(F32)
        final = total.astype(BF)
        s.fin[at, :] = final
        for jj in range(1, nb):
            to_b(n, jj).start()
        for j in (1, 2, 3):
            to_a(n, 0, j).start()
        final = final.astype(F32)
        squares = final * final
        count = squares.shape[0]
        if n == 2:
            index = lax.broadcasted_iota(jnp.int32, (count, LANES), 0) + (base_in + (a * nb + b) * count)
            copied = jnp.logical_and(index >= base_vec, index < base_vec + 24)
            squares = jnp.where(copied, 0.25 * squares, squares)
        s.norm_a[mine8, :] += jnp.sum(squares.reshape(count // 8, 8, LANES), axis=0)

    def spread(n):
        for jj in range(1, nb):
            ref = s.fin.at[piece(n, a, lax.rem(b + nb - jj, nb))]
            remote(ref, ref, s.fbsend.at[n, jj], s.fbrecv.at[n, jj], (b_row(jj), t)).wait_recv()
            for j in (1, 2, 3):
                to_a(n, jj, j).start()

    def spread_wait(n):
        for jj in range(nb):
            for j in (1, 2, 3):
                ref = s.fin.at[piece(n, lax.rem(a + 4 - j, 4), lax.rem(b + nb - jj, nb))]
                remote(ref, ref, s.fasend.at[n, jj, j], s.farecv.at[n, jj, j], (a_row(j), t)).wait_recv()

    def sums_done(n):
        for jj in range(nb):
            for j in (1, 2, 3):
                a_copy(n, jj, j, lax.rem(a + j, 4)).wait_send()
                to_a(n, jj, j).wait_send()
        for jj in range(1, nb):
            b_copy(n, jj, lax.rem(b + jj, nb)).wait_send()
            to_b(n, jj).wait_send()

    mine8 = rows_of(r * 8, 8, 8)
    s.norm_a[mine8, :] = jnp.zeros((8, LANES), F32)
    a_send(0)

    loads[7].wait()

    def backward_norm(k):
        rows = rows_of(k * TILE, TILE)
        table = s.rhot[rows, :]
        cot = s.ecot[rows, :].astype(F32)
        up = s.mcol[rows, :] * (cot + (mm(table, s.agh[...]) + mm(table, s.agl[...])))
        normed = s.normed[rows, :]
        grad = norm_back(up * s.fv[1:2, :], normed, s.inv[rows, :]).astype(BF)
        s.og[rows, :] = grad
        s.vsum[0:1, :] += row_sum(grad.astype(F32))
        s.vsum[1:2, :] += row_sum(up * normed)
        s.vsum[2:3, :] += row_sum(up)

    loop(0, tiles, backward_norm)
    out_part = tn(s.hid[h], s.og[...])
    for p in (0, 1):
        for q in range(L // LANES):
            at = base_out + q * Q
            s.g[p, at : at + Q, :] = out_part[p * Q : (p + 1) * Q, q * LANES : (q + 1) * LANES]
    pair_start(1)

    def slope_half(which, k):
        rows = rows_of(k * TILE, TILE)
        w_rows = rows_of(which * half, half)
        value = (nt(s.og[rows, :], s.weo[w_rows, :]) * s.pre[which, rows, :]).astype(BF)
        s.sl[which, rows, :] = value
        lanes = pl.ds(pl.multiple_of(k * TILE, TILE), TILE)
        s.rs[which] += mm(s.rhot_t[:, lanes], value)

        def slots(j):
            at = rows_of(j * TILE, TILE)
            s.ss[which, at, :] += mm(s.shot_t[at, lanes], value)

        loop(0, slot_tiles, slots)
        return value

    s.rs[...] = jnp.zeros_like(s.rs)
    s.ss[...] = jnp.zeros_like(s.ss)

    def backward_own(k):
        value = slope_half(h, k)
        s.vsum[6:7, 0:half] += row_sum(value.astype(F32))

    loop(0, tiles, backward_own)

    edge_part = tn(s.ef[...], s.sl[h])
    recv_part = tn(s.nf[...], s.rs[h].astype(BF))
    for p in (0, 1):
        cols = slice(p * Q, (p + 1) * Q)
        s.g[p, base_in : base_in + L, :] = edge_part[:, cols]
        s.g[p, base_in + 2 * L : base_in + 3 * L, :] = recv_part[:, cols]
        for j in range(6):
            for q in range(L // LANES):
                at = base_vec + j * (L // LANES) + q
                s.g[p, at : at + 1, :] = s.vsum[j : j + 1, q * LANES : (q + 1) * LANES]
        s.g[p, base_vec + 24 : base_vec + 25, :] = s.vsum[6:7, cols]
        s.g[p, base_vec + 25 : base_vec + 26, :] = 0.5 * row_sum(s.nsl[2 * h + p].astype(F32))

    def sender_part(k):
        at = rows_of(k * TILE, TILE)
        value = tn(s.slots[at, :], s.ss[h, at, :].astype(BF))
        for p in (0, 1):
            s.g[p, base_in + L : base_in + 2 * L, :] += value[:, p * Q : (p + 1) * Q]

    loop(0, slot_tiles, sender_part)
    pair_start(2)
    pair_finish(1)
    a_send(1)
    pair_finish(2)
    a_send(2)
    b_send(0)

    def backward_other(k):
        rows = rows_of(k * TILE, TILE)
        value = slope_half(oh, k)
        cot = s.ecot[rows, :].astype(F32)
        back = nt(s.sl[0, rows, :], s.wei[0, 0:L, :]) + nt(s.sl[1, rows, :], s.wei[1, 0:L, :])
        s.eg[rows, :] = (cot + back).astype(BF)
        out_start(k, s.eg, s.eg_h, 1)

    loop(0, tiles, backward_other)
    b_finish(0)
    b_send(1)
    b_send(2)

    def slot_grad(which, rows):
        at = rows_of(L + which * LH, LH)
        return nt(s.ss[0, rows, :].astype(BF), s.wei[0, at, :]) + nt(s.ss[1, rows, :].astype(BF), s.wei[1, at, :])

    def recv_grad(which):
        at = rows_of(2 * L + which * LH, LH)
        return nt(s.rs[0].astype(BF), s.wei[0, at, :]) + nt(s.rs[1].astype(BF), s.wei[1, at, :])

    def slot_other(k):
        rows = rows_of(k * TILE, TILE)
        s.tosend[rows, :] = slot_grad(oc, rows).astype(BF)

    loop(0, slot_tiles, slot_other)
    s.tosend[S : S + N, :] = recv_grad(oc).astype(BF)
    grad_swap = remote(s.tosend, s.torecv, s.xsend.at[1], s.xrecv.at[1], (r, pair))
    grad_swap.start()
    s.ntp[...] = (
        s.ncot[:, col_lane].astype(F32)
        + (nt(s.nsl[0], s.wni[rows_of(c * LH, LH), 0:Q]) + nt(s.nsl[1], s.wni[rows_of(c * LH, LH), Q : 2 * Q]))
        + (
            nt(s.nsl[2], s.wni[rows_of(c * LH, LH), 2 * Q : 3 * Q])
            + nt(s.nsl[3], s.wni[rows_of(c * LH, LH), 3 * Q : 4 * Q])
        )
        + recv_grad(c)
    )
    b_finish(1)
    grad_swap.wait_recv()

    def slot_own(k):
        rows = rows_of(k * TILE, TILE)
        s.served[rows, :] = (slot_grad(c, rows) + s.torecv[rows, :].astype(F32)).astype(BF)

    loop(1, R, lambda k: served_copy(k).wait_send())
    loop(0, slot_tiles, slot_own)

    def back_copy(k):
        to = lax.rem(r + k, R)
        return remote(s.served.at[rows_of(to * CAP, CAP)], s.ret.at[mine], s.ksend.at[k], s.krecv.at[k], (to, t))

    b_finish(2)

    def norm_row(k):
        to = lax.rem(r + k, R)
        ref = s.norm_a.at[mine8]
        return remote(ref, ref, s.qsend.at[k], s.qrecv.at[k], (to, t))

    loop(1, R, lambda k: norm_row(k).start())
    loop(1, R, lambda k: back_copy(k).start())
    s.ret[mine, :] = s.served[mine, :]
    s.ntp[...] += s.torecv[S : S + N, :].astype(F32)
    for n in (0, 1, 2):
        spread(n)

    def norm_row_wait(k):
        source = lax.rem(r + R - k, R)
        ref = s.norm_a.at[rows_of(source * 8, 8, 8)]
        remote(ref, ref, s.qsend.at[k], s.qrecv.at[k], (source, t)).wait_recv()
        norm_row(k).wait_send()

    loop(1, R, norm_row_wait)
    own_rows = rows_of(t * 8, 8, 8)
    s.nsq[own_rows, :] = jnp.sum(s.norm_a[...].reshape(R, 8, LANES), axis=0)
    for k, peer in enumerate((pair, far, diag)):
        ref = s.nsq.at[own_rows]
        remote(ref, ref, s.tsem.at[0, k], s.tsem.at[1, k], (r, peer)).start()

    def back_wait(k):
        source = lax.rem(r + R - k, R)
        ref = s.ret.at[rows_of(source * CAP, CAP)]
        remote(ref, ref, s.ksend.at[k], s.krecv.at[k], (source, t)).wait_recv()
        back_copy(k).wait_send()

    loop(1, R, back_wait)

    def gathered(k):
        lanes = pl.ds(pl.multiple_of(k * TILE, TILE), TILE)
        s.ntp[...] += mm(s.serve_t[:, lanes], s.ret[rows_of(k * TILE, TILE), :])

    loop(0, slot_tiles, gathered)
    s.ng[...] = s.ntp[...].astype(BF)
    ng_keep = local(s.ng, s.ng_h.at[:, col_lane], s.nsem.at[1])
    ng_keep.start()
    ng_send = remote(s.ng, s.ng_h.at[:, col_lane], s.xsend.at[3], s.xrecv.at[3], (r, pair))
    ng_send.start()

    for n in (0, 1, 2):
        spread_wait(n)
    s.fin_o[...] = s.fin[...]
    for k, peer in enumerate((pair, far, diag)):
        ref = s.nsq.at[rows_of(peer * 8, 8, 8)]
        remote(ref, ref, s.tsem.at[0, k], s.tsem.at[1, k], (r, peer)).wait()
    total = s.nsq[0:8, :] + s.nsq[8:16, :] + s.nsq[16:24, :] + s.nsq[24:32, :]
    s.norm_o[...] = jnp.sqrt(jnp.full((8, LANES), jnp.sum(total), F32))
    for n in (0, 1, 2):
        sums_done(n)
    for i in range(8):
        weight_copy(i, 0, t).wait_send()
        weight_copy(i, 1, t).wait_send()
        weight_copy(i, 2, far).wait_send()
    slot_swap.wait_send()
    grad_swap.wait_send()

    def finish(k):
        out_wait(k, s.ne, s.ne_h, 0)
        out_wait(k, s.eg, s.eg_h, 1)

    loop(0, tiles, finish)
    nn_copy.wait()
    ng_keep.wait()
    ng_send.wait_send()
    ref = s.ng_h.at[:, other_lane]
    remote(ref, ref, s.xsend.at[3], s.xrecv.at[3], (r, pair)).wait_recv()


def adam(weight, first, second, gradient, factor, rate):
    clipped = gradient * factor
    first_new = beta_one * first + (1.0 - beta_one) * clipped
    second_new = beta_two * second + (1.0 - beta_two) * clipped * clipped
    bias_one = 1.0 - beta_one**adam_step
    bias_two = 1.0 - beta_two**adam_step
    moved = first_new / bias_one / (jnp.sqrt(second_new / bias_two) + adam_eps) + decay_rate * weight
    return weight - rate * moved, first_new, second_new


def update(names, d, *refs):
    s = types.SimpleNamespace(**dict(zip(names, refs, strict=True)))
    L, Q = d.L, d.Q
    passes = [
        pltpu.make_async_copy(s.__dict__[f"pass{k}"], s.__dict__[f"out{k}"], s.psem.at[k]) for k in range(4)
    ]
    for copy in passes:
        copy.start()
    norm = s.norm[0:1, 0:1]
    s.norm_o[0] = s.norm[0, 0]
    factor = clip_level / jnp.maximum(norm, clip_level)
    copies = []

    def one(k, grad, at, rate):
        values = adam(
            s.__dict__[f"in{k}"][at], s.__dict__[f"in{6 + k}"][at], s.__dict__[f"in{12 + k}"][at], grad, factor, rate
        )
        for n, value in enumerate(values):
            s.__dict__[f"buf{6 * n + k}"][at] = value

    def send(k):
        for n in range(3):
            m = 6 * n + k
            copy = pltpu.make_async_copy(s.__dict__[f"buf{m}"], s.__dict__[f"new{m}"], s.osem.at[m])
            copy.start()
            copies.append(copy)

    everything = (slice(None), slice(None))
    for k, base in ((2, d.base_node), (0, d.base_in)):
        for low in range(0, (2 if k == 2 else 3) * L, 256):
            rows = slice(low, low + 256)
            one(k, s.fin[base + low : base + low + 256, :].astype(F32), (rows, slice(None)), learn_rate)
        send(k)
    for k, base in ((3, d.base_node + 2 * L), (1, d.base_out)):
        for q in range(L // LANES):
            at = (slice(None), slice(q * LANES, (q + 1) * LANES))
            one(k, s.fin[base + q * LANES : base + (q + 1) * LANES, :].astype(F32), at, learn_rate)
        send(k)
    vec = s.fin[d.base_in + 3 * L : d.base_in + 3 * L + 32, :].astype(F32)
    one(4, vec[24:26, :], everything, vector_rate)
    send(4)
    for j in range(6):
        for q in range(L // LANES):
            m = j * (L // LANES) + q
            at = (slice(j, j + 1), slice(q * LANES, (q + 1) * LANES))
            one(5, vec[m : m + 1, :], at, vector_rate)
    send(5)
    for copy in copies + passes:
        copy.wait()


def device_step(
    node_feats,
    edge_feats,
    edge_receiver,
    edge_slot,
    edge_mask,
    serve_rows,
    node_cot,
    edge_cot,
    *states,
):
    weights = states[:6]
    d = types.SimpleNamespace()
    d.R = lax.axis_size("rows")
    d.N, d.L = node_feats.shape
    d.E = edge_feats.shape[0]
    d.Q = weights[0].shape[1]
    d.H = d.Q * lax.axis_size("tp")
    d.CAP = serve_rows.shape[1]
    R, N, E, L, H, Q = d.R, d.N, d.E, d.L, d.H, d.Q
    EH, S, nb = E // 2, R * d.CAP, R // 4
    tiles = EH // TILE

    def padded(count):
        return -(-count // (16 * R)) * (16 * R)

    d.size_node, d.size_out, d.size_in = padded(3 * L), padded(L), padded(3 * L + 32)
    d.base_node, d.base_out, d.base_in = 0, d.size_node, d.size_node + d.size_out
    G = d.size_node + d.size_out + d.size_in
    any_spec = pl.BlockSpec(memory_space=pl.ANY)
    vmem_spec = pl.BlockSpec(memory_space=pltpu.VMEM)
    inputs = dict(
        nf_h=(node_feats, any_spec),
        ef_h=(edge_feats, any_spec),
        ncot_h=(node_cot, any_spec),
        ecot_h=(edge_cot, any_spec),
        wei_h=(weights[0], any_spec),
        weo_h=(weights[1], any_spec),
        wni_h=(weights[2], any_spec),
        wno_h=(weights[3], any_spec),
        hb=(weights[4], vmem_spec),
        fv=(weights[5], vmem_spec),
        rec2=(edge_receiver.reshape(-1, LANES), vmem_spec),
        slot2=(edge_slot.reshape(-1, LANES), vmem_spec),
        mask2=(edge_mask.reshape(-1, LANES), vmem_spec),
        rec1=(edge_receiver.reshape(1, -1), vmem_spec),
        slot1=(edge_slot.reshape(1, -1), vmem_spec),
        serve=(serve_rows, vmem_spec),
    )
    outputs = dict(
        nn_h=(jax.ShapeDtypeStruct((N, L), BF), any_spec),
        ne_h=(jax.ShapeDtypeStruct((E, L), BF), any_spec),
        ng_h=(jax.ShapeDtypeStruct((N, L), BF), any_spec),
        eg_h=(jax.ShapeDtypeStruct((E, L), BF), any_spec),
        fin_o=(jax.ShapeDtypeStruct((G, Q), BF), vmem_spec),
        norm_o=(jax.ShapeDtypeStruct((8, LANES), F32), vmem_spec),
    )
    dma = pltpu.SemaphoreType.DMA
    scratch = dict(
        wei32=pltpu.VMEM((3 * L, Q), F32),
        weo32=pltpu.VMEM((Q, L), F32),
        wni32=pltpu.VMEM((2 * L, Q), F32),
        wno32=pltpu.VMEM((Q, L), F32),
        nf=pltpu.VMEM((N, L), BF),
        ef=pltpu.VMEM((EH, L), BF),
        ncot=pltpu.VMEM((N, L), BF),
        ecot=pltpu.VMEM((EH, L), BF),
        wei=pltpu.VMEM((2, 3 * L, H // 2), BF),
        weo=pltpu.VMEM((H, L), BF),
        wni=pltpu.VMEM((2 * L, H), BF),
        wno=pltpu.VMEM((H, L), BF),
        bias=pltpu.VMEM((8, H), F32),
        serve_col=pltpu.VMEM((S, 1), F32),
        serve_t=pltpu.VMEM((N, S), BF),
        served=pltpu.VMEM((S, L // 2), BF),
        slots=pltpu.VMEM((S, L), BF),
        ret=pltpu.VMEM((S, L // 2), BF),
        rcol=pltpu.VMEM((EH, 1), F32),
        scol=pltpu.VMEM((EH, 1), F32),
        mcol=pltpu.VMEM((EH, 1), F32),
        rhot=pltpu.VMEM((EH, N), BF),
        rhot_t=pltpu.VMEM((N, EH), BF),
        shot_t=pltpu.VMEM((S, EH), BF),
        xr=pltpu.VMEM((EH, L), BF),
        xs=pltpu.VMEM((EH, L), BF),
        pre=pltpu.VMEM((2, EH, H // 2), F32),
        hid=pltpu.VMEM((2, EH, H // 2), BF),
        normed=pltpu.VMEM((EH, L), F32),
        inv=pltpu.VMEM((EH, 1), F32),
        ne=pltpu.VMEM((EH, L), BF),
        eg=pltpu.VMEM((EH, L), BF),
        aggp=pltpu.VMEM((N, L), F32),
        aggr=pltpu.VMEM((N, L), F32),
        nn=pltpu.VMEM((N, L), BF),
        ng=pltpu.VMEM((N, L // 2), BF),
        agh=pltpu.VMEM((N, L), BF),
        agl=pltpu.VMEM((N, L), BF),
        ntp=pltpu.VMEM((N, L // 2), F32),
        nsl=pltpu.VMEM((H // Q, N, Q), BF),
        nhid=pltpu.VMEM((H // Q, N, Q), BF),
        og=pltpu.VMEM((EH, L), BF),
        sl=pltpu.VMEM((2, EH, H // 2), BF),
        rs=pltpu.VMEM((2, N, H // 2), F32),
        ss=pltpu.VMEM((2, S, H // 2), F32),
        tosend=pltpu.VMEM((S + N, L // 2), BF),
        torecv=pltpu.VMEM((S + N, L // 2), BF),
        g=pltpu.VMEM((2, G, Q), F32),
        sb=pltpu.VMEM((G, Q), BF),
        rbp=pltpu.VMEM((G, Q), BF),
        rba=pltpu.VMEM((3, G, Q), BF),
        rbb=pltpu.VMEM((nb - 1, G // R, Q), BF),
        fin=pltpu.VMEM((G, Q), BF),
        vsum=pltpu.VMEM((8, L), F32),
        norm_a=pltpu.VMEM((8 * R, LANES), F32),
        nsq=pltpu.VMEM((32, LANES), F32),
        lsem=dma((8,)),
        wsend=dma((8, 3)),
        wrecv=dma((8, 3)),
        ssend=dma((R,)),
        srecv=dma((R,)),
        ksend=dma((R,)),
        krecv=dma((R,)),
        qsend=dma((R,)),
        qrecv=dma((R,)),
        osem=dma((2, tiles)),
        osend=dma((2, tiles)),
        orecv=dma((2, tiles)),
        xsend=dma((4,)),
        xrecv=dma((4,)),
        nsem=dma((2,)),
        psend=dma((3,)),
        precv=dma((3,)),
        asend=dma((3, nb, 4)),
        arecv=dma((3, nb, 4)),
        bsend=dma((3, nb)),
        brecv=dma((3, nb)),
        fbsend=dma((3, nb)),
        fbrecv=dma((3, nb)),
        fasend=dma((3, nb, 4)),
        farecv=dma((3, nb, 4)),
        tsem=dma((2, 3)),
    )
    names = (*inputs, *outputs, *scratch)
    limit = 6 * 1024 * 1024
    for x in scratch.values():
        if x.memory_space == pltpu.VMEM:
            *lead, rows, lanes = x.shape
            limit += math.prod(lead) * rows * -(-lanes // LANES) * LANES * jnp.dtype(x.dtype).itemsize
    new_nodes, new_edges, node_gradient, edge_gradient, fin, norm = pl.pallas_call(
        functools.partial(layer, names, d),
        out_shape=[shape for shape, _ in outputs.values()],
        in_specs=[spec for _, spec in inputs.values()],
        out_specs=[spec for _, spec in outputs.values()],
        scratch_shapes=list(scratch.values()),
        compiler_params=pltpu.CompilerParams(
            collective_id=0, has_side_effects=True, vmem_limit_bytes=limit
        ),
    )(*[value for value, _ in inputs.values()])

    passes = (new_nodes, new_edges, node_gradient, edge_gradient)
    names = (
        "fin",
        "norm",
        *(f"pass{k}" for k in range(4)),
        *(f"in{k}" for k in range(18)),
        *(f"out{k}" for k in range(4)),
        "norm_o",
        *(f"new{k}" for k in range(18)),
        *(f"buf{k}" for k in range(18)),
        "psem",
        "osem",
    )
    outs = pl.pallas_call(
        functools.partial(update, names, d),
        out_shape=[
            *(jax.ShapeDtypeStruct(x.shape, x.dtype) for x in passes),
            jax.ShapeDtypeStruct((1,), F32),
            *(jax.ShapeDtypeStruct(x.shape, F32) for x in states),
        ],
        in_specs=[vmem_spec, vmem_spec, *[any_spec] * 4, *[vmem_spec] * 18],
        out_specs=[*[any_spec] * 4, pl.BlockSpec(memory_space=pltpu.SMEM), *[any_spec] * 18],
        scratch_shapes=[*(pltpu.VMEM(x.shape, F32) for x in states), dma((4,)), dma((18,))],
        compiler_params=pltpu.CompilerParams(vmem_limit_bytes=32 * 1024 * 1024),
    )(fin, norm, *passes, *states)
    return tuple(outs)


def solution(mesh):
    split = [P(None, "tp"), P("tp", None), P(None, "tp"), P("tp", None), P(None, "tp"), P()]
    row = P("rows", None)
    return jax.shard_map(
        device_step,
        mesh=mesh,
        in_specs=(row, row, P("rows"), P("rows"), P("rows"), row, row, row, *split, *split, *split),
        out_specs=(row, row, row, row, P(), *split, *split, *split),
        check_vma=False,
    )
```

time: 136 us -> 86.1 us (0.63)
  Pallas kernels: 117 us -> 72.7 us
  local copies, waits for them, and re-layouts: 18.2 us -> 11.8 us
    pallas_call x1, Pallas kernels: 111 us -> 67.3 us  [device_step(): pl.pallas_call(functools.partial(layer, names, d), out_shape=[shape for s...]
    reshape x2 -> x0, local copies, waits for them, and re-layouts: 2.8 us -> none  [the longest x1 1.47 us: device_step(): serve_rows.reshape(-1, 1)]
    pad x2 -> x0, local copies, waits for them, and re-layouts: 2.6 us -> none  [the longest x1 1.33 us: device_step(): jnp.pad(weights[5], ((0, 2), (0, 0)))]
    unnamed x52 -> x50, local copies, waits for them, and re-layouts: 10.9 us -> 11.8 us
where the time goes in v2:
time: 86.1 us; the launch traced here: 85.5 us
  Pallas kernels  72.7 us (84%)
  local copies, waits for them, and re-layouts  11.8 us (14%)
  between operations  1.02 us (1%)
    pallas_call x1, Pallas kernels, device_step(): pl.pallas_call(functools.partial(layer, names, d), out_shape=[shape for s...  67.3 us
    unnamed x50, local copies, waits for them, and re-layouts  11.8 us
    pallas_call x1, Pallas kernels, device_step(): pl.pallas_call(functools.partial(update, names, d), out_shape=[*(jax.Shap...  5.37 us

profile of v2, /device:TPU:0, one launch (start us, length us, event | category | flops | bytes accessed | tf_op | source)
XLA Modules:
  0.0 85.5 jit_solution(6542328981755330885)
XLA Ops:
  0.7 0.0 copy-start
  0.7 1.1 %copy-done = f32[1536,128]{1,0:T(8,128)S(1)} copy-done((f32[1536,128]{1,0:T(8,128)S(1)}, f32[1536,128]{1,0:T(8,128)}, u32[]{:S(2)}) %copy-start) | copy-done | bytes 786456
  1.8 0.0 copy-start.1
  1.8 1.0 %copy-done.1 = f32[1024,128]{1,0:T(8,128)S(1)} copy-done((f32[1024,128]{1,0:T(8,128)S(1)}, f32[1024,128]{1,0:T(8,128)}, u32[]{:S(2)}) %copy-start.1) | copy-done | bytes 524312
  2.8 0.0 copy-start.2
  2.8 1.6 %copy-done.2 = bf16[2048,512]{1,0:T(8,128)(2,1)S(1)} copy-done((bf16[2048,512]{1,0:T(8,128)(2,1)S(1)}, bf16[2048,512]{1,0:T(8,128)(2,1)}, u32[]{:S(2)}) %copy-start.2) | copy-done | bytes 2097176
  4.4 0.0 copy-start.3
  4.4 0.9 %copy-done.3 = f32[128,512]{1,0:T(8,128)S(1)} copy-done((f32[128,512]{1,0:T(8,128)S(1)}, f32[128,512]{1,0:T(8,128)}, u32[]{:S(2)}) %copy-start.3) | copy-done | bytes 262168
  5.4 0.0 copy-start.4
  5.4 0.9 %copy-done.4 = f32[128,512]{1,0:T(8,128)S(1)} copy-done((f32[128,512]{1,0:T(8,128)S(1)}, f32[128,512]{1,0:T(8,128)}, u32[]{:S(2)}) %copy-start.4) | copy-done | bytes 262168
  6.3 0.0 copy-start.9
  6.3 0.9 %copy-done.9 = bf16[256,512]{1,0:T(8,128)(2,1)S(1)} copy-done((bf16[256,512]{1,0:T(8,128)(2,1)S(1)}, bf16[256,512]{1,0:T(8,128)(2,1)}, u32[]{:S(2)}) %copy-start.9) | copy-done | bytes 262168
  7.3 0.0 copy-start.10
  7.3 0.9 %copy-done.10 = bf16[256,512]{1,0:T(8,128)(2,1)S(1)} copy-done((bf16[256,512]{1,0:T(8,128)(2,1)S(1)}, bf16[256,512]{1,0:T(8,128)(2,1)}, u32[]{:S(2)}) %copy-start.10) | copy-done | bytes 262168
  8.2 0.0 copy-start.15
  8.2 0.7 copy-done.15
  9.0 0.0 copy-start.16
  9.0 0.7 copy-done.16
  9.7 0.0 copy-start.17
  9.7 0.7 copy-done.17
  10.3 0.0 copy-start.20
  10.4 0.7 copy-done.20
  11.0 0.0 copy-start.21
  11.0 0.7 copy-done.21
  11.7 0.0 copy-start.22
  11.7 0.7 copy-done.22
  12.4 0.0 copy-start.5
  12.4 0.0 copy-start.6
  12.4 0.0 copy-start.7
  12.4 0.0 copy-start.8
  12.4 0.0 copy-start.11
  12.4 0.0 copy-start.12
  12.4 0.0 copy-start.13
  12.5 0.0 copy-start.14
  12.5 0.0 copy-start.18
  12.5 0.0 copy-start.19
  12.5 0.0 copy-start.23
  12.5 0.0 copy-start.24
  12.5 67.3 %shard_map.425 = (bf16[256,512]{1,0:T(8,128)(2,1)S(1)}, bf16[2048,512]{1,0:T(8,128)(2,1)S(1)}, bf16[256,512]{1,0:T(8,128)(2,1)S(1)}, bf16[2048,512]{1,0:T(8,128)...) custom-call(bf16[256,512]{1,0:T(8,128)(2,1)S(1)} %copy-done.9, bf16[2048,512]{1,0:T(8,128)(2,1)S(1)} %copy-done.2, ...), custom_call_target="tpu_custom_call" | custom-call | tf_op jit(solution)/shard_map/pallas_call | solution.py:914
  79.9 0.0 copy-done.5
  79.9 0.0 copy-done.6
  79.9 0.0 copy-done.7
  79.9 0.0 copy-done.8
  79.9 0.0 copy-done.11
  79.9 0.0 copy-done.12
  79.9 0.0 copy-done.13
  79.9 0.0 copy-done.14
  79.9 0.0 copy-done.18
  79.9 0.0 copy-done.19
  80.0 0.0 copy-done.23
  80.0 0.0 copy-done.24
  80.0 5.4 %shard_map.426 = (bf16[256,512]{1,0:T(8,128)(2,1)}, bf16[2048,512]{1,0:T(8,128)(2,1)}, bf16[256,512]{1,0:T(8,128)(2,1)}, bf16[2048,512]{1,0:T(8,128)(2,1)}, f32[...) custom-call(bf16[3712,128]{1,0:T(8,128)(2,1)S(1)} %get-tuple-element, ...), custom_call_target="tpu_custom_call" | custom-call | tf_op jit(solution)/shard_map/pallas_call | solution.py:938
Async XLA Ops:
  0.7 1.1 %copy-start = (f32[1536,128]{1,0:T(8,128)S(1)}, f32[1536,128]{1,0:T(8,128)}, u32[]{:S(2)}) copy-start(f32[1536,128]{1,0:T(8,128)} %refs_6_.3) | copy-start | bytes 2359300
  1.8 1.0 %copy-start.1 = (f32[1024,128]{1,0:T(8,128)S(1)}, f32[1024,128]{1,0:T(8,128)}, u32[]{:S(2)}) copy-start(f32[1024,128]{1,0:T(8,128)} %refs_8_.3) | copy-start | bytes 1572868
  2.8 1.6 %copy-start.2 = (bf16[2048,512]{1,0:T(8,128)(2,1)S(1)}, bf16[2048,512]{1,0:T(8,128)(2,1)}, u32[]{:S(2)}) copy-start(bf16[2048,512]{1,0:T(8,128)(2,1)} %refs_1_.1) | copy-start | bytes 6291460
  4.4 0.9 %copy-start.3 = (f32[128,512]{1,0:T(8,128)S(1)}, f32[128,512]{1,0:T(8,128)}, u32[]{:S(2)}) copy-start(f32[128,512]{1,0:T(8,128)} %refs_7_.3) | copy-start | bytes 786436
  5.4 0.9 %copy-start.4 = (f32[128,512]{1,0:T(8,128)S(1)}, f32[128,512]{1,0:T(8,128)}, u32[]{:S(2)}) copy-start(f32[128,512]{1,0:T(8,128)} %refs_9_.3) | copy-start | bytes 786436
  6.3 0.9 %copy-start.9 = (bf16[256,512]{1,0:T(8,128)(2,1)S(1)}, bf16[256,512]{1,0:T(8,128)(2,1)}, u32[]{:S(2)}) copy-start(bf16[256,512]{1,0:T(8,128)(2,1)} %refs_0_.1) | copy-start | bytes 786436
  7.3 0.9 %copy-start.10 = (bf16[256,512]{1,0:T(8,128)(2,1)S(1)}, bf16[256,512]{1,0:T(8,128)(2,1)}, u32[]{:S(2)}) copy-start(bf16[256,512]{1,0:T(8,128)(2,1)} %refs_2_.1) | copy-start | bytes 786436
  8.2 0.7 copy-start.15
  9.0 0.7 copy-start.16
  9.7 0.7 copy-start.17
  10.3 0.7 copy-start.20
  11.0 0.7 copy-start.21
  11.7 0.7 copy-start.22
  12.4 67.4 %copy-start.5 = (f32[1536,128]{1,0:T(8,128)S(1)}, f32[1536,128]{1,0:T(8,128)}, u32[]{:S(2)}) copy-start(f32[1536,128]{1,0:T(8,128)} %refs_12_.1) | copy-start | bytes 2359300
  12.4 67.4 %copy-start.6 = (f32[1536,128]{1,0:T(8,128)S(1)}, f32[1536,128]{1,0:T(8,128)}, u32[]{:S(2)}) copy-start(f32[1536,128]{1,0:T(8,128)} %refs_18_.1) | copy-start | bytes 2359300
  12.4 67.5 %copy-start.7 = (f32[1024,128]{1,0:T(8,128)S(1)}, f32[1024,128]{1,0:T(8,128)}, u32[]{:S(2)}) copy-start(f32[1024,128]{1,0:T(8,128)} %refs_14_.1) | copy-start | bytes 1572868
  12.4 67.5 %copy-start.8 = (f32[1024,128]{1,0:T(8,128)S(1)}, f32[1024,128]{1,0:T(8,128)}, u32[]{:S(2)}) copy-start(f32[1024,128]{1,0:T(8,128)} %refs_20_.1) | copy-start | bytes 1572868
  12.4 67.5 %copy-start.11 = (f32[128,512]{1,0:T(8,128)S(1)}, f32[128,512]{1,0:T(8,128)}, u32[]{:S(2)}) copy-start(f32[128,512]{1,0:T(8,128)} %refs_13_.1) | copy-start | bytes 786436
  12.4 67.5 %copy-start.12 = (f32[128,512]{1,0:T(8,128)S(1)}, f32[128,512]{1,0:T(8,128)}, u32[]{:S(2)}) copy-start(f32[128,512]{1,0:T(8,128)} %refs_15_.3) | copy-start | bytes 786436
  12.4 67.5 %copy-start.13 = (f32[128,512]{1,0:T(8,128)S(1)}, f32[128,512]{1,0:T(8,128)}, u32[]{:S(2)}) copy-start(f32[128,512]{1,0:T(8,128)} %refs_19_.1) | copy-start | bytes 786436
  12.5 67.5 %copy-start.14 = (f32[128,512]{1,0:T(8,128)S(1)}, f32[128,512]{1,0:T(8,128)}, u32[]{:S(2)}) copy-start(f32[128,512]{1,0:T(8,128)} %refs_21_.1) | copy-start | bytes 786436
  12.5 67.5 %copy-start.18 = (f32[6,512]{1,0:T(8,128)S(1)}, f32[6,512]{1,0:T(8,128)}, u32[]{:S(2)}) copy-start(f32[6,512]{1,0:T(8,128)} %refs_17_.1) | copy-start | bytes 36868
  12.5 67.5 %copy-start.19 = (f32[6,512]{1,0:T(8,128)S(1)}, f32[6,512]{1,0:T(8,128)}, u32[]{:S(2)}) copy-start(f32[6,512]{1,0:T(8,128)} %refs_23_.1) | copy-start | bytes 36868
  12.5 67.5 %copy-start.23 = (f32[2,128]{1,0:T(2,128)S(1)}, f32[2,128]{1,0:T(2,128)}, u32[]{:S(2)}) copy-start(f32[2,128]{1,0:T(2,128)} %refs_16_.1) | copy-start | bytes 3076
  12.5 67.5 %copy-start.24 = (f32[2,128]{1,0:T(2,128)S(1)}, f32[2,128]{1,0:T(2,128)}, u32[]{:S(2)}) copy-start(f32[2,128]{1,0:T(2,128)} %refs_22_.1) | copy-start | bytes 3076

commit v3 on v2

--- a/solution.py
+++ b/solution.py
@@ -14,6 +14,7 @@
 MESH = pl.DeviceIdType.MESH
 LANES = 128
 TILE = 256
+ROWS = 512
 
 beta_one = 0.9
 beta_two = 0.999
@@ -74,7 +75,7 @@
     s = types.SimpleNamespace(**dict(zip(names, refs, strict=True)))
     R, N, E, L, H, Q, CAP = d.R, d.N, d.E, d.L, d.H, d.Q, d.CAP
     EH, S, half, LH = E // 2, R * CAP, H // 2, L // 2
-    tiles, slot_tiles, nb = EH // TILE, S // TILE, R // 4
+    tiles, slot_tiles, nb = EH // ROWS, S // TILE, R // 4
     r = lax.axis_index("rows")
     t = lax.axis_index("tp")
     h, c = t // 2, lax.rem(t, 2)
@@ -101,7 +102,11 @@
             body(k)
             return carry
 
-        lax.fori_loop(low, high, step, 0)
+        if high - low <= 8:
+            for k in range(low, high):
+                body(k)
+        else:
+            lax.fori_loop(low, high, step, 0)
 
     loads = [
         local(s.wei_h, s.wei32, s.lsem.at[0]),
@@ -112,9 +117,17 @@
         local(s.wno_h, s.wno32, s.lsem.at[5]),
         local(s.ncot_h, s.ncot, s.lsem.at[6]),
         local(s.ecot_h.at[rows_of(edge0, EH)], s.ecot, s.lsem.at[7]),
+        local(s.serve_h, s.serve, s.lsem.at[8]),
+        local(s.hb_h, s.hb, s.lsem.at[9]),
+        local(s.fv_h, s.fv, s.lsem.at[10]),
+        local(s.rec2_h, s.rec2, s.lsem.at[11]),
+        local(s.slot2_h, s.slot2, s.lsem.at[12]),
+        local(s.mask2_h, s.mask2, s.lsem.at[13]),
+        local(s.rec1_h, s.rec1, s.lsem.at[14]),
+        local(s.slot1_h, s.slot1, s.lsem.at[15]),
     ]
-    for load in loads:
-        load.start()
+    for k in (0, 1, 8, 9, 3, 11, 12, 13, 14, 15, 2, 4, 5, 10, 6, 7):
+        loads[k].start()
 
     barrier = pltpu.get_barrier_semaphore()
     for peer in (pair, far, diag):
@@ -125,42 +138,61 @@
 
     loop(1, R, greet)
 
-    def block(i, tt):
+    shared = (1, 2, 4, 5)
+
+    def block(i, tt, part=None):
         lane = pl.ds(pl.multiple_of(tt * Q, Q), Q)
         if i < 3:
             half_lane = pl.ds(pl.multiple_of(lax.rem(tt, 2) * Q, Q), Q)
-            return s.wei.at[tt // 2, pl.ds((0, 2 * L, L)[i], L), half_lane]
+            rows = pl.ds((0, 2 * L, L)[i], L) if part is None else rows_of((0, 2 * L, L)[i] + part * (L // 4), L // 4)
+            return s.wei.at[tt // 2, rows, half_lane]
         if i == 3:
             return s.weo.at[lane, :]
         if i < 6:
-            return s.wni.at[pl.ds((L, 0)[i - 4], L), lane]
+            low = (L, 0)[i - 4]
+            return s.wni.at[pl.ds(low, L) if part is None else rows_of(low + part * (L // 4), L // 4), lane]
         if i == 6:
             return s.wno.at[lane, :]
         return s.bias.at[:, lane]
 
     def weight_copy(i, way, who):
-        ref = block(i, who)
+        ref = block(i, who, a if way == 1 and i in shared else None)
         return remote(ref, ref, s.wsend.at[i, way], s.wrecv.at[i, way], (r, (pair, far, pair)[way]))
 
-    def weight_send(i):
-        weight_copy(i, 1, t).start()
-        weight_copy(i, 0, t).start()
+    def part_copy(i, j, part):
+        ref = block(i, far, part)
+        device = (b * 4 + lax.rem(a + j, 4), t)
+        return remote(ref, ref, s.wsend.at[i, 2 + j], s.wrecv.at[i, 2 + j], device)
+
+    def weight_send(i, way):
+        weight_copy(i, way, t).start()
 
     def weight_wait(i, way):
         weight_copy(i, way, (pair, far, diag)[way]).wait_recv()
 
+    def part_spread(i):
+        weight_wait(i, 1)
+        for j in (1, 2, 3):
+            part_copy(i, j, a).start()
+
     def weight_forward(i):
-        weight_wait(i, 1)
+        if i in shared:
+            for j in (1, 2, 3):
+                part_copy(i, j, lax.rem(a + 4 - j, 4)).wait_recv()
+        else:
+            weight_wait(i, 1)
         weight_copy(i, 2, far).start()
 
     loads[0].wait()
     for i in range(3):
         at = pl.ds((0, 2 * L, L)[i], L)
         s.wei[h, at, core_lane] = s.wei32[at, :].astype(BF)
+    loads[9].wait()
     s.bias[0:2, own_lane] = s.hb[...]
     s.bias[2:8, own_lane] = jnp.zeros((6, Q), F32)
     loads[1].wait()
 
+    loads[8].wait()
     turned = jnp.transpose(s.serve[...].astype(F32))
     for k in range(R):
         s.serve_col[k * CAP : (k + 1) * CAP, :] = turned[:, k : k + 1]
@@ -175,9 +207,8 @@
     loop(0, slot_tiles, serve)
     pl.semaphore_wait(barrier, R + 2)
 
-    for i in range(3):
-        weight_send(i)
-    weight_send(7)
+    for i in (1, 2, 7, 0):
+        weight_send(i, 1)
     mine = rows_of(r * CAP, CAP)
 
     def served_copy(k):
@@ -192,18 +223,24 @@
 
     loop(1, R, lambda k: served_copy(k).start())
     s.slots[mine, col_lane] = s.served[mine, :]
-    loads[3].wait()
-    s.weo[own_lane, :] = s.weo32[...].astype(BF)
-    weight_send(3)
+    for i in (0, 1, 2, 7):
+        weight_send(i, 0)
     loads[4].wait()
     for i in (4, 5):
         at = pl.ds((L, 0)[i - 4], L)
         s.wni[at, own_lane] = s.wni32[at, :].astype(BF)
-        weight_send(i)
+        weight_send(i, 1)
+    loads[3].wait()
+    s.weo[own_lane, :] = s.weo32[...].astype(BF)
     loads[5].wait()
     s.wno[own_lane, :] = s.wno32[...].astype(BF)
-    weight_send(6)
-
+    for i in (3, 6):
+        weight_send(i, 1)
+    for i in (3, 4, 5, 6):
+        weight_send(i, 0)
+
+    for k in (11, 12, 13, 14, 15):
+        loads[k].wait()
     per = EH // LANES
     at = rows_of(c * per, per, 8)
     for source, target in ((s.rec2, s.rcol), (s.slot2, s.scol), (s.mask2, s.mcol)):
@@ -212,6 +249,8 @@
             target[k * LANES : (k + 1) * LANES, :] = turned[:, k : k + 1]
     lanes_here = pl.ds(pl.multiple_of(edge0, EH), EH)
     s.rhot_t[...] = hot(s.rec1[:, lanes_here] == lax.broadcasted_iota(jnp.int32, (N, EH), 0))
+    part_spread(1)
+    part_spread(2)
 
     def slot_table(k):
         rows = rows_of(k * TILE, TILE)
@@ -222,34 +261,37 @@
     loop(0, slot_tiles, slot_table)
 
     def receivers(k):
-        rows = rows_of(k * TILE, TILE)
+        rows = rows_of(k * ROWS, ROWS)
         index = s.rcol[rows, :].astype(jnp.int32)
-        table = hot(index == lax.broadcasted_iota(jnp.int32, (TILE, N), 1))
+        table = hot(index == lax.broadcasted_iota(jnp.int32, (ROWS, N), 1))
         s.rhot[rows, :] = table
         s.xr[rows, :] = mm(table, s.nf[...]).astype(BF)
 
     loop(0, tiles, receivers)
+    loads[2].wait()
+
+    def first_two(which):
+        def body(k):
+            rows = rows_of(k * ROWS, ROWS)
+            value = mm(s.ef[rows, :], s.wei[which, 0:L, :])
+            s.pre[which, rows, :] = value + mm(s.xr[rows, :], s.wei[which, 2 * L : 3 * L, :])
+
+        loop(0, tiles, body)
+
+    def hidden_of(which, k):
+        rows = rows_of(k * ROWS, ROWS)
+        lanes = pl.ds(pl.multiple_of(which * half, half), half)
+        pre = s.pre[which, rows, :] + mm(s.xs[rows, :], s.wei[which, L : 2 * L, :]) + s.bias[0:1, lanes]
+        sig = 0.5 + 0.5 * jnp.tanh(0.5 * pre)
+        value = (pre * sig).astype(BF)
+        s.hid[which, rows, :] = value
+        s.pre[which, rows, :] = sig + (pre * sig) * (1.0 - sig)
+        return mm(value, s.weo[rows_of(which * half, half), :])
+
+    for i in (0, 1):
+        weight_wait(i, 0)
+    first_two(h)
     s.g[...] = jnp.zeros_like(s.g)
-    loads[2].wait()
-
-    def first_edges(which):
-        def body(k):
-            rows = rows_of(k * TILE, TILE)
-            s.pre[which, rows, :] = mm(s.ef[rows, :], s.wei[which, 0:L, :])
-
-        loop(0, tiles, body)
-
-    def first_more(which, source, low):
-        def body(k):
-            rows = rows_of(k * TILE, TILE)
-            s.pre[which, rows, :] += mm(source[rows, :], s.wei[which, low : low + L, :])
-
-        loop(0, tiles, body)
-
-    weight_wait(0, 0)
-    first_edges(h)
-    weight_wait(1, 0)
-    first_more(h, s.xr, 2 * L)
     weight_forward(0)
 
     def served_wait(k):
@@ -260,39 +302,40 @@
     loop(1, R, served_wait)
     slot_swap = remote(s.slots.at[:, col_lane], s.slots.at[:, col_lane], s.xsend.at[2], s.xrecv.at[2], (r, pair))
     slot_swap.start()
-    weight_wait(0, 2)
-    first_edges(oh)
     weight_forward(1)
     other_lane = pl.ds(pl.multiple_of(oc * LH, LH), LH)
     ref = s.slots.at[:, other_lane]
     remote(ref, ref, s.xsend.at[2], s.xrecv.at[2], (r, pair)).wait_recv()
 
     def senders(k):
-        rows = rows_of(k * TILE, TILE)
+        rows = rows_of(k * ROWS, ROWS)
         index = s.scol[rows, :].astype(jnp.int32)
-        table = hot(index == lax.broadcasted_iota(jnp.int32, (TILE, S), 1))
+        table = hot(index == lax.broadcasted_iota(jnp.int32, (ROWS, S), 1))
         s.xs[rows, :] = mm(table, s.slots[...]).astype(BF)
 
     loop(0, tiles, senders)
-    weight_wait(2, 0)
-    first_more(h, s.xs, L)
-    weight_wait(1, 2)
-    first_more(oh, s.xr, 2 * L)
     weight_forward(2)
+    part_spread(4)
+    part_spread(5)
+    for i in (2, 7, 3):
+        weight_wait(i, 0)
+
+    def own_half(k):
+        s.part[rows_of(k * ROWS, ROWS), :] = hidden_of(h, k)
+
+    loop(0, tiles, own_half)
     weight_forward(7)
+    for i in (0, 1):
+        weight_wait(i, 2)
+    first_two(oh)
     weight_forward(3)
-    weight_wait(2, 2)
-    first_more(oh, s.xs, L)
-    weight_wait(7, 0)
-    weight_wait(7, 2)
-    weight_wait(3, 0)
-    weight_wait(3, 2)
-
-    s.aggp[...] = jnp.zeros_like(s.aggp)
+    for i in (2, 7, 3):
+        weight_wait(i, 2)
+    loads[10].wait()
 
     def out_copies(k, source, target, which):
-        here = source.at[rows_of(k * TILE, TILE)]
-        there = target.at[rows_of(edge0 + k * TILE, TILE)]
+        here = source.at[rows_of(k * ROWS, ROWS)]
+        there = target.at[rows_of(edge0 + k * ROWS, ROWS)]
         keep = local(here, there, s.osem.at[which, k])
         send = remote(here, there, s.osend.at[which, k], s.orecv.at[which, k], (r, pair))
         return keep, send
@@ -306,36 +349,27 @@
         keep, send = out_copies(k, source, target, which)
         keep.wait()
         send.wait_send()
-        ref = target.at[rows_of(oc * EH + k * TILE, TILE)]
+        ref = target.at[rows_of(oc * EH + k * ROWS, ROWS)]
         remote(ref, ref, s.osend.at[which, k], s.orecv.at[which, k], (r, pair)).wait_recv()
 
     def forward(k):
-        rows = rows_of(k * TILE, TILE)
-        hidden = []
-        for p in (0, 1):
-            pre = s.pre[p, rows, :] + s.bias[0:1, p * half : (p + 1) * half]
-            sig = 1.0 / (1.0 + jnp.exp(-pre))
-            value = (pre * sig).astype(BF)
-            s.hid[p, rows, :] = value
-            s.pre[p, rows, :] = sig * (1.0 + pre * (1.0 - sig))
-            hidden.append(value)
-        outer = mm(hidden[0], s.weo[0:half, :]) + mm(hidden[1], s.weo[half:H, :]) + s.fv[0:1, :]
+        rows = rows_of(k * ROWS, ROWS)
+        outer = s.part[rows, :] + hidden_of(oh, k) + s.fv[0:1, :]
         normed, inverse = normalize(outer)
         s.normed[rows, :] = normed
         s.inv[rows, :] = inverse
         masked = s.mcol[rows, :] * (normed * s.fv[1:2, :] + s.fv[2:3, :])
         s.ne[rows, :] = (s.ef[rows, :].astype(F32) + masked).astype(BF)
         out_start(k, s.ne, s.ne_h, 0)
-        high, low = two(masked)
-        table = s.rhot_t[:, pl.ds(pl.multiple_of(k * TILE, TILE), TILE)]
-        s.aggp[...] += mm(table, high) + mm(table, low)
+        s.mk[rows, :] = masked.astype(BF)
 
     loop(0, tiles, forward)
+    s.aggp[...] = mm(s.rhot_t[...], s.mk[...])
     swap = remote(s.aggp, s.aggr, s.xsend.at[0], s.xrecv.at[0], (r, pair))
     swap.start()
+    for i in (4, 5, 6):
+        weight_forward(i)
     weight_wait(5, 0)
-    weight_forward(4)
-    weight_forward(5)
     weight_wait(5, 2)
     own_term = mm(s.nf[...], s.wni[0:L, :])
     weight_wait(4, 0)
@@ -344,10 +378,9 @@
 
     agg = (s.aggp[...] + s.aggr[...]).astype(BF)
     pre = own_term + mm(agg, s.wni[L : 2 * L, :]) + s.bias[1:2, :]
-    sig = 1.0 / (1.0 + jnp.exp(-pre))
+    sig = 0.5 + 0.5 * jnp.tanh(0.5 * pre)
     node_hidden = (pre * sig).astype(BF)
-    slope_of = sig * (1.0 + pre * (1.0 - sig))
-    weight_forward(6)
+    slope_of = sig + (pre * sig) * (1.0 - sig)
     weight_wait(6, 0)
     weight_wait(6, 2)
     outer = mm(node_hidden, s.wno[...]) + s.fv[3:4, :]
@@ -359,9 +392,7 @@
     up = s.ncot[...].astype(F32)
     node_outer_grad = norm_back(up * s.fv[4:5, :], normed, inverse).astype(BF)
     node_slope = (nt(node_outer_grad, s.wno[...]) * slope_of).astype(BF)
-    agg_high, agg_low = two(nt(node_slope, s.wni[L : 2 * L, :]))
-    s.agh[...] = agg_high
-    s.agl[...] = agg_low
+    s.agh[...] = nt(node_slope, s.wni[L : 2 * L, :]).astype(BF)
 
     for q in range(H // Q):
         s.nsl[q] = node_slope[:, q * Q : (q + 1) * Q]
@@ -448,11 +479,11 @@
             b_copy(n, jj, lax.rem(b + jj, nb)).start()
 
     def to_b(n, jj):
-        ref = s.fin.at[piece(n, a, b)]
+        ref = s.fin_o.at[piece(n, a, b)]
         return remote(ref, ref, s.fbsend.at[n, jj], s.fbrecv.at[n, jj], (b_row(jj), t))
 
     def to_a(n, jj, j):
-        ref = s.fin.at[piece(n, a, lax.rem(b + nb - jj, nb))]
+        ref = s.fin_o.at[piece(n, a, lax.rem(b + nb - jj, nb))]
         return remote(ref, ref, s.fasend.at[n, jj, j], s.farecv.at[n, jj, j], (a_row(j), t))
 
     def b_finish(n):
@@ -462,7 +493,7 @@
             b_copy(n, jj, b).wait_recv()
             total = total + s.rbb[jj - 1, b_slot(n), :].astype(F32)
         final = total.astype(BF)
-        s.fin[at, :] = final
+        s.fin_o[at, :] = final
         for jj in range(1, nb):
             to_b(n, jj).start()
         for j in (1, 2, 3):
@@ -478,7 +509,7 @@
 
     def spread(n):
         for jj in range(1, nb):
-            ref = s.fin.at[piece(n, a, lax.rem(b + nb - jj, nb))]
+            ref = s.fin_o.at[piece(n, a, lax.rem(b + nb - jj, nb))]
             remote(ref, ref, s.fbsend.at[n, jj], s.fbrecv.at[n, jj], (b_row(jj), t)).wait_recv()
             for j in (1, 2, 3):
                 to_a(n, jj, j).start()
@@ -486,7 +517,7 @@
     def spread_wait(n):
         for jj in range(nb):
             for j in (1, 2, 3):
-                ref = s.fin.at[piece(n, lax.rem(a + 4 - j, 4), lax.rem(b + nb - jj, nb))]
+                ref = s.fin_o.at[piece(n, lax.rem(a + 4 - j, 4), lax.rem(b + nb - jj, nb))]
                 remote(ref, ref, s.fasend.at[n, jj, j], s.farecv.at[n, jj, j], (a_row(j), t)).wait_recv()
 
     def sums_done(n):
@@ -505,10 +536,10 @@
     loads[7].wait()
 
     def backward_norm(k):
-        rows = rows_of(k * TILE, TILE)
+        rows = rows_of(k * ROWS, ROWS)
         table = s.rhot[rows, :]
         cot = s.ecot[rows, :].astype(F32)
-        up = s.mcol[rows, :] * (cot + (mm(table, s.agh[...]) + mm(table, s.agl[...])))
+        up = s.mcol[rows, :] * (cot + mm(table, s.agh[...]))
         normed = s.normed[rows, :]
         grad = norm_back(up * s.fv[1:2, :], normed, s.inv[rows, :]).astype(BF)
         s.og[rows, :] = grad
@@ -525,28 +556,30 @@
     pair_start(1)
 
     def slope_half(which, k):
-        rows = rows_of(k * TILE, TILE)
+        rows = rows_of(k * ROWS, ROWS)
         w_rows = rows_of(which * half, half)
         value = (nt(s.og[rows, :], s.weo[w_rows, :]) * s.pre[which, rows, :]).astype(BF)
         s.sl[which, rows, :] = value
-        lanes = pl.ds(pl.multiple_of(k * TILE, TILE), TILE)
-        s.rs[which] += mm(s.rhot_t[:, lanes], value)
+        return value
+
+    def slope_sums(which):
+        s.rs[which] = mm(s.rhot_t[...], s.sl[which])
 
         def slots(j):
             at = rows_of(j * TILE, TILE)
-            s.ss[which, at, :] += mm(s.shot_t[at, lanes], value)
+            s.ss[which, at, :] = mm(s.shot_t[at, :], s.sl[which])
 
         loop(0, slot_tiles, slots)
-        return value
-
-    s.rs[...] = jnp.zeros_like(s.rs)
-    s.ss[...] = jnp.zeros_like(s.ss)
 
     def backward_own(k):
         value = slope_half(h, k)
         s.vsum[6:7, 0:half] += row_sum(value.astype(F32))
 
     loop(0, tiles, backward_own)
+    slope_sums(h)
+
+    pair_finish(1)
+    a_send(1)
 
     edge_part = tn(s.ef[...], s.sl[h])
     recv_part = tn(s.nf[...], s.rs[h].astype(BF))
@@ -569,14 +602,12 @@
 
     loop(0, slot_tiles, sender_part)
     pair_start(2)
-    pair_finish(1)
-    a_send(1)
+    b_send(0)
     pair_finish(2)
     a_send(2)
-    b_send(0)
 
     def backward_other(k):
-        rows = rows_of(k * TILE, TILE)
+        rows = rows_of(k * ROWS, ROWS)
         value = slope_half(oh, k)
         cot = s.ecot[rows, :].astype(F32)
         back = nt(s.sl[0, rows, :], s.wei[0, 0:L, :]) + nt(s.sl[1, rows, :], s.wei[1, 0:L, :])
@@ -584,9 +615,9 @@
         out_start(k, s.eg, s.eg_h, 1)
 
     loop(0, tiles, backward_other)
+    slope_sums(oh)
+    b_send(1)
     b_finish(0)
-    b_send(1)
-    b_send(2)
 
     def slot_grad(which, rows):
         at = rows_of(L + which * LH, LH)
@@ -604,6 +635,7 @@
     s.tosend[S : S + N, :] = recv_grad(oc).astype(BF)
     grad_swap = remote(s.tosend, s.torecv, s.xsend.at[1], s.xrecv.at[1], (r, pair))
     grad_swap.start()
+    b_send(2)
     s.ntp[...] = (
         s.ncot[:, col_lane].astype(F32)
         + (nt(s.nsl[0], s.wni[rows_of(c * LH, LH), 0:Q]) + nt(s.nsl[1], s.wni[rows_of(c * LH, LH), Q : 2 * Q]))
@@ -613,7 +645,6 @@
         )
         + recv_grad(c)
     )
-    b_finish(1)
     grad_swap.wait_recv()
 
     def slot_own(k):
@@ -627,6 +658,9 @@
         to = lax.rem(r + k, R)
         return remote(s.served.at[rows_of(to * CAP, CAP)], s.ret.at[mine], s.ksend.at[k], s.krecv.at[k], (to, t))
 
+    loop(1, R, lambda k: back_copy(k).start())
+    b_finish(1)
+    spread(0)
     b_finish(2)
 
     def norm_row(k):
@@ -635,10 +669,9 @@
         return remote(ref, ref, s.qsend.at[k], s.qrecv.at[k], (to, t))
 
     loop(1, R, lambda k: norm_row(k).start())
-    loop(1, R, lambda k: back_copy(k).start())
     s.ret[mine, :] = s.served[mine, :]
     s.ntp[...] += s.torecv[S : S + N, :].astype(F32)
-    for n in (0, 1, 2):
+    for n in (1, 2):
         spread(n)
 
     def norm_row_wait(k):
@@ -675,7 +708,6 @@
 
     for n in (0, 1, 2):
         spread_wait(n)
-    s.fin_o[...] = s.fin[...]
     for k, peer in enumerate((pair, far, diag)):
         ref = s.nsq.at[rows_of(peer * 8, 8, 8)]
         remote(ref, ref, s.tsem.at[0, k], s.tsem.at[1, k], (r, peer)).wait()
@@ -687,6 +719,9 @@
         weight_copy(i, 0, t).wait_send()
         weight_copy(i, 1, t).wait_send()
         weight_copy(i, 2, far).wait_send()
+        if i in shared:
+            for j in (1, 2, 3):
+                part_copy(i, j, a).wait_send()
     slot_swap.wait_send()
     grad_swap.wait_send()
 
@@ -784,7 +819,7 @@
     d.CAP = serve_rows.shape[1]
     R, N, E, L, H, Q = d.R, d.N, d.E, d.L, d.H, d.Q
     EH, S, nb = E // 2, R * d.CAP, R // 4
-    tiles = EH // TILE
+    tiles = EH // ROWS
 
     def padded(count):
         return -(-count // (16 * R)) * (16 * R)
@@ -792,36 +827,44 @@
     d.size_node, d.size_out, d.size_in = padded(3 * L), padded(L), padded(3 * L + 32)
     d.base_node, d.base_out, d.base_in = 0, d.size_node, d.size_node + d.size_out
     G = d.size_node + d.size_out + d.size_in
-    any_spec = pl.BlockSpec(memory_space=pl.ANY)
     vmem_spec = pl.BlockSpec(memory_space=pltpu.VMEM)
     inputs = dict(
-        nf_h=(node_feats, any_spec),
-        ef_h=(edge_feats, any_spec),
-        ncot_h=(node_cot, any_spec),
-        ecot_h=(edge_cot, any_spec),
-        wei_h=(weights[0], any_spec),
-        weo_h=(weights[1], any_spec),
-        wni_h=(weights[2], any_spec),
-        wno_h=(weights[3], any_spec),
-        hb=(weights[4], vmem_spec),
-        fv=(weights[5], vmem_spec),
-        rec2=(edge_receiver.reshape(-1, LANES), vmem_spec),
-        slot2=(edge_slot.reshape(-1, LANES), vmem_spec),
-        mask2=(edge_mask.reshape(-1, LANES), vmem_spec),
-        rec1=(edge_receiver.reshape(1, -1), vmem_spec),
-        slot1=(edge_slot.reshape(1, -1), vmem_spec),
-        serve=(serve_rows, vmem_spec),
+        nf_h=node_feats,
+        ef_h=edge_feats,
+        ncot_h=node_cot,
+        ecot_h=edge_cot,
+        wei_h=weights[0],
+        weo_h=weights[1],
+        wni_h=weights[2],
+        wno_h=weights[3],
+        hb_h=weights[4],
+        fv_h=weights[5],
+        rec2_h=edge_receiver.reshape(-1, LANES),
+        slot2_h=edge_slot.reshape(-1, LANES),
+        mask2_h=edge_mask.reshape(-1, LANES),
+        rec1_h=edge_receiver.reshape(1, -1),
+        slot1_h=edge_slot.reshape(1, -1),
+        serve_h=serve_rows,
     )
+    hbm_spec = pl.BlockSpec(memory_space=pltpu.HBM)
     outputs = dict(
-        nn_h=(jax.ShapeDtypeStruct((N, L), BF), any_spec),
-        ne_h=(jax.ShapeDtypeStruct((E, L), BF), any_spec),
-        ng_h=(jax.ShapeDtypeStruct((N, L), BF), any_spec),
-        eg_h=(jax.ShapeDtypeStruct((E, L), BF), any_spec),
+        nn_h=(jax.ShapeDtypeStruct((N, L), BF), hbm_spec),
+        ne_h=(jax.ShapeDtypeStruct((E, L), BF), hbm_spec),
+        ng_h=(jax.ShapeDtypeStruct((N, L), BF), hbm_spec),
+        eg_h=(jax.ShapeDtypeStruct((E, L), BF), hbm_spec),
         fin_o=(jax.ShapeDtypeStruct((G, Q), BF), vmem_spec),
         norm_o=(jax.ShapeDtypeStruct((8, LANES), F32), vmem_spec),
     )
     dma = pltpu.SemaphoreType.DMA
     scratch = dict(
+        hb=pltpu.VMEM((2, Q), F32),
+        fv=pltpu.VMEM((6, L), F32),
+        rec2=pltpu.VMEM((E // LANES, LANES), jnp.int32),
+        slot2=pltpu.VMEM((E // LANES, LANES), jnp.int32),
+        mask2=pltpu.VMEM((E // LANES, LANES), jnp.int32),
+        rec1=pltpu.VMEM((1, E), jnp.int32),
+        slot1=pltpu.VMEM((1, E), jnp.int32),
+        serve=pltpu.VMEM((R, d.CAP), jnp.int32),
         wei32=pltpu.VMEM((3 * L, Q), F32),
         weo32=pltpu.VMEM((Q, L), F32),
         wni32=pltpu.VMEM((2 * L, Q), F32),
@@ -848,6 +891,8 @@
         shot_t=pltpu.VMEM((S, EH), BF),
         xr=pltpu.VMEM((EH, L), BF),
         xs=pltpu.VMEM((EH, L), BF),
+        part=pltpu.VMEM((EH, L), F32),
+        mk=pltpu.VMEM((EH, L), BF),
         pre=pltpu.VMEM((2, EH, H // 2), F32),
         hid=pltpu.VMEM((2, EH, H // 2), BF),
         normed=pltpu.VMEM((EH, L), F32),
@@ -859,7 +904,6 @@
         nn=pltpu.VMEM((N, L), BF),
         ng=pltpu.VMEM((N, L // 2), BF),
         agh=pltpu.VMEM((N, L), BF),
-        agl=pltpu.VMEM((N, L), BF),
         ntp=pltpu.VMEM((N, L // 2), F32),
         nsl=pltpu.VMEM((H // Q, N, Q), BF),
         nhid=pltpu.VMEM((H // Q, N, Q), BF),
@@ -874,13 +918,12 @@
         rbp=pltpu.VMEM((G, Q), BF),
         rba=pltpu.VMEM((3, G, Q), BF),
         rbb=pltpu.VMEM((nb - 1, G // R, Q), BF),
-        fin=pltpu.VMEM((G, Q), BF),
         vsum=pltpu.VMEM((8, L), F32),
         norm_a=pltpu.VMEM((8 * R, LANES), F32),
         nsq=pltpu.VMEM((32, LANES), F32),
-        lsem=dma((8,)),
-        wsend=dma((8, 3)),
-        wrecv=dma((8, 3)),
+        lsem=dma((16,)),
+        wsend=dma((8, 6)),
+        wrecv=dma((8, 6)),
         ssend=dma((R,)),
         srecv=dma((R,)),
         ksend=dma((R,)),
@@ -914,13 +957,13 @@
     new_nodes, new_edges, node_gradient, edge_gradient, fin, norm = pl.pallas_call(
         functools.partial(layer, names, d),
         out_shape=[shape for shape, _ in outputs.values()],
-        in_specs=[spec for _, spec in inputs.values()],
+        in_specs=[hbm_spec] * len(inputs),
         out_specs=[spec for _, spec in outputs.values()],
         scratch_shapes=list(scratch.values()),
         compiler_params=pltpu.CompilerParams(
             collective_id=0, has_side_effects=True, vmem_limit_bytes=limit
         ),
-    )(*[value for value, _ in inputs.values()])
+    )(*(pltpu.with_memory_space_constraint(x, pltpu.HBM) for x in inputs.values()))
 
     passes = (new_nodes, new_edges, node_gradient, edge_gradient)
     names = (
@@ -942,10 +985,10 @@
             jax.ShapeDtypeStruct((1,), F32),
             *(jax.ShapeDtypeStruct(x.shape, F32) for x in states),
         ],
-        in_specs=[vmem_spec, vmem_spec, *[any_spec] * 4, *[vmem_spec] * 18],
-        out_specs=[*[any_spec] * 4, pl.BlockSpec(memory_space=pltpu.SMEM), *[any_spec] * 18],
+        in_specs=[vmem_spec, vmem_spec, *[hbm_spec] * 4, *[vmem_spec] * 18],
+        out_specs=[*[hbm_spec] * 4, pl.BlockSpec(memory_space=pltpu.SMEM), *[hbm_spec] * 18],
         scratch_shapes=[*(pltpu.VMEM(x.shape, F32) for x in states), dma((4,)), dma((18,))],
-        compiler_params=pltpu.CompilerParams(vmem_limit_bytes=32 * 1024 * 1024),
+        compiler_params=pltpu.CompilerParams(vmem_limit_bytes=12 * 1024 * 1024),
     )(fin, norm, *passes, *states)
     return tuple(outs)
 

time: 86.1 us -> 65.5 us (0.76)
  local copies, waits for them, and re-layouts: 11.8 us -> 0.08 us
  Pallas kernels: 72.7 us -> 64.2 us
    unnamed x50 -> x36, local copies, waits for them, and re-layouts: 11.8 us -> 0.08 us
    pallas_call x1, Pallas kernels: 67.3 us -> 58.8 us  [device_step(): pl.pallas_call(functools.partial(layer, names, d), out_shape=[shape for s...]
where the time goes in v3:
time: 65.5 us; the launch traced here: 65.4 us
  Pallas kernels  64.2 us (98%)
  between operations  1.14 us (2%)
    pallas_call x1, Pallas kernels, device_step(): pl.pallas_call(functools.partial(layer, names, d), out_shape=[shape for s...  58.8 us
    pallas_call x1, Pallas kernels, device_step(): pl.pallas_call(functools.partial(update, names, d), out_shape=[*(jax.Shap...  5.36 us

profile of v3, /device:TPU:0, one launch (start us, length us, event | category | flops | bytes accessed | tf_op | source)
XLA Modules:
  0.0 65.4 jit_solution(11234060317455164626)
XLA Ops:
  0.7 0.0 copy-start
  0.7 0.0 copy-start.1
  0.7 0.0 copy-start.2
  0.7 0.0 copy-start.3
  0.7 0.0 copy-start.4
  0.7 0.0 copy-start.5
  0.7 0.0 copy-start.6
  0.7 0.0 copy-start.7
  0.7 0.0 copy-start.8
  0.8 0.0 copy-start.9
  0.8 0.0 copy-start.10
  0.8 0.0 copy-start.11
  0.8 0.0 copy-start.12
  0.8 0.0 copy-start.13
  0.8 0.0 copy-start.14
  0.8 0.0 copy-start.15
  0.8 0.0 copy-start.16
  0.8 0.0 copy-start.17
  0.8 58.8 %shard_map.425 = (bf16[256,512]{1,0:T(8,128)(2,1)S(1)}, bf16[2048,512]{1,0:T(8,128)(2,1)S(1)}, bf16[256,512]{1,0:T(8,128)(2,1)S(1)}, bf16[2048,512]{1,0:T(8,128)...) custom-call(bf16[256,512]{1,0:T(8,128)(2,1)} %refs_0_.1, bf16[2048,512]{1,0:T(8,128)(2,1)} %refs_1_.1, ...), custom_call_target="tpu_custom_call" | custom-call | tf_op jit(solution)/shard_map/pallas_call | solution.py:957
  59.7 0.0 copy-done
  59.7 0.0 copy-done.1
  59.7 0.0 copy-done.2
  59.7 0.0 copy-done.3
  59.7 0.0 copy-done.4
  59.7 0.0 copy-done.5
  59.7 0.0 copy-done.6
  59.7 0.0 copy-done.7
  59.7 0.0 copy-done.8
  59.8 0.0 copy-done.9
  59.8 0.0 copy-done.10
  59.8 0.0 copy-done.11
  59.8 0.0 copy-done.12
  59.8 0.0 copy-done.13
  59.8 0.0 copy-done.14
  59.8 0.0 copy-done.15
  59.8 0.0 copy-done.16
  59.8 0.0 copy-done.17
  59.8 5.4 %shard_map.426 = (bf16[256,512]{1,0:T(8,128)(2,1)}, bf16[2048,512]{1,0:T(8,128)(2,1)}, bf16[256,512]{1,0:T(8,128)(2,1)}, bf16[2048,512]{1,0:T(8,128)(2,1)}, f32[...) custom-call(bf16[3712,128]{1,0:T(8,128)(2,1)S(1)} %get-tuple-element, ...), custom_call_target="tpu_custom_call" | custom-call | tf_op jit(solution)/shard_map/pallas_call | solution.py:981
Async XLA Ops:
  0.7 59.0 %copy-start = (f32[1536,128]{1,0:T(8,128)S(1)}, f32[1536,128]{1,0:T(8,128)}, u32[]{:S(2)}) copy-start(f32[1536,128]{1,0:T(8,128)} %refs_6_.3) | copy-start | bytes 2359300
  0.7 59.0 %copy-start.1 = (f32[1024,128]{1,0:T(8,128)S(1)}, f32[1024,128]{1,0:T(8,128)}, u32[]{:S(2)}) copy-start(f32[1024,128]{1,0:T(8,128)} %refs_8_.3) | copy-start | bytes 1572868
  0.7 59.0 %copy-start.2 = (f32[128,512]{1,0:T(8,128)S(1)}, f32[128,512]{1,0:T(8,128)}, u32[]{:S(2)}) copy-start(f32[128,512]{1,0:T(8,128)} %refs_7_.3) | copy-start | bytes 786436
  0.7 59.0 %copy-start.3 = (f32[128,512]{1,0:T(8,128)S(1)}, f32[128,512]{1,0:T(8,128)}, u32[]{:S(2)}) copy-start(f32[128,512]{1,0:T(8,128)} %refs_9_.3) | copy-start | bytes 786436
  0.7 59.0 %copy-start.4 = (f32[1536,128]{1,0:T(8,128)S(1)}, f32[1536,128]{1,0:T(8,128)}, u32[]{:S(2)}) copy-start(f32[1536,128]{1,0:T(8,128)} %refs_12_.1) | copy-start | bytes 2359300
  0.7 59.0 %copy-start.5 = (f32[1536,128]{1,0:T(8,128)S(1)}, f32[1536,128]{1,0:T(8,128)}, u32[]{:S(2)}) copy-start(f32[1536,128]{1,0:T(8,128)} %refs_18_.1) | copy-start | bytes 2359300
  0.7 59.0 %copy-start.6 = (f32[1024,128]{1,0:T(8,128)S(1)}, f32[1024,128]{1,0:T(8,128)}, u32[]{:S(2)}) copy-start(f32[1024,128]{1,0:T(8,128)} %refs_14_.1) | copy-start | bytes 1572868
  0.7 59.0 %copy-start.7 = (f32[1024,128]{1,0:T(8,128)S(1)}, f32[1024,128]{1,0:T(8,128)}, u32[]{:S(2)}) copy-start(f32[1024,128]{1,0:T(8,128)} %refs_20_.1) | copy-start | bytes 1572868
  0.7 59.0 %copy-start.8 = (f32[128,512]{1,0:T(8,128)S(1)}, f32[128,512]{1,0:T(8,128)}, u32[]{:S(2)}) copy-start(f32[128,512]{1,0:T(8,128)} %refs_13_.1) | copy-start | bytes 786436
  0.8 59.0 %copy-start.9 = (f32[128,512]{1,0:T(8,128)S(1)}, f32[128,512]{1,0:T(8,128)}, u32[]{:S(2)}) copy-start(f32[128,512]{1,0:T(8,128)} %refs_15_.3) | copy-start | bytes 786436
  0.8 59.0 %copy-start.10 = (f32[128,512]{1,0:T(8,128)S(1)}, f32[128,512]{1,0:T(8,128)}, u32[]{:S(2)}) copy-start(f32[128,512]{1,0:T(8,128)} %refs_19_.1) | copy-start | bytes 786436
  0.8 59.0 %copy-start.11 = (f32[128,512]{1,0:T(8,128)S(1)}, f32[128,512]{1,0:T(8,128)}, u32[]{:S(2)}) copy-start(f32[128,512]{1,0:T(8,128)} %refs_21_.1) | copy-start | bytes 786436
  0.8 59.0 %copy-start.12 = (f32[6,512]{1,0:T(8,128)S(1)}, f32[6,512]{1,0:T(8,128)}, u32[]{:S(2)}) copy-start(f32[6,512]{1,0:T(8,128)} %refs_11_.1) | copy-start | bytes 36868
  0.8 59.0 %copy-start.13 = (f32[6,512]{1,0:T(8,128)S(1)}, f32[6,512]{1,0:T(8,128)}, u32[]{:S(2)}) copy-start(f32[6,512]{1,0:T(8,128)} %refs_17_.1) | copy-start | bytes 36868
  0.8 59.0 %copy-start.14 = (f32[6,512]{1,0:T(8,128)S(1)}, f32[6,512]{1,0:T(8,128)}, u32[]{:S(2)}) copy-start(f32[6,512]{1,0:T(8,128)} %refs_23_.1) | copy-start | bytes 36868
  0.8 59.0 %copy-start.15 = (f32[2,128]{1,0:T(2,128)S(1)}, f32[2,128]{1,0:T(2,128)}, u32[]{:S(2)}) copy-start(f32[2,128]{1,0:T(2,128)} %refs_10_.1) | copy-start | bytes 3076
  0.8 59.0 %copy-start.16 = (f32[2,128]{1,0:T(2,128)S(1)}, f32[2,128]{1,0:T(2,128)}, u32[]{:S(2)}) copy-start(f32[2,128]{1,0:T(2,128)} %refs_16_.1) | copy-start | bytes 3076
  0.8 59.0 %copy-start.17 = (f32[2,128]{1,0:T(2,128)S(1)}, f32[2,128]{1,0:T(2,128)}, u32[]{:S(2)}) copy-start(f32[2,128]{1,0:T(2,128)} %refs_22_.1) | copy-start | bytes 3076

commit v4 on v3

--- a/solution.py
+++ b/solution.py
@@ -15,6 +15,8 @@
 LANES = 128
 TILE = 256
 ROWS = 512
+DOWN = (4, 4, 4)
+UP = (4, 4, 4)
 
 beta_one = 0.9
 beta_two = 0.999
@@ -85,8 +87,10 @@
     diag = pair + 2 - 4 * h
     a, b = lax.rem(r, 4), r // 4
     edge0 = c * EH
+    near_row = lax.rem(r + 1, R)
     own_lane = pl.ds(pl.multiple_of(t * Q, Q), Q)
     core_lane = pl.ds(pl.multiple_of(c * Q, Q), Q)
+    far_lane = pl.ds(pl.multiple_of(far * Q, Q), Q)
     col_lane = pl.ds(pl.multiple_of(c * LH, LH), LH)
 
     def local(src, dst, sem):
@@ -155,14 +159,34 @@
             return s.wno.at[lane, :]
         return s.bias.at[:, lane]
 
+    groups = (0, 0, 0, 1, 2, 2, 3, 4)
+
     def weight_copy(i, way, who):
         ref = block(i, who, a if way == 1 and i in shared else None)
-        return remote(ref, ref, s.wsend.at[i, way], s.wrecv.at[i, way], (r, (pair, far, pair)[way]))
-
-    def part_copy(i, j, part):
-        ref = block(i, far, part)
+        sent = 10 + i if way == 1 else groups[i] + 5 * (way // 2)
+        return remote(ref, ref, s.wsend.at[sent], s.wrecv.at[8 * way + i], (r, (pair, far, pair)[way]))
+
+    def part_copy(i, j, ref):
+        at = shared.index(i)
         device = (b * 4 + lax.rem(a + j, 4), t)
-        return remote(ref, ref, s.wsend.at[i, 2 + j], s.wrecv.at[i, 2 + j], device)
+        return remote(ref, ref, s.wsend.at[18 + at], s.wrecv.at[24 + at], device)
+
+    def three_parts(i):
+        low, size = (0, 2 * L, L, 0, L, 0)[i], 3 * (L // 4)
+        if i < 3:
+            return s.wei.at[oh, pl.ds(low, size), core_lane]
+        return s.wni.at[pl.ds(low, size), far_lane]
+
+    def weights_sent():
+        for way, tt, th, lane in ((0, t, h, own_lane), (2, far, oh, far_lane)):
+            for k, ref in enumerate(
+                (s.wei.at[th, :, core_lane], block(3, tt), s.wni.at[:, lane], block(6, tt), block(7, tt))
+            ):
+                remote(ref, ref, s.wsend.at[k + 5 * (way // 2)], s.wrecv.at[0], (r, pair)).wait_send()
+        for i in range(8):
+            weight_copy(i, 1, t).wait_send()
+        for i in shared:
+            part_copy(i, 1, three_parts(i)).wait_send()
 
     def weight_send(i, way):
         weight_copy(i, way, t).start()
@@ -173,12 +197,11 @@
     def part_spread(i):
         weight_wait(i, 1)
         for j in (1, 2, 3):
-            part_copy(i, j, a).start()
+            part_copy(i, j, block(i, far, a)).start()
 
     def weight_forward(i):
         if i in shared:
-            for j in (1, 2, 3):
-                part_copy(i, j, lax.rem(a + 4 - j, 4)).wait_recv()
+            part_copy(i, 1, three_parts(i)).wait_recv()
         else:
             weight_wait(i, 1)
         weight_copy(i, 2, far).start()
@@ -216,8 +239,8 @@
         return remote(
             s.served.at[rows_of(to * CAP, CAP)],
             s.slots.at[mine, col_lane],
-            s.ssend.at[k],
-            s.srecv.at[k],
+            s.ssend.at[0],
+            s.srecv.at[0],
             (to, t),
         )
 
@@ -286,7 +309,9 @@
         value = (pre * sig).astype(BF)
         s.hid[which, rows, :] = value
         s.pre[which, rows, :] = sig + (pre * sig) * (1.0 - sig)
-        return mm(value, s.weo[rows_of(which * half, half), :])
+
+    def outer_of(which, k):
+        return mm(s.hid[which, rows_of(k * ROWS, ROWS), :], s.weo[rows_of(which * half, half), :])
 
     for i in (0, 1):
         weight_wait(i, 0)
@@ -294,12 +319,9 @@
     s.g[...] = jnp.zeros_like(s.g)
     weight_forward(0)
 
-    def served_wait(k):
-        source = lax.rem(r + R - k, R)
-        ref = s.slots.at[rows_of(source * CAP, CAP), col_lane]
-        remote(ref, ref, s.ssend.at[k], s.srecv.at[k], (source, t)).wait_recv()
-
-    loop(1, R, served_wait)
+    others = pl.ds(0, (R - 1) * CAP)
+    ref = s.slots.at[others, col_lane]
+    remote(ref, ref, s.ssend.at[0], s.srecv.at[0], (near_row, t)).wait_recv()
     slot_swap = remote(s.slots.at[:, col_lane], s.slots.at[:, col_lane], s.xsend.at[2], s.xrecv.at[2], (r, pair))
     slot_swap.start()
     weight_forward(1)
@@ -321,40 +343,43 @@
         weight_wait(i, 0)
 
     def own_half(k):
-        s.part[rows_of(k * ROWS, ROWS), :] = hidden_of(h, k)
+        hidden_of(h, k)
+        s.part[rows_of(k * ROWS, ROWS), :] = outer_of(h, k)
 
     loop(0, tiles, own_half)
     weight_forward(7)
     for i in (0, 1):
         weight_wait(i, 2)
     first_two(oh)
+    for i in (2, 7):
+        weight_wait(i, 2)
     weight_forward(3)
-    for i in (2, 7, 3):
-        weight_wait(i, 2)
+    loop(0, tiles, lambda k: hidden_of(oh, k))
+    weight_wait(3, 2)
     loads[10].wait()
 
-    def out_copies(k, source, target, which):
-        here = source.at[rows_of(k * ROWS, ROWS)]
-        there = target.at[rows_of(edge0 + k * ROWS, ROWS)]
-        keep = local(here, there, s.osem.at[which, k])
-        send = remote(here, there, s.osend.at[which, k], s.orecv.at[which, k], (r, pair))
+    def out_copies(rows, source, target, which):
+        here = source.at[rows]
+        there = target.at[rows_of(edge0 + rows.start, rows.size)]
+        keep = local(here, there, s.osem.at[which])
+        send = remote(here, there, s.osend.at[which], s.orecv.at[which], (r, pair))
         return keep, send
 
     def out_start(k, source, target, which):
-        keep, send = out_copies(k, source, target, which)
+        keep, send = out_copies(pl.ds(k * ROWS, ROWS), source, target, which)
         keep.start()
         send.start()
 
-    def out_wait(k, source, target, which):
-        keep, send = out_copies(k, source, target, which)
+    def out_wait(source, target, which):
+        keep, send = out_copies(pl.ds(0, EH), source, target, which)
         keep.wait()
         send.wait_send()
-        ref = target.at[rows_of(oc * EH + k * ROWS, ROWS)]
-        remote(ref, ref, s.osend.at[which, k], s.orecv.at[which, k], (r, pair)).wait_recv()
+        ref = target.at[rows_of(oc * EH, EH)]
+        remote(ref, ref, s.osend.at[which], s.orecv.at[which], (r, pair)).wait_recv()
 
     def forward(k):
         rows = rows_of(k * ROWS, ROWS)
-        outer = s.part[rows, :] + hidden_of(oh, k) + s.fv[0:1, :]
+        outer = s.part[rows, :] + outer_of(oh, k) + s.fv[0:1, :]
         normed, inverse = normalize(outer)
         s.normed[rows, :] = normed
         s.inv[rows, :] = inverse
@@ -364,9 +389,13 @@
         s.mk[rows, :] = masked.astype(BF)
 
     loop(0, tiles, forward)
-    s.aggp[...] = mm(s.rhot_t[...], s.mk[...])
-    swap = remote(s.aggp, s.aggr, s.xsend.at[0], s.xrecv.at[0], (r, pair))
-    swap.start()
+    swaps = []
+    for k in (0, 1):
+        at = pl.ds(k * (N // 2), N // 2)
+        s.aggp[at, :] = mm(s.rhot_t[at, :], s.mk[...])
+        swap = remote(s.aggp.at[at], s.aggr.at[at], s.xsend.at[4 * k], s.xrecv.at[4 * k], (r, pair))
+        swap.start()
+        swaps.append(swap)
     for i in (4, 5, 6):
         weight_forward(i)
     weight_wait(5, 0)
@@ -374,7 +403,8 @@
     own_term = mm(s.nf[...], s.wni[0:L, :])
     weight_wait(4, 0)
     weight_wait(4, 2)
-    swap.wait()
+    for swap in swaps:
+        swap.wait()
 
     agg = (s.aggp[...] + s.aggr[...]).astype(BF)
     pre = own_term + mm(agg, s.wni[L : 2 * L, :]) + s.bias[1:2, :]
@@ -410,10 +440,26 @@
 
     chunks = ((base_node, d.size_node), (base_out, d.size_out), (base_in, d.size_in))
 
-    def piece(n, q, bb):
+    down, up_ways = d.down, d.up
+
+    def piece(n, row):
         base, size = chunks[n]
-        count = size // R
-        return rows_of(base + (q * nb + bb) * count, count)
+        m = down[n]
+        return rows_of(base + (lax.rem(row, m) * (R // m) + row // m) * (size // R), size // R)
+
+    v = r
+
+    def placed(row):
+        return row
+
+    def near(m, j):
+        return (v // m) * m + lax.rem(v + j, m)
+
+    def across(m, j):
+        return lax.rem(v // m + j, R // m) * m + lax.rem(v, m)
+
+    def crossed(m, row, j):
+        return lax.rem(row // m + j, R // m) * m + lax.rem(row, m)
 
     def pair_copy(n):
         at = pl.ds(*chunks[n])
@@ -432,102 +478,102 @@
             s.g[c, vec, :] = s.g[c, vec, :].astype(BF).astype(F32)
         s.g[c, at, :] += s.rbp[at, :].astype(F32)
 
-    def a_row(j):
-        return b * 4 + lax.rem(a + j, 4)
-
-    def b_row(j):
-        return lax.rem(b + j, nb) * 4 + a
-
-    def a_copy(n, jj, j, q):
-        at = piece(n, q, lax.rem(b + jj, nb))
-        return remote(s.sb.at[at], s.rba.at[j - 1, at], s.asend.at[n, jj, j], s.arecv.at[n, jj, j], (a_row(j), t))
+    def a_copy(n, jj, j, target):
+        at = piece(n, crossed(down[n], target, jj))
+        return remote(
+            s.sb.at[at], s.rba.at[j - 1, at], s.asend.at[n], s.arecv.at[n, jj], (placed(near(down[n], j)), t)
+        )
 
     def b_slot(n):
         base, size = chunks[n]
         return pl.ds(base // R, size // R)
 
-    def b_copy(n, jj, bb):
+    def b_copy(n, jj, row):
         return remote(
-            s.sb.at[piece(n, a, bb)],
+            s.sb.at[piece(n, row)],
             s.rbb.at[jj - 1, b_slot(n)],
-            s.bsend.at[n, jj],
-            s.brecv.at[n, jj],
-            (b_row(jj), t),
+            s.bsend.at[n, jj - 1],
+            s.brecv.at[n, jj - 1],
+            (placed(across(down[n], jj)), t),
         )
-
-    order = (*range(1, nb), 0)
 
     def a_send(n):
         at = pl.ds(*chunks[n])
         s.sb[at, :] = s.g[c, at, :].astype(BF)
-        for jj in order:
-            for j in (1, 2, 3):
-                a_copy(n, jj, j, lax.rem(a + j, 4)).start()
+        for jj in (*range(1, R // down[n]), 0):
+            for j in range(1, down[n]):
+                a_copy(n, jj, j, near(down[n], j)).start()
 
     def a_sum(n, jj):
-        at = piece(n, a, lax.rem(b + jj, nb))
-        for j in (1, 2, 3):
-            a_copy(n, jj, j, a).wait_recv()
-        return s.g[c, at, :] + (
-            s.rba[0, at, :].astype(F32) + s.rba[1, at, :].astype(F32) + s.rba[2, at, :].astype(F32)
-        )
+        at = piece(n, across(down[n], jj))
+        total = s.g[c, at, :]
+        ref = s.rba.at[pl.ds(0, down[n] - 1), at]
+        remote(ref, ref, s.asend.at[n], s.arecv.at[n, jj], (near_row, t)).wait_recv()
+        for j in range(1, down[n]):
+            total = total + s.rba[j - 1, at, :].astype(F32)
+        return total
 
     def b_send(n):
-        for jj in range(1, nb):
-            at = piece(n, a, lax.rem(b + jj, nb))
-            s.sb[at, :] = a_sum(n, jj).astype(BF)
-            b_copy(n, jj, lax.rem(b + jj, nb)).start()
-
-    def to_b(n, jj):
-        ref = s.fin_o.at[piece(n, a, b)]
-        return remote(ref, ref, s.fbsend.at[n, jj], s.fbrecv.at[n, jj], (b_row(jj), t))
-
-    def to_a(n, jj, j):
-        ref = s.fin_o.at[piece(n, a, lax.rem(b + nb - jj, nb))]
-        return remote(ref, ref, s.fasend.at[n, jj, j], s.farecv.at[n, jj, j], (a_row(j), t))
+        for jj in range(1, R // down[n]):
+            row = across(down[n], jj)
+            s.sb[piece(n, row), :] = a_sum(n, jj).astype(BF)
+            b_copy(n, jj, row).start()
+
+    def to_b(n, jj, row):
+        ref = s.fin_o.at[piece(n, row)]
+        return remote(ref, ref, s.fbsend.at[n, jj - 1], s.fbrecv.at[n, jj - 1], (placed(across(up_ways[n], jj)), t))
+
+    def to_a(n, jj, j, row):
+        ref = s.fin_o.at[piece(n, row)]
+        return remote(ref, ref, s.fasend.at[n], s.farecv.at[n], (placed(near(up_ways[n], j)), t))
 
     def b_finish(n):
         total = a_sum(n, 0)
-        at = piece(n, a, b)
-        for jj in range(1, nb):
-            b_copy(n, jj, b).wait_recv()
+        at = piece(n, v)
+        for jj in range(1, R // down[n]):
+            b_copy(n, jj, v).wait_recv()
             total = total + s.rbb[jj - 1, b_slot(n), :].astype(F32)
         final = total.astype(BF)
         s.fin_o[at, :] = final
-        for jj in range(1, nb):
-            to_b(n, jj).start()
-        for j in (1, 2, 3):
-            to_a(n, 0, j).start()
+        for jj in range(1, R // up_ways[n]):
+            to_b(n, jj, v).start()
+        for j in range(1, up_ways[n]):
+            to_a(n, 0, j, v).start()
         final = final.astype(F32)
         squares = final * final
         count = squares.shape[0]
         if n == 2:
-            index = lax.broadcasted_iota(jnp.int32, (count, LANES), 0) + (base_in + (a * nb + b) * count)
+            m = down[n]
+            low = base_in + (lax.rem(v, m) * (R // m) + v // m) * count
+            index = lax.broadcasted_iota(jnp.int32, (count, LANES), 0) + low
             copied = jnp.logical_and(index >= base_vec, index < base_vec + 24)
             squares = jnp.where(copied, 0.25 * squares, squares)
         s.norm_a[mine8, :] += jnp.sum(squares.reshape(count // 8, 8, LANES), axis=0)
 
     def spread(n):
-        for jj in range(1, nb):
-            ref = s.fin_o.at[piece(n, a, lax.rem(b + nb - jj, nb))]
-            remote(ref, ref, s.fbsend.at[n, jj], s.fbrecv.at[n, jj], (b_row(jj), t)).wait_recv()
-            for j in (1, 2, 3):
-                to_a(n, jj, j).start()
+        m = up_ways[n]
+        for jj in range(1, R // m):
+            row = crossed(m, v, R // m - jj)
+            to_b(n, jj, row).wait_recv()
+            for j in range(1, m):
+                to_a(n, jj, j, row).start()
+
+    def all_but_own(n, m):
+        base, size = chunks[n]
+        return pl.ds(base, (R - R // m) * (size // R))
 
     def spread_wait(n):
-        for jj in range(nb):
-            for j in (1, 2, 3):
-                ref = s.fin_o.at[piece(n, lax.rem(a + 4 - j, 4), lax.rem(b + nb - jj, nb))]
-                remote(ref, ref, s.fasend.at[n, jj, j], s.farecv.at[n, jj, j], (a_row(j), t)).wait_recv()
+        ref = s.fin_o.at[all_but_own(n, up_ways[n])]
+        remote(ref, ref, s.fasend.at[n], s.farecv.at[n], (near_row, t)).wait()
 
     def sums_done(n):
-        for jj in range(nb):
-            for j in (1, 2, 3):
-                a_copy(n, jj, j, lax.rem(a + j, 4)).wait_send()
-                to_a(n, jj, j).wait_send()
-        for jj in range(1, nb):
-            b_copy(n, jj, lax.rem(b + jj, nb)).wait_send()
-            to_b(n, jj).wait_send()
+        m = down[n]
+        ref = s.sb.at[all_but_own(n, m)]
+        remote(ref, ref, s.asend.at[n], s.arecv.at[n, 0], (near_row, t)).wait_send()
+        for jj in range(1, R // m):
+            b_copy(n, jj, across(m, jj)).wait_send()
+        for jj in range(1, R // up_ways[n]):
+            to_b(n, jj, v).wait_send()
 
     mine8 = rows_of(r * 8, 8, 8)
     s.norm_a[mine8, :] = jnp.zeros((8, LANES), F32)
@@ -651,12 +697,13 @@
         rows = rows_of(k * TILE, TILE)
         s.served[rows, :] = (slot_grad(c, rows) + s.torecv[rows, :].astype(F32)).astype(BF)
 
-    loop(1, R, lambda k: served_copy(k).wait_send())
+    ref = s.served.at[others]
+    remote(ref, ref, s.ssend.at[0], s.srecv.at[0], (near_row, t)).wait_send()
     loop(0, slot_tiles, slot_own)
 
     def back_copy(k):
         to = lax.rem(r + k, R)
-        return remote(s.served.at[rows_of(to * CAP, CAP)], s.ret.at[mine], s.ksend.at[k], s.krecv.at[k], (to, t))
+        return remote(s.served.at[rows_of(to * CAP, CAP)], s.ret.at[mine], s.ksend.at[0], s.krecv.at[0], (to, t))
 
     loop(1, R, lambda k: back_copy(k).start())
     b_finish(1)
@@ -666,7 +713,7 @@
     def norm_row(k):
         to = lax.rem(r + k, R)
         ref = s.norm_a.at[mine8]
-        return remote(ref, ref, s.qsend.at[k], s.qrecv.at[k], (to, t))
+        return remote(ref, ref, s.qsend.at[0], s.qrecv.at[0], (to, t))
 
     loop(1, R, lambda k: norm_row(k).start())
     s.ret[mine, :] = s.served[mine, :]
@@ -674,26 +721,16 @@
     for n in (1, 2):
         spread(n)
 
-    def norm_row_wait(k):
-        source = lax.rem(r + R - k, R)
-        ref = s.norm_a.at[rows_of(source * 8, 8, 8)]
-        remote(ref, ref, s.qsend.at[k], s.qrecv.at[k], (source, t)).wait_recv()
-        norm_row(k).wait_send()
-
-    loop(1, R, norm_row_wait)
+    ref = s.norm_a.at[pl.ds(0, (R - 1) * 8)]
+    remote(ref, ref, s.qsend.at[0], s.qrecv.at[0], (near_row, t)).wait()
     own_rows = rows_of(t * 8, 8, 8)
     s.nsq[own_rows, :] = jnp.sum(s.norm_a[...].reshape(R, 8, LANES), axis=0)
-    for k, peer in enumerate((pair, far, diag)):
+    for peer in (pair, far, diag):
         ref = s.nsq.at[own_rows]
-        remote(ref, ref, s.tsem.at[0, k], s.tsem.at[1, k], (r, peer)).start()
-
-    def back_wait(k):
-        source = lax.rem(r + R - k, R)
-        ref = s.ret.at[rows_of(source * CAP, CAP)]
-        remote(ref, ref, s.ksend.at[k], s.krecv.at[k], (source, t)).wait_recv()
-        back_copy(k).wait_send()
-
-    loop(1, R, back_wait)
+        remote(ref, ref, s.tsem.at[0], s.tsem.at[1], (r, peer)).start()
+
+    ref = s.ret.at[others]
+    remote(ref, ref, s.ksend.at[0], s.krecv.at[0], (near_row, t)).wait()
 
     def gathered(k):
         lanes = pl.ds(pl.multiple_of(k * TILE, TILE), TILE)
@@ -708,28 +745,18 @@
 
     for n in (0, 1, 2):
         spread_wait(n)
-    for k, peer in enumerate((pair, far, diag)):
-        ref = s.nsq.at[rows_of(peer * 8, 8, 8)]
-        remote(ref, ref, s.tsem.at[0, k], s.tsem.at[1, k], (r, peer)).wait()
+    ref = s.nsq.at[pl.ds(0, 24)]
+    remote(ref, ref, s.tsem.at[0], s.tsem.at[1], (r, pair)).wait()
     total = s.nsq[0:8, :] + s.nsq[8:16, :] + s.nsq[16:24, :] + s.nsq[24:32, :]
     s.norm_o[...] = jnp.sqrt(jnp.full((8, LANES), jnp.sum(total), F32))
     for n in (0, 1, 2):
         sums_done(n)
-    for i in range(8):
-        weight_copy(i, 0, t).wait_send()
-        weight_copy(i, 1, t).wait_send()
-        weight_copy(i, 2, far).wait_send()
-        if i in shared:
-            for j in (1, 2, 3):
-                part_copy(i, j, a).wait_send()
+    weights_sent()
     slot_swap.wait_send()
     grad_swap.wait_send()
 
-    def finish(k):
-        out_wait(k, s.ne, s.ne_h, 0)
-        out_wait(k, s.eg, s.eg_h, 1)
-
-    loop(0, tiles, finish)
+    out_wait(s.ne, s.ne_h, 0)
+    out_wait(s.eg, s.eg_h, 1)
     nn_copy.wait()
     ng_keep.wait()
     ng_send.wait_send()
@@ -818,7 +845,7 @@
     d.H = d.Q * lax.axis_size("tp")
     d.CAP = serve_rows.shape[1]
     R, N, E, L, H, Q = d.R, d.N, d.E, d.L, d.H, d.Q
-    EH, S, nb = E // 2, R * d.CAP, R // 4
+    EH, S = E // 2, R * d.CAP
     tiles = EH // ROWS
 
     def padded(count):
@@ -827,6 +854,8 @@
     d.size_node, d.size_out, d.size_in = padded(3 * L), padded(L), padded(3 * L + 32)
     d.base_node, d.base_out, d.base_in = 0, d.size_node, d.size_node + d.size_out
     G = d.size_node + d.size_out + d.size_in
+    d.down, d.up = DOWN, UP
+    most = R // min(*DOWN, *UP)
     vmem_spec = pl.BlockSpec(memory_space=pltpu.VMEM)
     inputs = dict(
         nf_h=node_feats,
@@ -917,36 +946,36 @@
         sb=pltpu.VMEM((G, Q), BF),
         rbp=pltpu.VMEM((G, Q), BF),
         rba=pltpu.VMEM((3, G, Q), BF),
-        rbb=pltpu.VMEM((nb - 1, G // R, Q), BF),
+        rbb=pltpu.VMEM((most - 1, G // R, Q), BF),
         vsum=pltpu.VMEM((8, L), F32),
         norm_a=pltpu.VMEM((8 * R, LANES), F32),
         nsq=pltpu.VMEM((32, LANES), F32),
         lsem=dma((16,)),
-        wsend=dma((8, 6)),
-        wrecv=dma((8, 6)),
-        ssend=dma((R,)),
-        srecv=dma((R,)),
-        ksend=dma((R,)),
-        krecv=dma((R,)),
-        qsend=dma((R,)),
-        qrecv=dma((R,)),
-        osem=dma((2, tiles)),
-        osend=dma((2, tiles)),
-        orecv=dma((2, tiles)),
-        xsend=dma((4,)),
-        xrecv=dma((4,)),
+        wsend=dma((22,)),
+        wrecv=dma((28,)),
+        ssend=dma((1,)),
+        srecv=dma((1,)),
+        ksend=dma((1,)),
+        krecv=dma((1,)),
+        qsend=dma((1,)),
+        qrecv=dma((1,)),
+        osem=dma((2,)),
+        osend=dma((2,)),
+        orecv=dma((2,)),
+        xsend=dma((5,)),
+        xrecv=dma((5,)),
         nsem=dma((2,)),
         psend=dma((3,)),
         precv=dma((3,)),
-        asend=dma((3, nb, 4)),
-        arecv=dma((3, nb, 4)),
-        bsend=dma((3, nb)),
-        brecv=dma((3, nb)),
-        fbsend=dma((3, nb)),
-        fbrecv=dma((3, nb)),
-        fasend=dma((3, nb, 4)),
-        farecv=dma((3, nb, 4)),
-        tsem=dma((2, 3)),
+        asend=dma((3,)),
+        arecv=dma((3, most)),
+        bsend=dma((3, most - 1)),
+        brecv=dma((3, most - 1)),
+        fbsend=dma((3, most - 1)),
+        fbrecv=dma((3, most - 1)),
+        fasend=dma((3,)),
+        farecv=dma((3,)),
+        tsem=dma((2,)),
     )
     names = (*inputs, *outputs, *scratch)
     limit = 6 * 1024 * 1024

time: 65.5 us -> 63 us (0.962)
  Pallas kernels: 64.2 us -> 61.6 us
    pallas_call x1, Pallas kernels: 58.8 us -> 56.3 us  [device_step(): pl.pallas_call(functools.partial(layer, names, d), out_shape=[shape for s...]
where the time goes in v4:
time: 63 us; the launch traced here: 62.8 us
  Pallas kernels  61.6 us (98%)
  between operations  1.12 us (2%)
    pallas_call x1, Pallas kernels, device_step(): pl.pallas_call(functools.partial(layer, names, d), out_shape=[shape for s...  56.3 us
    pallas_call x1, Pallas kernels, device_step(): pl.pallas_call(functools.partial(update, names, d), out_shape=[*(jax.Shap...  5.36 us

profile of v4, /device:TPU:0, one launch (start us, length us, event | category | flops | bytes accessed | tf_op | source)
XLA Modules:
  0.0 62.8 jit_solution(6569107566260927978)
XLA Ops:
  0.7 0.0 copy-start
  0.7 0.0 copy-start.1
  0.7 0.0 copy-start.2
  0.7 0.0 copy-start.3
  0.7 0.0 copy-start.4
  0.7 0.0 copy-start.5
  0.7 0.0 copy-start.6
  0.7 0.0 copy-start.7
  0.7 0.0 copy-start.8
  0.8 0.0 copy-start.9
  0.8 0.0 copy-start.10
  0.8 0.0 copy-start.11
  0.8 0.0 copy-start.12
  0.8 0.0 copy-start.13
  0.8 0.0 copy-start.14
  0.8 0.0 copy-start.15
  0.8 0.0 copy-start.16
  0.8 0.0 copy-start.17
  0.8 56.3 %shard_map.425 = (bf16[256,512]{1,0:T(8,128)(2,1)S(1)}, bf16[2048,512]{1,0:T(8,128)(2,1)S(1)}, bf16[256,512]{1,0:T(8,128)(2,1)S(1)}, bf16[2048,512]{1,0:T(8,128)...) custom-call(bf16[256,512]{1,0:T(8,128)(2,1)} %refs_0_.1, bf16[2048,512]{1,0:T(8,128)(2,1)} %refs_1_.1, ...), custom_call_target="tpu_custom_call" | custom-call | tf_op jit(solution)/shard_map/pallas_call | solution.py:986
  57.1 0.0 copy-done
  57.1 0.0 copy-done.1
  57.1 0.0 copy-done.2
  57.2 0.0 copy-done.3
  57.2 0.0 copy-done.4
  57.2 0.0 copy-done.5
  57.2 0.0 copy-done.6
  57.2 0.0 copy-done.7
  57.2 0.0 copy-done.8
  57.2 0.0 copy-done.9
  57.2 0.0 copy-done.10
  57.2 0.0 copy-done.11
  57.2 0.0 copy-done.12
  57.3 0.0 copy-done.13
  57.3 0.0 copy-done.14
  57.3 0.0 copy-done.15
  57.3 0.0 copy-done.16
  57.3 0.0 copy-done.17
  57.3 5.4 %shard_map.426 = (bf16[256,512]{1,0:T(8,128)(2,1)}, bf16[2048,512]{1,0:T(8,128)(2,1)}, bf16[256,512]{1,0:T(8,128)(2,1)}, bf16[2048,512]{1,0:T(8,128)(2,1)}, f32[...) custom-call(bf16[3712,128]{1,0:T(8,128)(2,1)S(1)} %get-tuple-element, ...), custom_call_target="tpu_custom_call" | custom-call | tf_op jit(solution)/shard_map/pallas_call | solution.py:1010
Async XLA Ops:
  0.7 56.5 %copy-start = (f32[1536,128]{1,0:T(8,128)S(1)}, f32[1536,128]{1,0:T(8,128)}, u32[]{:S(2)}) copy-start(f32[1536,128]{1,0:T(8,128)} %refs_6_.3) | copy-start | bytes 2359300
  0.7 56.5 %copy-start.1 = (f32[1024,128]{1,0:T(8,128)S(1)}, f32[1024,128]{1,0:T(8,128)}, u32[]{:S(2)}) copy-start(f32[1024,128]{1,0:T(8,128)} %refs_8_.3) | copy-start | bytes 1572868
  0.7 56.5 %copy-start.2 = (f32[128,512]{1,0:T(8,128)S(1)}, f32[128,512]{1,0:T(8,128)}, u32[]{:S(2)}) copy-start(f32[128,512]{1,0:T(8,128)} %refs_7_.3) | copy-start | bytes 786436
  0.7 56.5 %copy-start.3 = (f32[128,512]{1,0:T(8,128)S(1)}, f32[128,512]{1,0:T(8,128)}, u32[]{:S(2)}) copy-start(f32[128,512]{1,0:T(8,128)} %refs_9_.3) | copy-start | bytes 786436
  0.7 56.5 %copy-start.4 = (f32[1536,128]{1,0:T(8,128)S(1)}, f32[1536,128]{1,0:T(8,128)}, u32[]{:S(2)}) copy-start(f32[1536,128]{1,0:T(8,128)} %refs_12_.1) | copy-start | bytes 2359300
  0.7 56.5 %copy-start.5 = (f32[1536,128]{1,0:T(8,128)S(1)}, f32[1536,128]{1,0:T(8,128)}, u32[]{:S(2)}) copy-start(f32[1536,128]{1,0:T(8,128)} %refs_18_.1) | copy-start | bytes 2359300
  0.7 56.5 %copy-start.6 = (f32[1024,128]{1,0:T(8,128)S(1)}, f32[1024,128]{1,0:T(8,128)}, u32[]{:S(2)}) copy-start(f32[1024,128]{1,0:T(8,128)} %refs_14_.1) | copy-start | bytes 1572868
  0.7 56.5 %copy-start.7 = (f32[1024,128]{1,0:T(8,128)S(1)}, f32[1024,128]{1,0:T(8,128)}, u32[]{:S(2)}) copy-start(f32[1024,128]{1,0:T(8,128)} %refs_20_.1) | copy-start | bytes 1572868
  0.7 56.5 %copy-start.8 = (f32[128,512]{1,0:T(8,128)S(1)}, f32[128,512]{1,0:T(8,128)}, u32[]{:S(2)}) copy-start(f32[128,512]{1,0:T(8,128)} %refs_13_.1) | copy-start | bytes 786436
  0.8 56.5 %copy-start.9 = (f32[128,512]{1,0:T(8,128)S(1)}, f32[128,512]{1,0:T(8,128)}, u32[]{:S(2)}) copy-start(f32[128,512]{1,0:T(8,128)} %refs_15_.3) | copy-start | bytes 786436
  0.8 56.5 %copy-start.10 = (f32[128,512]{1,0:T(8,128)S(1)}, f32[128,512]{1,0:T(8,128)}, u32[]{:S(2)}) copy-start(f32[128,512]{1,0:T(8,128)} %refs_19_.1) | copy-start | bytes 786436
  0.8 56.5 %copy-start.11 = (f32[128,512]{1,0:T(8,128)S(1)}, f32[128,512]{1,0:T(8,128)}, u32[]{:S(2)}) copy-start(f32[128,512]{1,0:T(8,128)} %refs_21_.1) | copy-start | bytes 786436
  0.8 56.5 %copy-start.12 = (f32[6,512]{1,0:T(8,128)S(1)}, f32[6,512]{1,0:T(8,128)}, u32[]{:S(2)}) copy-start(f32[6,512]{1,0:T(8,128)} %refs_11_.1) | copy-start | bytes 36868
  0.8 56.5 %copy-start.13 = (f32[6,512]{1,0:T(8,128)S(1)}, f32[6,512]{1,0:T(8,128)}, u32[]{:S(2)}) copy-start(f32[6,512]{1,0:T(8,128)} %refs_17_.1) | copy-start | bytes 36868
  0.8 56.5 %copy-start.14 = (f32[6,512]{1,0:T(8,128)S(1)}, f32[6,512]{1,0:T(8,128)}, u32[]{:S(2)}) copy-start(f32[6,512]{1,0:T(8,128)} %refs_23_.1) | copy-start | bytes 36868
  0.8 56.5 %copy-start.15 = (f32[2,128]{1,0:T(2,128)S(1)}, f32[2,128]{1,0:T(2,128)}, u32[]{:S(2)}) copy-start(f32[2,128]{1,0:T(2,128)} %refs_10_.1) | copy-start | bytes 3076
  0.8 56.5 %copy-start.16 = (f32[2,128]{1,0:T(2,128)S(1)}, f32[2,128]{1,0:T(2,128)}, u32[]{:S(2)}) copy-start(f32[2,128]{1,0:T(2,128)} %refs_16_.1) | copy-start | bytes 3076
  0.8 56.5 %copy-start.17 = (f32[2,128]{1,0:T(2,128)S(1)}, f32[2,128]{1,0:T(2,128)}, u32[]{:S(2)}) copy-start(f32[2,128]{1,0:T(2,128)} %refs_22_.1) | copy-start | bytes 3076

commit v5 on v4

--- a/solution.py
+++ b/solution.py
@@ -76,7 +76,7 @@
 def layer(names, d, *refs):
     s = types.SimpleNamespace(**dict(zip(names, refs, strict=True)))
     R, N, E, L, H, Q, CAP = d.R, d.N, d.E, d.L, d.H, d.Q, d.CAP
-    EH, S, half, LH = E // 2, R * CAP, H // 2, L // 2
+    EH, S, half, LH, LQ = E // 2, R * CAP, H // 2, L // 2, L // 4
     tiles, slot_tiles, nb = EH // ROWS, S // TILE, R // 4
     r = lax.axis_index("rows")
     t = lax.axis_index("tp")
@@ -316,7 +316,14 @@
     for i in (0, 1):
         weight_wait(i, 0)
     first_two(h)
-    s.g[...] = jnp.zeros_like(s.g)
+    for low, high in (
+        (d.base_node + 3 * L, d.base_out),
+        (d.base_out + L, d.base_in),
+        (d.base_in + L, d.base_in + 2 * L),
+        (d.base_in + 3 * L, d.base_in + d.size_in),
+    ):
+        if high > low:
+            s.g[:, low:high, :] = jnp.zeros((2, high - low, Q), F32)
     weight_forward(0)
 
     others = pl.ds(0, (R - 1) * CAP)
@@ -665,12 +672,17 @@
     b_send(1)
     b_finish(0)
 
+    def quarter(hh, cc):
+        return pl.ds(pl.multiple_of(cc * LH + hh * LQ, LQ), LQ)
+
+    quarter_rows = rows_of(c * LH + h * LQ, LQ)
+
     def slot_grad(which, rows):
-        at = rows_of(L + which * LH, LH)
+        at = rows_of(L + which * LH + h * LQ, LQ)
         return nt(s.ss[0, rows, :].astype(BF), s.wei[0, at, :]) + nt(s.ss[1, rows, :].astype(BF), s.wei[1, at, :])
 
     def recv_grad(which):
-        at = rows_of(2 * L + which * LH, LH)
+        at = rows_of(2 * L + which * LH + h * LQ, LQ)
         return nt(s.rs[0].astype(BF), s.wei[0, at, :]) + nt(s.rs[1].astype(BF), s.wei[1, at, :])
 
     def slot_other(k):
@@ -683,11 +695,11 @@
     grad_swap.start()
     b_send(2)
     s.ntp[...] = (
-        s.ncot[:, col_lane].astype(F32)
-        + (nt(s.nsl[0], s.wni[rows_of(c * LH, LH), 0:Q]) + nt(s.nsl[1], s.wni[rows_of(c * LH, LH), Q : 2 * Q]))
+        s.ncot[:, quarter(h, c)].astype(F32)
+        + (nt(s.nsl[0], s.wni[quarter_rows, 0:Q]) + nt(s.nsl[1], s.wni[quarter_rows, Q : 2 * Q]))
         + (
-            nt(s.nsl[2], s.wni[rows_of(c * LH, LH), 2 * Q : 3 * Q])
-            + nt(s.nsl[3], s.wni[rows_of(c * LH, LH), 3 * Q : 4 * Q])
+            nt(s.nsl[2], s.wni[quarter_rows, 2 * Q : 3 * Q])
+            + nt(s.nsl[3], s.wni[quarter_rows, 3 * Q : 4 * Q])
         )
         + recv_grad(c)
     )
@@ -695,7 +707,7 @@
 
     def slot_own(k):
         rows = rows_of(k * TILE, TILE)
-        s.served[rows, :] = (slot_grad(c, rows) + s.torecv[rows, :].astype(F32)).astype(BF)
+        s.back[rows, :] = (slot_grad(c, rows) + s.torecv[rows, :].astype(F32)).astype(BF)
 
     ref = s.served.at[others]
     remote(ref, ref, s.ssend.at[0], s.srecv.at[0], (near_row, t)).wait_send()
@@ -703,7 +715,7 @@
 
     def back_copy(k):
         to = lax.rem(r + k, R)
-        return remote(s.served.at[rows_of(to * CAP, CAP)], s.ret.at[mine], s.ksend.at[0], s.krecv.at[0], (to, t))
+        return remote(s.back.at[rows_of(to * CAP, CAP)], s.ret.at[mine], s.ksend.at[0], s.krecv.at[0], (to, t))
 
     loop(1, R, lambda k: back_copy(k).start())
     b_finish(1)
@@ -716,7 +728,7 @@
         return remote(ref, ref, s.qsend.at[0], s.qrecv.at[0], (to, t))
 
     loop(1, R, lambda k: norm_row(k).start())
-    s.ret[mine, :] = s.served[mine, :]
+    s.ret[mine, :] = s.back[mine, :]
     s.ntp[...] += s.torecv[S : S + N, :].astype(F32)
     for n in (1, 2):
         spread(n)
@@ -738,10 +750,12 @@
 
     loop(0, slot_tiles, gathered)
     s.ng[...] = s.ntp[...].astype(BF)
-    ng_keep = local(s.ng, s.ng_h.at[:, col_lane], s.nsem.at[1])
+    ng_at = s.ng_h.at[:, quarter(h, c)]
+    ng_keep = local(s.ng, ng_at, s.nsem.at[1])
     ng_keep.start()
-    ng_send = remote(s.ng, s.ng_h.at[:, col_lane], s.xsend.at[3], s.xrecv.at[3], (r, pair))
-    ng_send.start()
+    takers = ((3, pair, h, oc), (5, far, oh, c), (6, diag, oh, oc))
+    for k, peer, _, _ in takers:
+        remote(s.ng, ng_at, s.xsend.at[k], s.xrecv.at[k], (r, peer)).start()
 
     for n in (0, 1, 2):
         spread_wait(n)
@@ -759,9 +773,8 @@
     out_wait(s.eg, s.eg_h, 1)
     nn_copy.wait()
     ng_keep.wait()
-    ng_send.wait_send()
-    ref = s.ng_h.at[:, other_lane]
-    remote(ref, ref, s.xsend.at[3], s.xrecv.at[3], (r, pair)).wait_recv()
+    for k, peer, hh, cc in takers:
+        remote(s.ng, s.ng_h.at[:, quarter(hh, cc)], s.xsend.at[k], s.xrecv.at[k], (r, peer)).wait()
 
 
 def adam(weight, first, second, gradient, factor, rate):
@@ -911,7 +924,8 @@
         serve_t=pltpu.VMEM((N, S), BF),
         served=pltpu.VMEM((S, L // 2), BF),
         slots=pltpu.VMEM((S, L), BF),
-        ret=pltpu.VMEM((S, L // 2), BF),
+        ret=pltpu.VMEM((S, L // 4), BF),
+        back=pltpu.VMEM((S, L // 4), BF),
         rcol=pltpu.VMEM((EH, 1), F32),
         scol=pltpu.VMEM((EH, 1), F32),
         mcol=pltpu.VMEM((EH, 1), F32),
@@ -931,17 +945,17 @@
         aggp=pltpu.VMEM((N, L), F32),
         aggr=pltpu.VMEM((N, L), F32),
         nn=pltpu.VMEM((N, L), BF),
-        ng=pltpu.VMEM((N, L // 2), BF),
+        ng=pltpu.VMEM((N, L // 4), BF),
         agh=pltpu.VMEM((N, L), BF),
-        ntp=pltpu.VMEM((N, L // 2), F32),
+        ntp=pltpu.VMEM((N, L // 4), F32),
         nsl=pltpu.VMEM((H // Q, N, Q), BF),
         nhid=pltpu.VMEM((H // Q, N, Q), BF),
         og=pltpu.VMEM((EH, L), BF),
         sl=pltpu.VMEM((2, EH, H // 2), BF),
         rs=pltpu.VMEM((2, N, H // 2), F32),
         ss=pltpu.VMEM((2, S, H // 2), F32),
-        tosend=pltpu.VMEM((S + N, L // 2), BF),
-        torecv=pltpu.VMEM((S + N, L // 2), BF),
+        tosend=pltpu.VMEM((S + N, L // 4), BF),
+        torecv=pltpu.VMEM((S + N, L // 4), BF),
         g=pltpu.VMEM((2, G, Q), F32),
         sb=pltpu.VMEM((G, Q), BF),
         rbp=pltpu.VMEM((G, Q), BF),
@@ -962,8 +976,8 @@
         osem=dma((2,)),
         osend=dma((2,)),
         orecv=dma((2,)),
-        xsend=dma((5,)),
-        xrecv=dma((5,)),
+        xsend=dma((7,)),
+        xrecv=dma((7,)),
         nsem=dma((2,)),
         psend=dma((3,)),
         precv=dma((3,)),

time: 63 us -> 62.7 us (level)
  no operation moved by 1% of the time
where the time goes in v5:
time: 62.7 us; the launch traced here: 62.5 us
  Pallas kernels  61.3 us (98%)
  between operations  1.12 us (2%)
    pallas_call x1, Pallas kernels, device_step(): pl.pallas_call(functools.partial(layer, names, d), out_shape=[shape for s...  55.9 us
    pallas_call x1, Pallas kernels, device_step(): pl.pallas_call(functools.partial(update, names, d), out_shape=[*(jax.Shap...  5.36 us

profile of v5, /device:TPU:0, one launch (start us, length us, event | category | flops | bytes accessed | tf_op | source)
XLA Modules:
  0.0 62.5 jit_solution(10195117178108598313)
XLA Ops:
  0.7 0.0 copy-start
  0.7 0.0 copy-start.1
  0.7 0.0 copy-start.2
  0.7 0.0 copy-start.3
  0.7 0.0 copy-start.4
  0.7 0.0 copy-start.5
  0.7 0.0 copy-start.6
  0.7 0.0 copy-start.7
  0.7 0.0 copy-start.8
  0.8 0.0 copy-start.9
  0.8 0.0 copy-start.10
  0.8 0.0 copy-start.11
  0.8 0.0 copy-start.12
  0.8 0.0 copy-start.13
  0.8 0.0 copy-start.14
  0.8 0.0 copy-start.15
  0.8 0.0 copy-start.16
  0.8 0.0 copy-start.17
  0.8 55.9 %shard_map.425 = (bf16[256,512]{1,0:T(8,128)(2,1)S(1)}, bf16[2048,512]{1,0:T(8,128)(2,1)S(1)}, bf16[256,512]{1,0:T(8,128)(2,1)S(1)}, bf16[2048,512]{1,0:T(8,128)...) custom-call(bf16[256,512]{1,0:T(8,128)(2,1)} %refs_0_.1, bf16[2048,512]{1,0:T(8,128)(2,1)} %refs_1_.1, ...), custom_call_target="tpu_custom_call" | custom-call | tf_op jit(solution)/shard_map/pallas_call | solution.py:1000
  56.8 0.0 copy-done
  56.8 0.0 copy-done.1
  56.8 0.0 copy-done.2
  56.8 0.0 copy-done.3
  56.8 0.0 copy-done.4
  56.8 0.0 copy-done.5
  56.8 0.0 copy-done.6
  56.9 0.0 copy-done.7
  56.9 0.0 copy-done.8
  56.9 0.0 copy-done.9
  56.9 0.0 copy-done.10
  56.9 0.0 copy-done.11
  56.9 0.0 copy-done.12
  56.9 0.0 copy-done.13
  56.9 0.0 copy-done.14
  56.9 0.0 copy-done.15
  56.9 0.0 copy-done.16
  57.0 0.0 copy-done.17
  57.0 5.4 %shard_map.426 = (bf16[256,512]{1,0:T(8,128)(2,1)}, bf16[2048,512]{1,0:T(8,128)(2,1)}, bf16[256,512]{1,0:T(8,128)(2,1)}, bf16[2048,512]{1,0:T(8,128)(2,1)}, f32[...) custom-call(bf16[3712,128]{1,0:T(8,128)(2,1)S(1)} %get-tuple-element, ...), custom_call_target="tpu_custom_call" | custom-call | tf_op jit(solution)/shard_map/pallas_call | solution.py:1024
Async XLA Ops:
  0.7 56.1 %copy-start = (f32[1536,128]{1,0:T(8,128)S(1)}, f32[1536,128]{1,0:T(8,128)}, u32[]{:S(2)}) copy-start(f32[1536,128]{1,0:T(8,128)} %refs_6_.3) | copy-start | bytes 2359300
  0.7 56.1 %copy-start.1 = (f32[1024,128]{1,0:T(8,128)S(1)}, f32[1024,128]{1,0:T(8,128)}, u32[]{:S(2)}) copy-start(f32[1024,128]{1,0:T(8,128)} %refs_8_.3) | copy-start | bytes 1572868
  0.7 56.1 %copy-start.2 = (f32[128,512]{1,0:T(8,128)S(1)}, f32[128,512]{1,0:T(8,128)}, u32[]{:S(2)}) copy-start(f32[128,512]{1,0:T(8,128)} %refs_7_.3) | copy-start | bytes 786436
  0.7 56.1 %copy-start.3 = (f32[128,512]{1,0:T(8,128)S(1)}, f32[128,512]{1,0:T(8,128)}, u32[]{:S(2)}) copy-start(f32[128,512]{1,0:T(8,128)} %refs_9_.3) | copy-start | bytes 786436
  0.7 56.1 %copy-start.4 = (f32[1536,128]{1,0:T(8,128)S(1)}, f32[1536,128]{1,0:T(8,128)}, u32[]{:S(2)}) copy-start(f32[1536,128]{1,0:T(8,128)} %refs_12_.1) | copy-start | bytes 2359300
  0.7 56.1 %copy-start.5 = (f32[1536,128]{1,0:T(8,128)S(1)}, f32[1536,128]{1,0:T(8,128)}, u32[]{:S(2)}) copy-start(f32[1536,128]{1,0:T(8,128)} %refs_18_.1) | copy-start | bytes 2359300
  0.7 56.1 %copy-start.6 = (f32[1024,128]{1,0:T(8,128)S(1)}, f32[1024,128]{1,0:T(8,128)}, u32[]{:S(2)}) copy-start(f32[1024,128]{1,0:T(8,128)} %refs_14_.1) | copy-start | bytes 1572868
  0.7 56.1 %copy-start.7 = (f32[1024,128]{1,0:T(8,128)S(1)}, f32[1024,128]{1,0:T(8,128)}, u32[]{:S(2)}) copy-start(f32[1024,128]{1,0:T(8,128)} %refs_20_.1) | copy-start | bytes 1572868
  0.7 56.1 %copy-start.8 = (f32[128,512]{1,0:T(8,128)S(1)}, f32[128,512]{1,0:T(8,128)}, u32[]{:S(2)}) copy-start(f32[128,512]{1,0:T(8,128)} %refs_13_.1) | copy-start | bytes 786436
  0.8 56.1 %copy-start.9 = (f32[128,512]{1,0:T(8,128)S(1)}, f32[128,512]{1,0:T(8,128)}, u32[]{:S(2)}) copy-start(f32[128,512]{1,0:T(8,128)} %refs_15_.3) | copy-start | bytes 786436
  0.8 56.1 %copy-start.10 = (f32[128,512]{1,0:T(8,128)S(1)}, f32[128,512]{1,0:T(8,128)}, u32[]{:S(2)}) copy-start(f32[128,512]{1,0:T(8,128)} %refs_19_.1) | copy-start | bytes 786436
  0.8 56.1 %copy-start.11 = (f32[128,512]{1,0:T(8,128)S(1)}, f32[128,512]{1,0:T(8,128)}, u32[]{:S(2)}) copy-start(f32[128,512]{1,0:T(8,128)} %refs_21_.1) | copy-start | bytes 786436
  0.8 56.1 %copy-start.12 = (f32[6,512]{1,0:T(8,128)S(1)}, f32[6,512]{1,0:T(8,128)}, u32[]{:S(2)}) copy-start(f32[6,512]{1,0:T(8,128)} %refs_11_.1) | copy-start | bytes 36868
  0.8 56.1 %copy-start.13 = (f32[6,512]{1,0:T(8,128)S(1)}, f32[6,512]{1,0:T(8,128)}, u32[]{:S(2)}) copy-start(f32[6,512]{1,0:T(8,128)} %refs_17_.1) | copy-start | bytes 36868
  0.8 56.1 %copy-start.14 = (f32[6,512]{1,0:T(8,128)S(1)}, f32[6,512]{1,0:T(8,128)}, u32[]{:S(2)}) copy-start(f32[6,512]{1,0:T(8,128)} %refs_23_.1) | copy-start | bytes 36868
  0.8 56.1 %copy-start.15 = (f32[2,128]{1,0:T(2,128)S(1)}, f32[2,128]{1,0:T(2,128)}, u32[]{:S(2)}) copy-start(f32[2,128]{1,0:T(2,128)} %refs_10_.1) | copy-start | bytes 3076
  0.8 56.1 %copy-start.16 = (f32[2,128]{1,0:T(2,128)S(1)}, f32[2,128]{1,0:T(2,128)}, u32[]{:S(2)}) copy-start(f32[2,128]{1,0:T(2,128)} %refs_16_.1) | copy-start | bytes 3076
  0.8 56.1 %copy-start.17 = (f32[2,128]{1,0:T(2,128)S(1)}, f32[2,128]{1,0:T(2,128)}, u32[]{:S(2)}) copy-start(f32[2,128]{1,0:T(2,128)} %refs_22_.1) | copy-start | bytes 3076

commit v6 on v5

--- a/solution.py
+++ b/solution.py
@@ -468,18 +468,20 @@
     def crossed(m, row, j):
         return lax.rem(row // m + j, R // m) * m + lax.rem(row, m)
 
+    spans = (*chunks[:2], (base_in + L, d.size_in - L), (base_in, L))
+
     def pair_copy(n):
-        at = pl.ds(*chunks[n])
+        at = pl.ds(*spans[n])
         return remote(s.sb.at[at], s.rbp.at[at], s.psend.at[n], s.precv.at[n], (r, pair))
 
     def pair_start(n):
-        at = pl.ds(*chunks[n])
+        at = pl.ds(*spans[n])
         s.sb[at, :] = s.g[oc, at, :].astype(BF)
         pair_copy(n).start()
 
     def pair_finish(n):
         pair_copy(n).wait()
-        at = pl.ds(*chunks[n])
+        at = pl.ds(*spans[n])
         if n == 2:
             vec = pl.ds(base_vec, 32)
             s.g[c, vec, :] = s.g[c, vec, :].astype(BF).astype(F32)
@@ -635,10 +637,12 @@
     a_send(1)
 
     edge_part = tn(s.ef[...], s.sl[h])
+    for p in (0, 1):
+        s.g[p, base_in : base_in + L, :] = edge_part[:, p * Q : (p + 1) * Q]
+    pair_start(3)
     recv_part = tn(s.nf[...], s.rs[h].astype(BF))
     for p in (0, 1):
         cols = slice(p * Q, (p + 1) * Q)
-        s.g[p, base_in : base_in + L, :] = edge_part[:, cols]
         s.g[p, base_in + 2 * L : base_in + 3 * L, :] = recv_part[:, cols]
         for j in range(6):
             for q in range(L // LANES):
@@ -656,6 +660,7 @@
     loop(0, slot_tiles, sender_part)
     pair_start(2)
     b_send(0)
+    pair_finish(3)
     pair_finish(2)
     a_send(2)
 
@@ -979,8 +984,8 @@
         xsend=dma((7,)),
         xrecv=dma((7,)),
         nsem=dma((2,)),
-        psend=dma((3,)),
-        precv=dma((3,)),
+        psend=dma((4,)),
+        precv=dma((4,)),
         asend=dma((3,)),
         arecv=dma((3, most)),
         bsend=dma((3, most - 1)),

time: 62.7 us -> 62.7 us (level)
  no operation moved by 1% of the time
where the time goes in v6:
time: 62.7 us; the launch traced here: 62.5 us
  Pallas kernels  61.3 us (98%)
  between operations  1.12 us (2%)
    pallas_call x1, Pallas kernels, device_step(): pl.pallas_call(functools.partial(layer, names, d), out_shape=[shape for s...  55.9 us
    pallas_call x1, Pallas kernels, device_step(): pl.pallas_call(functools.partial(update, names, d), out_shape=[*(jax.Shap...  5.36 us

profile of v6, /device:TPU:0, one launch (start us, length us, event | category | flops | bytes accessed | tf_op | source)
XLA Modules:
  0.0 62.5 jit_solution(2321211598049429198)
XLA Ops:
  0.7 0.0 copy-start
  0.7 0.0 copy-start.1
  0.7 0.0 copy-start.2
  0.7 0.0 copy-start.3
  0.7 0.0 copy-start.4
  0.7 0.0 copy-start.5
  0.7 0.0 copy-start.6
  0.7 0.0 copy-start.7
  0.7 0.0 copy-start.8
  0.8 0.0 copy-start.9
  0.8 0.0 copy-start.10
  0.8 0.0 copy-start.11
  0.8 0.0 copy-start.12
  0.8 0.0 copy-start.13
  0.8 0.0 copy-start.14
  0.8 0.0 copy-start.15
  0.8 0.0 copy-start.16
  0.8 0.0 copy-start.17
  0.8 55.9 %shard_map.425 = (bf16[256,512]{1,0:T(8,128)(2,1)S(1)}, bf16[2048,512]{1,0:T(8,128)(2,1)S(1)}, bf16[256,512]{1,0:T(8,128)(2,1)S(1)}, bf16[2048,512]{1,0:T(8,128)...) custom-call(bf16[256,512]{1,0:T(8,128)(2,1)} %refs_0_.1, bf16[2048,512]{1,0:T(8,128)(2,1)} %refs_1_.1, ...), custom_call_target="tpu_custom_call" | custom-call | tf_op jit(solution)/shard_map/pallas_call | solution.py:1005
  56.8 0.0 copy-done
  56.8 0.0 copy-done.1
  56.8 0.0 copy-done.2
  56.8 0.0 copy-done.3
  56.8 0.0 copy-done.4
  56.8 0.0 copy-done.5
  56.8 0.0 copy-done.6
  56.8 0.0 copy-done.7
  56.8 0.0 copy-done.8
  56.9 0.0 copy-done.9
  56.9 0.0 copy-done.10
  56.9 0.0 copy-done.11
  56.9 0.0 copy-done.12
  56.9 0.0 copy-done.13
  56.9 0.0 copy-done.14
  56.9 0.0 copy-done.15
  56.9 0.0 copy-done.16
  56.9 0.0 copy-done.17
  56.9 5.4 %shard_map.426 = (bf16[256,512]{1,0:T(8,128)(2,1)}, bf16[2048,512]{1,0:T(8,128)(2,1)}, bf16[256,512]{1,0:T(8,128)(2,1)}, bf16[2048,512]{1,0:T(8,128)(2,1)}, f32[...) custom-call(bf16[3712,128]{1,0:T(8,128)(2,1)S(1)} %get-tuple-element, ...), custom_call_target="tpu_custom_call" | custom-call | tf_op jit(solution)/shard_map/pallas_call | solution.py:1029
Async XLA Ops:
  0.7 56.1 %copy-start = (f32[1536,128]{1,0:T(8,128)S(1)}, f32[1536,128]{1,0:T(8,128)}, u32[]{:S(2)}) copy-start(f32[1536,128]{1,0:T(8,128)} %refs_6_.3) | copy-start | bytes 2359300
  0.7 56.1 %copy-start.1 = (f32[1024,128]{1,0:T(8,128)S(1)}, f32[1024,128]{1,0:T(8,128)}, u32[]{:S(2)}) copy-start(f32[1024,128]{1,0:T(8,128)} %refs_8_.3) | copy-start | bytes 1572868
  0.7 56.1 %copy-start.2 = (f32[128,512]{1,0:T(8,128)S(1)}, f32[128,512]{1,0:T(8,128)}, u32[]{:S(2)}) copy-start(f32[128,512]{1,0:T(8,128)} %refs_7_.3) | copy-start | bytes 786436
  0.7 56.1 %copy-start.3 = (f32[128,512]{1,0:T(8,128)S(1)}, f32[128,512]{1,0:T(8,128)}, u32[]{:S(2)}) copy-start(f32[128,512]{1,0:T(8,128)} %refs_9_.3) | copy-start | bytes 786436
  0.7 56.1 %copy-start.4 = (f32[1536,128]{1,0:T(8,128)S(1)}, f32[1536,128]{1,0:T(8,128)}, u32[]{:S(2)}) copy-start(f32[1536,128]{1,0:T(8,128)} %refs_12_.1) | copy-start | bytes 2359300
  0.7 56.1 %copy-start.5 = (f32[1536,128]{1,0:T(8,128)S(1)}, f32[1536,128]{1,0:T(8,128)}, u32[]{:S(2)}) copy-start(f32[1536,128]{1,0:T(8,128)} %refs_18_.1) | copy-start | bytes 2359300
  0.7 56.1 %copy-start.6 = (f32[1024,128]{1,0:T(8,128)S(1)}, f32[1024,128]{1,0:T(8,128)}, u32[]{:S(2)}) copy-start(f32[1024,128]{1,0:T(8,128)} %refs_14_.1) | copy-start | bytes 1572868
  0.7 56.1 %copy-start.7 = (f32[1024,128]{1,0:T(8,128)S(1)}, f32[1024,128]{1,0:T(8,128)}, u32[]{:S(2)}) copy-start(f32[1024,128]{1,0:T(8,128)} %refs_20_.1) | copy-start | bytes 1572868
  0.7 56.1 %copy-start.8 = (f32[128,512]{1,0:T(8,128)S(1)}, f32[128,512]{1,0:T(8,128)}, u32[]{:S(2)}) copy-start(f32[128,512]{1,0:T(8,128)} %refs_13_.1) | copy-start | bytes 786436
  0.8 56.1 %copy-start.9 = (f32[128,512]{1,0:T(8,128)S(1)}, f32[128,512]{1,0:T(8,128)}, u32[]{:S(2)}) copy-start(f32[128,512]{1,0:T(8,128)} %refs_15_.3) | copy-start | bytes 786436
  0.8 56.1 %copy-start.10 = (f32[128,512]{1,0:T(8,128)S(1)}, f32[128,512]{1,0:T(8,128)}, u32[]{:S(2)}) copy-start(f32[128,512]{1,0:T(8,128)} %refs_19_.1) | copy-start | bytes 786436
  0.8 56.1 %copy-start.11 = (f32[128,512]{1,0:T(8,128)S(1)}, f32[128,512]{1,0:T(8,128)}, u32[]{:S(2)}) copy-start(f32[128,512]{1,0:T(8,128)} %refs_21_.1) | copy-start | bytes 786436
  0.8 56.1 %copy-start.12 = (f32[6,512]{1,0:T(8,128)S(1)}, f32[6,512]{1,0:T(8,128)}, u32[]{:S(2)}) copy-start(f32[6,512]{1,0:T(8,128)} %refs_11_.1) | copy-start | bytes 36868
  0.8 56.1 %copy-start.13 = (f32[6,512]{1,0:T(8,128)S(1)}, f32[6,512]{1,0:T(8,128)}, u32[]{:S(2)}) copy-start(f32[6,512]{1,0:T(8,128)} %refs_17_.1) | copy-start | bytes 36868
  0.8 56.1 %copy-start.14 = (f32[6,512]{1,0:T(8,128)S(1)}, f32[6,512]{1,0:T(8,128)}, u32[]{:S(2)}) copy-start(f32[6,512]{1,0:T(8,128)} %refs_23_.1) | copy-start | bytes 36868
  0.8 56.1 %copy-start.15 = (f32[2,128]{1,0:T(2,128)S(1)}, f32[2,128]{1,0:T(2,128)}, u32[]{:S(2)}) copy-start(f32[2,128]{1,0:T(2,128)} %refs_10_.1) | copy-start | bytes 3076
  0.8 56.1 %copy-start.16 = (f32[2,128]{1,0:T(2,128)S(1)}, f32[2,128]{1,0:T(2,128)}, u32[]{:S(2)}) copy-start(f32[2,128]{1,0:T(2,128)} %refs_16_.1) | copy-start | bytes 3076
  0.8 56.1 %copy-start.17 = (f32[2,128]{1,0:T(2,128)S(1)}, f32[2,128]{1,0:T(2,128)}, u32[]{:S(2)}) copy-start(f32[2,128]{1,0:T(2,128)} %refs_22_.1) | copy-start | bytes 3076
